TPU v7x, 32 devices: a whole 2x2x4 slice. The times are simulated.
32 devices in a mesh: wide: 8 (over y, x, core), narrow: 4 (over z).
Axes of the slice: x: 2, y: 2, z: 4, core: 2. Of those that a mesh axis runs over, the one named last changes fastest.
Arguments:
- tokens: bfloat16 [8192, 768], P(('wide', 'narrow')), may hold values from -6 to 6
- memory: bfloat16 [8192, 768], P(('wide', 'narrow')), may hold values from -6 to 6
- doc_lengths: int32 [32, 8], P(('wide', 'narrow')), may hold values from 0 to 256, as said below
- mem_lengths: int32 [32, 8], P(('wide', 'narrow')), may hold values from 0 to 256, as said below
- pad_mask: int32 [8192], P(('wide', 'narrow')), may hold values 0 or 1
- self_query: bfloat16 [768, 768], P(('wide', 'narrow')), may hold values from -0.078125 to 0.078125
- self_key: bfloat16 [768, 768], P(('wide', 'narrow')), may hold values from -0.078125 to 0.078125
- self_value: bfloat16 [768, 768], P(('wide', 'narrow')), may hold values from -0.21875 to 0.21875
- self_output: bfloat16 [768, 768], P(('wide', 'narrow')), may hold values from -0.875 to 0.875
- self_gain: bfloat16 [768], P(('wide', 'narrow')), may hold values from 0.5 to 1.5
- bias_table: bfloat16 [32, 12], P('narrow'), may hold values from -4 to 4
- cross_query: bfloat16 [768, 768], P(('wide', 'narrow')), may hold values from -0.078125 to 0.078125
- cross_key: bfloat16 [768, 768], P(('wide', 'narrow')), may hold values from -0.078125 to 0.078125
- cross_value: bfloat16 [768, 768], P(('wide', 'narrow')), may hold values from -0.21875 to 0.21875
- cross_output: bfloat16 [768, 768], P(('wide', 'narrow')), may hold values from -0.875 to 0.875
- cross_gain: bfloat16 [768], P(('wide', 'narrow')), may hold values from 0.5 to 1.5
- hidden_in: bfloat16 [768, 3072], P(('wide', 'narrow')), may hold values from -0.21875 to 0.21875
- hidden_out: bfloat16 [3072, 768], P(('wide', 'narrow')), may hold values from -0.109375 to 0.109375
- hidden_gain: bfloat16 [768], P(('wide', 'narrow')), may hold values from 0.5 to 1.5
- out_grad: bfloat16 [8192, 768], P(('wide', 'narrow')), may hold values from -6 to 6
Outputs:
- layer_out: bfloat16 [8192, 768], P(('wide', 'narrow'))
- tokens_grad: float32 [8192, 768], P(('wide', 'narrow'))
- memory_grad: float32 [8192, 768], P(('wide', 'narrow'))
- self_query_grad: float32 [768, 768], P(('wide', 'narrow'))
- self_key_grad: float32 [768, 768], P(('wide', 'narrow'))
- self_value_grad: float32 [768, 768], P(('wide', 'narrow'))
- self_output_grad: float32 [768, 768], P(('wide', 'narrow'))
- self_gain_grad: float32 [768], P(('wide', 'narrow'))
- bias_table_grad: float32 [32, 12], P('narrow')
- cross_query_grad: float32 [768, 768], P(('wide', 'narrow'))
- cross_key_grad: float32 [768, 768], P(('wide', 'narrow'))
- cross_value_grad: float32 [768, 768], P(('wide', 'narrow'))
- cross_output_grad: float32 [768, 768], P(('wide', 'narrow'))
- cross_gain_grad: float32 [768], P(('wide', 'narrow'))
- hidden_in_grad: float32 [768, 3072], P(('wide', 'narrow'))
- hidden_out_grad: float32 [3072, 768], P(('wide', 'narrow'))
- hidden_gain_grad: float32 [768], P(('wide', 'narrow'))
Inputs may be any that keep to these rules, and one draw needn't show every extreme that they name: `doc_lengths`: each row holds, in order, the lengths of the 8 sequences packed into one device's 256 token slots and sums to 256; lengths may be 0; in every draw one device holds a single sequence of 256 tokens. `mem_lengths`: each row holds, in order, the lengths of the encoder memories of the 8 sequences of that device, packed into its 256 memory slots, and sums to 256; every sequence with tokens has one memory token or more; the device that holds a single sequence gives it all 256 memory slots.
All inputs are finite; a program needn't handle non-finite values. No bound on the sum of `pad_mask` on one device may be relied on, other than what follows from the above.
Results may differ from a plain program's by a relative error of at most 0.023.
Values may be sent and summed in bfloat16 or wider, within the bound.
No kernel may reach another device: no remote copies, remote signals or barrier semaphores. Data moves between devices by JAX's collectives and lax.ppermute only.
A program may use at most 192 MiB of HBM per device.

v0:
```python
import math

import jax
import jax.numpy as jnp
import numpy as np
from jax import lax
from jax.experimental import pallas as pl
from jax.experimental.pallas import tpu as pltpu
from jax.sharding import PartitionSpec as P

BUCKETS = 32
REACH = 128
LOW = jnp.bfloat16
F32 = jnp.float32
NN = (((1,), (0,)), ((), ()))
NT = (((1,), (1,)), ((), ()))
TN = (((0,), (0,)), ((), ()))
PAIRS = 6
LANES = 128
TABLE_LANE = 16
CHUNK = 384
MiB = 1024 * 1024
FIRST_AT = 4


def bucket_edges(bucket_count, far_reach):
    exact_span = bucket_count // 2
    edge_list = list(range(1, exact_span + 1))
    for target in range(exact_span + 1, bucket_count):
        distance = exact_span
        while (
            exact_span
            + int(
                math.log(distance / exact_span)
                / math.log(far_reach / exact_span)
                * (bucket_count - exact_span)
            )
            < target
        ):
            distance += 1
        edge_list.append(distance)
    return edge_list


def rolled_one_hot(rows):
    edges = np.array(bucket_edges(BUCKETS, REACH))
    distances = (rows - np.arange(rows)) % rows
    buckets = (distances[:, None] >= edges[None, :]).sum(axis=1)
    return (np.arange(BUCKETS)[:, None] == buckets[None, :]).astype(np.float32)


def table_hot(rows, blocks, share, table_rows):
    one_hot = rolled_one_hot(rows)
    groups = -(-table_rows // share)
    hot = np.zeros((groups, blocks * share, rows), np.float32)
    for block in range(blocks):
        for row in range(table_rows):
            hot[row // share, block * share + row % share] = one_hot[block * table_rows + row]
    return hot


def grid_sizes():
    wide = lax.axis_size("wide")
    inner = wide // 2
    across = 1
    while across * across < inner:
        across *= 2
    return {"y": inner // across, "x": across, "c": 2, "z": lax.axis_size("narrow")}


def grid_place():
    sizes = grid_sizes()
    wide = lax.axis_index("wide")
    return {
        "y": wide // (2 * sizes["x"]),
        "x": (wide // 2) % sizes["x"],
        "c": wide % 2,
        "z": lax.axis_index("narrow"),
    }


def shifted(array, dim, step):
    sizes = grid_sizes()
    count = sizes[dim]
    if dim == "z":
        return lax.ppermute(array, "narrow", [(i, (i + step) % count) for i in range(count)])
    stride = {"y": 2 * sizes["x"], "x": 2, "c": 1}[dim]
    pairs = []
    for source in range(lax.axis_size("wide")):
        place = (source // stride) % count
        pairs.append((source, source + ((place + step) % count - place) * stride))
    return lax.ppermute(array, "wide", pairs)


def after(value, *earlier):
    return lax.optimization_barrier((value, *earlier))[0]


def received(block, dim):
    count = grid_sizes()[dim]
    return [shifted(block, dim, count - step) for step in range(1, count)]


def swapped(array):
    return shifted(array, "c", 1)


def in_order(block, others, dim, axis):
    here = grid_place()[dim]
    cyclic = [block] + others
    count = len(cyclic)
    ordered = []
    for place in range(count):
        picked = cyclic[0]
        for step in range(1, count):
            picked = jnp.where((here + step) % count == place, cyclic[step], picked)
        ordered.append(picked)
    return jnp.stack(ordered, axis)


class Weights:
    def __init__(self, arrays, spots):
        self.arrays = arrays
        self.spots = spots

    def load(self, place, refs, matrices):
        for source, first, rows, at, block, row, matrix in self.spots:
            start = row if at is None else pl.multiple_of(place[at] * block, block) + row
            matrices[matrix][pl.ds(start, rows), :] = refs[source][first : first + rows, :]


def in_pieces(block):
    sizes = grid_sizes()
    return sizes["y"] == 2 and sizes["x"] == 2 and block % 32 == 0


def from_neighbours(block):
    return [block, shifted(block, "x", 1), shifted(block, "y", 1)]


def from_corner(upper, lower):
    return [shifted(upper, "y", 1), shifted(lower, "x", 1)]


def gather_whole(block):
    block = in_order(block, received(block, "x"), "x", 0)
    block = in_order(block, received(block, "y"), "y", 0)
    block = in_order(block, received(block, "c"), "c", 2)
    return block.reshape(-1, block.shape[-1])


def piece_spots(neighbours, corners, block, first, matrix):
    spots = [(source, first, block, FIRST_AT + n, block, 0, matrix) for n, source in enumerate(neighbours)]
    if len(corners) == 4:
        half = block // 2
        for n, source in enumerate(corners):
            spots.append((source, 0, half, FIRST_AT + 6 + n % 2, block, (n // 2) * half, matrix))
    else:
        for n, source in enumerate(corners):
            spots.append((source, 0, block, FIRST_AT + 6 + n, block, 0, matrix))
    return spots


def with_twins(arrays):
    return [array for own in arrays for array in (own, swapped(own))]


def run(name, kernel, inputs, outputs, scratch=(), flops=0, weights=(), aliases=()):
    inputs = list(inputs)
    for group in weights:
        inputs += vmem(*group.arrays)
    size = sum(math.prod(array.shape) * array.dtype.itemsize for array, _ in inputs)
    arrays = [
        pltpu.with_memory_space_constraint(array, space) if space == pltpu.VMEM else array
        for array, space in inputs
    ]
    shapes = [
        jax.ShapeDtypeStruct(*output[:2]) if len(output) > 2 else pltpu.VMEM(*output) for output in outputs
    ]
    return pl.pallas_call(
        kernel,
        name=name,
        in_specs=[pl.BlockSpec(memory_space=space) for _, space in inputs],
        out_specs=[pl.BlockSpec(memory_space=pltpu.VMEM) for _ in outputs],
        out_shape=shapes,
        scratch_shapes=list(scratch),
        input_output_aliases=dict(aliases),
        compiler_params=pltpu.CompilerParams(vmem_limit_bytes=24 * MiB),
        cost_estimate=pl.CostEstimate(flops=flops, bytes_accessed=size // 2, transcendentals=0),
    )(*arrays)


def vmem(*arrays):
    return [(array, pltpu.VMEM) for array in arrays]


def dot(left, right, dims=NN):
    return lax.dot_general(left, right, dims, preferred_element_type=F32)


def scale_of(values):
    return lax.rsqrt(jnp.mean(values * values, axis=-1, keepdims=True) + 1e-06)


def norm_back(values, gain, grad):
    scale = scale_of(values)
    weighted = grad * gain
    middle = jnp.mean(values * weighted, axis=-1, keepdims=True)
    return (
        scale * weighted - values * (scale * scale * scale * middle),
        jnp.sum(grad * values * scale, axis=0, keepdims=True),
    )


def split_rows(matrix, core, keep, send):
    count, rows, _ = keep.shape
    if rows % 16:
        matrix = matrix.astype(F32)
    pieces = [matrix[n * rows : (n + 1) * rows].astype(keep.dtype) for n in range(2 * count)]

    @pl.when(core == 0)
    def _():
        for n in range(count):
            keep[n] = pieces[2 * n]
            send[n] = pieces[2 * n + 1]

    @pl.when(core == 1)
    def _():
        for n in range(count):
            keep[n] = pieces[2 * n + 1]
            send[n] = pieces[2 * n]


def lanes_of(pair, column=0):
    return pl.ds(pl.multiple_of(column + pair * LANES, LANES), LANES)


def head_mask(rows, head):
    lanes = lax.broadcasted_iota(jnp.int32, (rows, LANES), 1)
    return (lanes >= 64) if head else (lanes < 64)


def attend(q_ref, k_ref, v_ref, columns, allowed, bias, prob_ref, out_ref):
    rows = q_ref.shape[0]
    cols = k_ref.shape[0]

    def step(pair, carry):
        q = q_ref[:, lanes_of(pair, columns[0])]
        k = k_ref[:, lanes_of(pair, columns[1])]
        v = v_ref[:, lanes_of(pair, columns[2])]
        result = None
        for head in range(2):
            mine = head_mask(rows, head)
            scores = dot(jnp.where(mine, q, jnp.zeros_like(q)), k, NT)
            if bias is not None:
                row = jnp.broadcast_to(bias[pl.ds(2 * pair + head, 1), :], (rows, cols))
                scores = scores + pltpu.roll(row, 0, 1, stride=1, stride_axis=0)
            scores = jnp.where(allowed[...] > 0, scores, -1e9)
            weights = jnp.exp(scores - jnp.max(scores, axis=1, keepdims=True))
            probs = (weights * (1.0 / jnp.sum(weights, axis=1, keepdims=True))).astype(LOW)
            prob_ref[2 * pair + head] = probs
            part = dot(probs, v)
            result = part if head == 0 else jnp.where(mine, part, result)
        out_ref[:, lanes_of(pair)] = result.astype(LOW)
        return carry

    lax.fori_loop(0, PAIRS, step, 0)


def attend_back(q_ref, k_ref, v_ref, columns, g_ref, prob_ref, outs, dist_ref):
    rows = q_ref.shape[0]
    cols = k_ref.shape[0]

    def step(pair, carry):
        q = q_ref[:, lanes_of(pair, columns[0])]
        k = k_ref[:, lanes_of(pair, columns[1])]
        v = v_ref[:, lanes_of(pair, columns[2])]
        g = g_ref[:, lanes_of(pair)]
        if dist_ref is not None:
            i = lax.broadcasted_iota(jnp.int32, (rows, rows), 0)
            j = lax.broadcasted_iota(jnp.int32, (rows, rows), 1)
            flip = (i + j == rows - 1).astype(LOW)
        grads = None
        for head in range(2):
            mine = head_mask(rows, head)
            low_probs = prob_ref[2 * pair + head]
            probs = low_probs.astype(F32)
            moved = probs * dot(jnp.where(mine, g, jnp.zeros_like(g)), v, NT)
            low_scores = (moved - probs * jnp.sum(moved, axis=1, keepdims=True)).astype(LOW)
            if dist_ref is not None:
                lined = pltpu.roll(dot(flip, low_scores), 1, 1, stride=1, stride_axis=0)
                dist_ref[pl.ds(2 * pair + head, 1), :] = jnp.sum(lined, axis=0, keepdims=True)
            new = (dot(low_scores, k), dot(low_scores, q, TN), dot(low_probs, g, TN))
            grads = new if head == 0 else tuple(jnp.where(mine, b, a) for a, b in zip(grads, new))
        for (ref, column), grad in zip(outs, grads):
            ref[:, lanes_of(pair, column)] = grad.astype(LOW)
        return carry

    lax.fori_loop(0, PAIRS, step, 0)


def head_lanes(group, heads):
    head = lax.broadcasted_iota(jnp.int32, (16, LANES), 0)
    lane = lax.broadcasted_iota(jnp.int32, (16, LANES), 1)
    return ((head < heads) & (lane == TABLE_LANE + group * heads + head)).astype(F32)


def self_forward(place, tokens, row_ids, col_ids, pad, hot, weights, cut, block):
    rows, width = tokens.shape
    count = len(weights.arrays)
    heads = 2 * PAIRS
    groups = hot.shape[0]
    blocks = (width // block) // 2

    def kernel(place, tok, row_ids, col_ids, pad, hot, *refs):
        pieces, refs = refs[:count], refs[count:]
        qk, v, probs, out, nt_keep, nt_send, at_keep, at_send, gains, matrix, allowed, bias, att = refs
        weights.load(place, pieces, [matrix])
        i = lax.broadcasted_iota(jnp.int32, (rows, rows), 0)
        j = lax.broadcasted_iota(jnp.int32, (rows, rows), 1)
        same = (row_ids[...] == col_ids[...]) & (j <= i) & ((pad[...] == 1) | (i == j))
        allowed[...] = same.astype(F32)
        residual = tok[...].astype(F32)
        scaled = residual * scale_of(residual)
        extra = matrix[:, 2 * width : cut].astype(F32)
        gains[...] = extra.T[:8]
        normed = (scaled * gains[0:1, :]).astype(LOW)
        total = None
        for group in range(groups):
            table = dot(extra[: hot.shape[1]], head_lanes(group, heads), NT)
            part = dot(table.astype(LOW), hot[group], TN)
            total = part if total is None else total + part
        bias[...] = total
        split_rows(normed.T, place[2], nt_keep, nt_send)
        qk[...] = dot(normed, matrix[:, : 2 * width]).astype(LOW)
        v[...] = dot(normed, matrix[:, cut : cut + width]).astype(LOW)
        attend(qk, qk, v, (0, width, 0), allowed, bias, probs, att)
        attended = att[...]
        split_rows(attended.T, place[2], at_keep, at_send)
        out[...] = residual + dot(attended, matrix[:, cut + width :])

    halves = ((blocks, block, rows), LOW)
    return run(
        "self_forward",
        kernel,
        [(place, pltpu.SMEM)] + vmem(tokens, row_ids, col_ids, pad, hot),
        [
            ((rows, 2 * width), LOW),
            ((rows, width), LOW),
            ((heads, rows, rows), LOW),
            ((rows, width), F32),
            halves,
            halves,
            halves,
            halves,
            ((8, width), F32),
            ((width, cut + 2 * width), LOW),
        ],
        [
            pltpu.VMEM((rows, rows), F32),
            pltpu.VMEM((16, rows), F32),
            pltpu.VMEM((rows, width), LOW),
        ],
        flops=8 * rows * width * width,
        weights=[weights],
    )


def cross_forward(place, after_self, memory, gains, row_ids, col_ids, weights, block):
    rows, width = after_self.shape
    mem_rows = memory.shape[0]
    count = len(weights.arrays)
    blocks = (width // block) // 2

    def kernel(place, x, mem, gains, row_ids, col_ids, *refs):
        pieces, refs = refs[:count], refs[count:]
        q, kv, probs, out, nt_keep, nt_send, at_keep, at_send, mt_keep, mt_send, matrix, allowed, att = refs
        weights.load(place, pieces, [matrix])
        allowed[...] = (row_ids[...] == col_ids[...]).astype(F32)
        residual = x[...]
        normed = (residual * scale_of(residual) * gains[1:2, :]).astype(LOW)
        split_rows(normed.T, place[2], nt_keep, nt_send)
        split_rows(mem[...].T, place[2], mt_keep, mt_send)
        kv[...] = dot(mem[...], matrix[:, 2 * width :]).astype(LOW)
        q[...] = dot(normed, matrix[:, :width]).astype(LOW)
        attend(q, kv, kv, (0, 0, width), allowed, None, probs, att)
        attended = att[...]
        split_rows(attended.T, place[2], at_keep, at_send)
        out[...] = residual + dot(attended, matrix[:, width : 2 * width])

    halves = ((blocks, block, rows), LOW)
    mem_halves = ((blocks, block, mem_rows), LOW)
    return run(
        "cross_forward",
        kernel,
        [(place, pltpu.SMEM)] + vmem(after_self, memory, gains, row_ids, col_ids),
        [
            ((rows, width), LOW),
            ((mem_rows, 2 * width), LOW),
            ((2 * PAIRS, rows, mem_rows), LOW),
            ((rows, width), F32),
            halves,
            halves,
            halves,
            halves,
            mem_halves,
            mem_halves,
            ((width, 4 * width), LOW),
        ],
        [
            pltpu.VMEM((rows, mem_rows), F32),
            pltpu.VMEM((rows, width), LOW),
        ],
        flops=8 * rows * width * width,
        weights=[weights],
    )


def hidden_early(place, weights, width, ff):
    count = len(weights.arrays)

    def kernel(place, *refs):
        weights.load(place, refs[:count], refs[count:])

    return run(
        "hidden_early",
        kernel,
        [(place, pltpu.SMEM)],
        [((width, ff), LOW), ((ff, width), LOW)],
        weights=[weights],
    )


def hidden_first(place, after_cross, out_grad, gains, m_in, m_out, weights, block):
    rows, width = after_cross.shape
    ff = m_in.shape[1]
    count = len(weights.arrays)
    blocks = (width // block) // 2
    ff_block = ff // (2 * blocks)
    factor = math.sqrt(2.0 / math.pi)

    def kernel(place, x, og, gains, m_in_before, m_out_before, *refs):
        pieces, refs = refs[:count], refs[count:]
        act, gu, nt_keep, nt_send, at_keep, at_send, m_in, m_out = refs[:8]
        weights.load(place, pieces, [m_in, m_out])
        residual = x[...]
        normed = (residual * scale_of(residual) * gains[2:3, :]).astype(LOW)
        split_rows(normed.T, place[2], nt_keep, nt_send)
        grad = og[...]
        for start in range(0, ff, CHUNK):
            stop = start + CHUNK
            u = dot(normed, m_in[:, start:stop])
            ga = dot(grad, m_out[start:stop, :], NT).astype(LOW).astype(F32)
            square = u * u
            t = jnp.tanh(factor * u * (1.0 + 0.044715 * square))
            half = 0.5 * (1.0 + t)
            a = (u * half).astype(LOW)
            slope = half + (0.5 * factor) * u * (1.0 - t * t) * (1.0 + 3 * 0.044715 * square)
            gu[:, start:stop] = (slope * ga).astype(LOW)
            act[:, start:stop] = a
            turned = a.T
            for first in range(start, stop, ff_block):
                n = first // ff_block
                piece = turned[first - start : first - start + ff_block]

                @pl.when(place[2] == n % 2)
                def _(n=n, piece=piece):
                    at_keep[n // 2] = piece

                @pl.when(place[2] != n % 2)
                def _(n=n, piece=piece):
                    at_send[n // 2] = piece

    halves = ((blocks, block, rows), LOW)
    ff_halves = ((blocks, ff_block, rows), LOW)
    return run(
        "hidden_first",
        kernel,
        [(place, pltpu.SMEM)] + vmem(after_cross, out_grad, gains, m_in, m_out),
        [
            ((rows, ff), LOW),
            ((rows, ff), LOW),
            halves,
            halves,
            ff_halves,
            ff_halves,
            (m_in.shape, LOW),
            (m_out.shape, LOW),
        ],
        flops=4 * rows * width * ff,
        weights=[weights],
        aliases={4: 6, 5: 7},
    )


def hidden_second(after_cross, out_grad, gains, act, gu, m_in, m_out):
    rows, width = after_cross.shape
    ff = m_in.shape[1]

    def kernel(x, og, gains, act, gu, m_in, m_out, out, back_out, gain_out):
        residual = x[...]
        back, gain = norm_back(residual, gains[2:3, :], dot(gu[...], m_in[...], NT))
        back_out[...] = og[...].astype(F32) + back
        gain_out[...] = gain
        out[...] = (residual + dot(act[...], m_out[...])).astype(LOW)

    return run(
        "hidden_second",
        kernel,
        vmem(after_cross, out_grad, gains, act, gu, m_in, m_out),
        [((rows, width), LOW, None), ((rows, width), F32), ((1, width), F32)],
        flops=4 * rows * width * ff,
    )


def cross_backward(grad, after_self, gains, q, kv, probs, matrix):
    rows, width = after_self.shape
    mem_rows = kv.shape[0]

    def kernel(grad, x, gains, q, kv, probs, matrix, tok_out, mem_out, mem_grad, back_out, gain_out, att):
        branch = grad[...].astype(LOW)
        tok_out[:, width:] = branch
        att[...] = dot(branch, matrix[:, width : 2 * width], NT).astype(LOW)
        outs = ((tok_out, 0), (mem_out, 0), (mem_out, width))
        attend_back(q, kv, kv, (0, 0, width), att, probs, outs, None)
        back, gain = norm_back(x[...], gains[1:2, :], dot(tok_out[:, :width], matrix[:, :width], NT))
        back_out[...] = grad[...] + back
        gain_out[...] = gain
        mem_grad[...] = dot(mem_out[...], matrix[:, 2 * width :], NT)

    return run(
        "cross_backward",
        kernel,
        vmem(grad, after_self, gains, q, kv, probs, matrix),
        [
            ((rows, 2 * width), LOW),
            ((mem_rows, 2 * width), LOW),
            ((mem_rows, width), F32, None),
            ((rows, width), F32),
            ((1, width), F32),
        ],
        [pltpu.VMEM((rows, width), LOW)],
        flops=8 * rows * width * width,
    )


def self_backward(place, grad, tokens, gains, cross_gain, hidden_gain, qk, v, probs, hot, matrix, cut, block):
    rows, width = tokens.shape
    heads = 2 * PAIRS
    groups = hot.shape[0]
    blocks = (width // block) // 2

    def kernel(place, grad, tok, gains, cross_gain, hidden_gain, qk, v, probs, hot, matrix, *refs):
        out, tok_grad, extra_keep, extra_send, att, dist, parts = refs
        branch = grad[...].astype(LOW)
        out[:, 3 * width :] = branch
        att[...] = dot(branch, matrix[:, cut + width :], NT).astype(LOW)
        outs = ((out, 0), (out, width), (out, 2 * width))
        dist[...] = jnp.zeros_like(dist)
        attend_back(qk, qk, v, (0, width, 0), att, probs, outs, dist)
        normed_grad = dot(out[:, : 2 * width], matrix[:, : 2 * width], NT)
        normed_grad = normed_grad + dot(out[:, 2 * width : 3 * width], matrix[:, cut : cut + width], NT)
        back, gain = norm_back(tok[...].astype(F32), gains[0:1, :], normed_grad)
        tok_grad[...] = grad[...] + back
        parts[...] = jnp.zeros_like(parts)
        parts[0:1, :] = gain
        parts[1:2, :] = cross_gain[...]
        parts[2:3, :] = hidden_gain[...]
        columns = parts[...].T
        table = None
        for group in range(groups):
            sums = lax.dot_general(
                hot[group].astype(F32), dist[...], NT, precision=lax.Precision.HIGHEST, preferred_element_type=F32
            )
            part = lax.dot_general(
                sums, head_lanes(group, heads), NN, precision=lax.Precision.HIGHEST, preferred_element_type=F32
            )
            table = part if table is None else table + part
        columns = columns + jnp.concatenate([table] * (2 * blocks), axis=0)
        split_rows(columns, place[2], extra_keep, extra_send)

    halves = ((blocks, block, LANES), LOW)
    return run(
        "self_backward",
        kernel,
        [(place, pltpu.SMEM)]
        + vmem(grad, tokens, gains, cross_gain, hidden_gain, qk, v, probs, hot, matrix),
        [((rows, 4 * width), LOW), ((rows, width), F32, None), halves, halves],
        [
            pltpu.VMEM((rows, width), LOW),
            pltpu.VMEM((16, rows), F32),
            pltpu.VMEM((LANES, width), F32),
        ],
        flops=8 * rows * width * width,
    )


def weight_grads(place, lefts, rights, sections, cols, extras=()):
    sizes = grid_sizes()
    counts = (sizes["y"], sizes["x"])
    left_count, right_count = len(lefts), len(rights)
    block = [None, None]
    for section in sections:
        block[section[4]] = lefts[section[0]][0].shape[1]

    def kernel(place, *refs):
        refs = list(refs)
        left = [(refs.pop(0), refs.pop(0)) for _ in range(left_count)]
        right = [(refs.pop(0), refs.pop(0)) for _ in range(right_count)]
        extra = [refs.pop(0) for _ in extras]
        outs = (refs[: counts[0]], refs[counts[0] :])
        for half in range(2):
            mine, across = counts[half], counts[1 - half]
            here = place[half]
            for step in range(mine):
                for other in range(across):
                    index = ((here + step) % mine) * across + other
                    if half == 1:
                        index = other * mine + (here + step) % mine
                    target = outs[half][step]
                    for l, r, column, width, where, at in sections:
                        if where != half:
                            continue
                        for first in range(0, width, 768):
                            size = min(768, width - first)
                            own = dot(left[l][0][index], right[r][0][:, column + first : column + first + size])
                            far = dot(left[l][1][index], right[r][1][:, column + first : column + first + size])
                            target[other, :, at + first : at + first + size] = (own + far).astype(LOW)
                    if extras and half == 0:
                        target[other, :, cols[0] - LANES :] = (
                            extra[0][index].astype(F32) + extra[1][index].astype(F32)
                        ).astype(LOW)

    arrays = [array for pair in lefts for array in pair] + [array for pair in rights for array in pair]
    outputs = [((counts[1], block[0], cols[0]), LOW)] * counts[0]
    outputs += [((counts[0], block[1], cols[1]), LOW)] * counts[1]
    return run(
        "weight_grads",
        kernel,
        [(place, pltpu.SMEM)] + vmem(*arrays, *extras),
        outputs,
        flops=sum(2 * lefts[s[0]][0].size * s[3] for s in sections),
    )


def add_stage(place, firsts, seconds):
    sizes = grid_sizes()
    counts = (sizes["x"], sizes["y"])

    def kernel(place, *refs):
        halves = (refs[: len(firsts)], refs[len(firsts) : len(firsts) + len(seconds)])
        outs = refs[len(firsts) + len(seconds) :]
        outs = (outs[: counts[0]], outs[counts[0] :])
        for half in range(2):
            here = place[1 - half]
            for step in range(counts[half]):
                index = (here + step) % counts[half]
                total = halves[half][0][index].astype(F32)
                for part in halves[half][1:]:
                    total = total + part[index].astype(F32)
                outs[half][step][...] = total.astype(LOW)

    outputs = [(firsts[0].shape[1:], LOW)] * counts[0] + [(seconds[0].shape[1:], LOW)] * counts[1]
    return run("add_stage", kernel, [(place, pltpu.SMEM)] + vmem(*firsts, *seconds), outputs)


def add_last(place, firsts, seconds, by_z):
    sizes = grid_sizes()
    if by_z:
        count = sizes["z"]
        share = firsts[0].shape[0] // count
        firsts = [part.reshape(count, share, part.shape[-1]) for part in firsts]
        seconds = [part.reshape(count, share, part.shape[-1]) for part in seconds]
        cut = firsts[0].shape[-1]
        outputs = [((share, cut + seconds[0].shape[-1]), LOW)] * count
    else:
        outputs = [(firsts[0].shape, LOW), (seconds[0].shape, LOW)]

    def kernel(place, *refs):
        halves = (refs[: len(firsts)], refs[len(firsts) : len(firsts) + len(seconds)])
        outs = refs[len(firsts) + len(seconds) :]
        for half, parts in enumerate(halves):
            if not by_z:
                total = parts[0][...].astype(F32)
                for part in parts[1:]:
                    total = total + part[...].astype(F32)
                outs[half][...] = total.astype(LOW)
                continue
            for step in range(count):
                index = (place[3] + step) % count
                total = parts[0][index].astype(F32)
                for part in parts[1:]:
                    total = total + part[index].astype(F32)
                total = total.astype(LOW)
                if half == 0:
                    outs[step][:, :cut] = total
                else:
                    outs[step][:, cut:] = total

    return run("add_last", kernel, [(place, pltpu.SMEM)] + vmem(*firsts, *seconds), outputs)


def sent(parts, dim):
    return [parts[0]] + [shifted(part, dim, step) for step, part in enumerate(parts) if step]


def segment_ids(length_row, slot_count):
    ends = jnp.cumsum(length_row).astype(jnp.int32)
    places = jnp.arange(slot_count, dtype=jnp.int32)
    return jnp.sum((places[:, None] >= ends[None, :]).astype(jnp.int32), axis=1).astype(jnp.int32)


def local(
    tokens, memory, doc_lengths, mem_lengths, pad_mask,
    self_query, self_key, self_value, self_output, self_gain, bias_table,
    cross_query, cross_key, cross_value, cross_output, cross_gain,
    hidden_in, hidden_out, hidden_gain, out_grad,
):
    sizes = grid_sizes()
    here = grid_place()
    ny, nx, nz = sizes["y"], sizes["x"], sizes["z"]
    rows, width = tokens.shape
    mem_rows = memory.shape[0]
    ff = hidden_in.shape[1]
    share = self_query.shape[0]
    ff_share = hidden_out.shape[0]
    table_rows, heads = bias_table.shape
    block = nz * share
    ff_block = nz * ff_share
    cut = 2 * width + LANES

    spots = []
    for step in range(4):
        y = (here["y"] + step // 2) % ny
        x = (here["x"] + step % 2) % nx
        for core in range(2):
            spots.append((y * nx + x) * 2 + (here["c"] + core) % 2)
    place = jnp.stack([here["y"], here["x"], here["c"], here["z"]] + spots).astype(jnp.int32)

    hot = jnp.asarray(table_hot(rows, nz, share, table_rows)).astype(LOW)
    groups = hot.shape[0]
    table = jnp.pad(bias_table, ((0, groups * share - table_rows), (0, 0)))
    table = jnp.transpose(table.reshape(groups, share, heads), (1, 0, 2)).reshape(share, groups * heads)
    extra = jnp.concatenate(
        [
            self_gain[:, None],
            cross_gain[:, None],
            hidden_gain[:, None],
            jnp.zeros((share, TABLE_LANE - 3), LOW),
            table,
            jnp.zeros((share, LANES - TABLE_LANE - groups * heads), LOW),
        ],
        axis=1,
    )
    self_own = jnp.concatenate([self_query, self_key, extra, self_value, self_output], axis=1)
    self_others = received(self_own, "z")
    self_z = in_order(self_own, self_others, "z", 0).reshape(block, -1)
    wide_out = jnp.transpose(hidden_out.reshape(ff // width, share, width), (1, 0, 2)).reshape(share, ff)
    rest = jnp.concatenate(
        [
            jnp.concatenate([cross_query, cross_output, cross_key, cross_value], axis=1),
            hidden_in,
            wide_out,
        ],
        axis=0,
    )
    rest = lax.all_gather(rest, "narrow", axis=0, tiled=True)

    def ordered(rest):
        parts = rest.reshape(nz, 3, share, ff)
        both = jnp.transpose(parts[:, :2], (1, 0, 2, 3)).reshape(2 * block, ff)
        out = jnp.transpose(parts[:, 2].reshape(nz, share, ff // width, width), (0, 2, 1, 3))
        return both, out.reshape(ff_block, width)

    seg_ids = segment_ids(doc_lengths[0], rows)
    mem_ids = segment_ids(mem_lengths[0], mem_rows)
    pieces = in_pieces(block)
    half = block // 2
    if pieces:
        near = from_neighbours(self_z)
        corner = from_corner(near[1][:half], near[2][half:])
        both, out_z = ordered(after(rest, *corner))
        both_near = from_neighbours(both)
        out_near = from_neighbours(out_z)
        w_self = Weights(
            with_twins(near) + with_twins(corner), piece_spots(range(6), range(6, 10), block, 0, 0)
        )
    else:
        w_self = Weights([gather_whole(self_z)], [(0, 0, width, None, 0, 0, 0)])

    qk, v, self_probs, after_self, sn_keep, sn_send, sa_keep, sa_send, gains, m_self = self_forward(
        place, tokens, seg_ids[:, None], seg_ids[None], pad_mask[None], hot, w_self, cut, block
    )
    if pieces:
        corner = from_corner(after(both_near[1][:half], after_self), after(both_near[2][half:block], after_self))
        both_twins = with_twins(both_near)
        out_twins = with_twins(out_near)
        w_cross = Weights(both_twins + with_twins(corner), piece_spots(range(6), range(6, 10), block, 0, 0))
        last = from_corner(after(both_near[1][block:], *corner), after(out_near[2], *corner))
        spots = piece_spots(range(6), (), block, block, 0) + piece_spots(range(6, 12), (), ff_block, 0, 1)
        m_in, m_out = hidden_early(place, Weights(both_twins + out_twins, spots), width, ff)
        cross_in = after(after_self, m_in)
    else:
        both, out_z = ordered(rest)
        w_cross = Weights([gather_whole(both[:block])], [(0, 0, width, None, 0, 0, 0)])
        m_in, m_out = gather_whole(both[block:]), gather_whole(out_z)
        cross_in = after_self
    q, kv, cross_probs, after_cross, cn_keep, cn_send, ca_keep, ca_send, mt_keep, mt_send, m_cross = cross_forward(
        place, cross_in, memory, gains, seg_ids[:, None], mem_ids[None], w_cross, block
    )
    if pieces:
        last = with_twins([after(array, after_cross) for array in last])
        spots = piece_spots((), (0, 1), block, 0, 0) + piece_spots((), (2, 3), ff_block, 0, 1)
        w_last = Weights(last, spots)
    else:
        w_last = Weights([], [])
    sn_far, sa_far = swapped(sn_send), swapped(sa_send)
    cn_far, ca_far, mt_far = swapped(cn_send), swapped(ca_send), swapped(mt_send)
    og_far = swapped(out_grad)

    act, gu, hn_keep, hn_send, ha_keep, ha_send, m_in, m_out = hidden_first(
        place, after_cross, out_grad, gains, m_in, m_out, w_last, block
    )
    hn_far, ha_far, gu_far = swapped(hn_send), swapped(ha_send), swapped(gu)
    layer_out, grad, hidden_gain_part = hidden_second(after_cross, out_grad, gains, act, gu, m_in, m_out)
    hn_keep = after(hn_keep, grad)
    ff_parts = weight_grads(
        place,
        [(hn_keep, hn_far), (ha_keep, ha_far)],
        [(gu, gu_far), (out_grad, og_far)],
        [(0, 0, 0, ff, 0, 0), (1, 1, 0, width, 1, 0)],
        (ff, width),
    )
    ff_first, ff_second = ff_parts[:ny], ff_parts[ny:]
    ff_first, ff_second = sent(ff_first, "y"), sent(ff_second, "x")

    grad = after(grad, *ff_parts)
    cross_tok, cross_mem, memory_grad, grad, cross_gain_part = cross_backward(
        grad, after_self, gains, q, kv, cross_probs, m_cross
    )
    cross_tok_far, cross_mem_far = swapped(cross_tok), swapped(cross_mem)
    cross_parts = weight_grads(
        place,
        [(cn_keep, cn_far), (ca_keep, ca_far), (mt_keep, mt_far)],
        [(cross_tok, cross_tok_far), (cross_mem, cross_mem_far)],
        [
            (0, 0, 0, width, 0, 0),
            (1, 0, width, width, 0, width),
            (2, 1, 0, 2 * width, 1, 0),
        ],
        (2 * width, 2 * width),
    )
    cross_first, cross_second = cross_parts[:ny], cross_parts[ny:]
    ff_first = [after(ff_first[0], *cross_parts)] + ff_first[1:]
    ff_parts = add_stage(place, ff_first, ff_second)
    ff_first, ff_second = ff_parts[:nx], ff_parts[nx:]
    ff_first, ff_second = sent(ff_first, "x"), sent(ff_second, "y")
    cross_first, cross_second = sent(cross_first, "y"), sent(cross_second, "x")

    grad = after(grad, *ff_parts)
    self_grads, tokens_grad, extra_keep, extra_send = self_backward(
        place, grad, tokens, gains, cross_gain_part, hidden_gain_part, qk, v, self_probs, hot, m_self, cut, block
    )
    self_grads_far, extra_far = swapped(self_grads), swapped(extra_send)
    ff_first = [after(ff_first[0], self_grads)] + ff_first[1:]
    ff_first, ff_second = add_last(place, ff_first, ff_second, False)
    ff_total = jnp.concatenate(
        [
            jnp.transpose(ff_first.reshape(nz, share, ff // width, width), (0, 2, 1, 3)).reshape(nz, ff_share, width),
            ff_second.reshape(nz, ff_share, width),
        ],
        axis=1,
    ).reshape(-1, width)
    ff_total = lax.psum_scatter(ff_total, "narrow", scatter_dimension=0, tiled=True)
    cross_first = [after(cross_first[0], self_grads)] + cross_first[1:]
    cross_parts = add_stage(place, cross_first, cross_second)
    cross_first, cross_second = cross_parts[:nx], cross_parts[nx:]
    cross_first, cross_second = sent(cross_first, "x"), sent(cross_second, "y")
    sn_keep = after(sn_keep, ff_first, *cross_parts)
    self_parts = weight_grads(
        place,
        [(sn_keep, sn_far), (sa_keep, sa_far)],
        [(self_grads, self_grads_far)],
        [
            (0, 0, 0, 2 * width, 0, 0),
            (0, 0, 2 * width, width, 1, 0),
            (1, 0, 3 * width, width, 1, width),
        ],
        (cut, 2 * width),
        (extra_keep, extra_far),
    )
    self_first, self_second = self_parts[:ny], self_parts[ny:]
    self_first, self_second = sent(self_first, "y"), sent(self_second, "x")
    cross_first = [after(cross_first[0], *self_parts)] + cross_first[1:]
    cross_parts = add_last(place, cross_first, cross_second, True)
    cross_total = sum(part.astype(F32) for part in sent(cross_parts, "z"))
    self_first = [after(self_first[0], *cross_parts)] + self_first[1:]
    self_parts = add_stage(place, self_first, self_second)
    self_first, self_second = self_parts[:nx], self_parts[nx:]
    self_first, self_second = sent(self_first, "x"), sent(self_second, "y")
    self_parts = add_last(place, self_first, self_second, True)
    self_total = sum(part.astype(F32) for part in sent(self_parts, "z"))

    ff_total = ff_total.astype(F32)
    in_grad = jnp.transpose(ff_total[:ff_share].reshape(ff // width, share, width), (1, 0, 2)).reshape(share, ff)
    last = self_total[:, 2 * width : cut]
    table_grad = last[:, TABLE_LANE : TABLE_LANE + groups * heads].reshape(share, groups, heads)
    table_grad = jnp.transpose(table_grad, (1, 0, 2)).reshape(groups * share, heads)[:table_rows]
    return (
        layer_out,
        tokens_grad,
        memory_grad,
        self_total[:, :width],
        self_total[:, width : 2 * width],
        self_total[:, cut : cut + width],
        self_total[:, cut + width :],
        last[:, 0],
        table_grad,
        cross_total[:, :width],
        cross_total[:, 2 * width : 3 * width],
        cross_total[:, 3 * width :],
        cross_total[:, width : 2 * width],
        last[:, 1],
        in_grad,
        ff_total[ff_share:],
        last[:, 2],
    )


def solution(mesh):
    rows = P(("wide", "narrow"), None)
    line = P(("wide", "narrow"))
    table = P("narrow", None)
    return jax.shard_map(
        local,
        mesh=mesh,
        in_specs=(
            (rows,) * 4 + (line,) + (rows,) * 4 + (line, table) + (rows,) * 4 + (line,) + (rows,) * 2 + (line, rows)
        ),
        out_specs=(rows,) * 7 + (line, table) + (rows,) * 4 + (line,) + (rows,) * 2 + (line,),
        check_vma=False,
    )
```

profile of v0, /device:TPU:0, one launch (start us, length us, event | category | flops | bytes accessed | tf_op | source)
XLA Modules:
  0.0 329.1 jit_solution(7182879888839440424)
XLA Ops:
  11.1 3.1 collective-permute-start
  21.1 5.7 %collective-permute-done.1 = bf16[24,3200]{1,0:T(8,128)(2,1)S(1)} collective-permute-done((bf16[24,3200]{1,0:T(8,128)(2,1)S(1)}, bf16[24,3200]{1,0:T(8,128)(2,1)S(1)}, u32[]{:S(2)}, u32[]{:S(2)}) %collective-permute-start.1) | collective-permute-done | bytes 153632 | tf_op jit(solution)/shard_map/ppermute | solution.py:86
  30.1 12.8 %collective-permute-done.6.refs_4_ = bf16[96,3200]{1,0:T(8,128)(2,1)} collective-permute-done((bf16[96,3200]{1,0:T(8,128)(2,1)S(1)}, bf16[96,3200]{1,0:T(8,128)(2,1)}, u32[]{:S(2)}, u32[]{:S(2)}) %collective-permute-start.6) | collective-permute-done | bytes 614432 | tf_op jit(solution)/shard_map/ppermute | solution.py:92
  48.0 4.2 %collective-permute-done.10.refs_8_ = bf16[48,3200]{1,0:T(8,128)(2,1)S(1)} collective-permute-done((bf16[48,3200]{1,0:T(8,128)(2,1)S(1)}, bf16[48,3200]{1,0:T(8,128)(2,1)S(1)}, u32[]{:S(2)}, u32[]{:S(2)}) %collective-permute-start.10) | collective-permute-done | bytes 307232 | tf_op jit(solution)/shard_map/ppermute | solution.py:92
  54.6 5.0 %all-gather.2.cloned.1.call-done = bf16[288,3072]{1,0:T(8,128)(2,1)} async-done(((bf16[72,3072]{1,0:T(8,128)(2,1)}), bf16[288,3072]{1,0:T(8,128)(2,1)}) %all-gather.2.cloned.1.call-update) | async-done | bytes 1769488 | tf_op jit(solution)/shard_map/all_gather | solution.py:767
  73.0 31.2 %collective-permute-done.20.refs_10_ = bf16[384,768]{1,0:T(8,128)(2,1)} collective-permute-done((bf16[384,768]{1,0:T(8,128)(2,1)}, bf16[384,768]{1,0:T(8,128)(2,1)}, u32[]{:S(2)}, u32[]{:S(2)}) %collective-permute-start.20) | collective-permute-done | bytes 589856 | tf_op jit(solution)/shard_map/ppermute | solution.py:92
  112.7 9.9 %self_forward.1 = (bf16[256,1536]{1,0:T(8,128)(2,1)S(1)}, bf16[256,768]{1,0:T(8,128)(2,1)S(1)}, bf16[12,256,256]{2,1,0:T(8,128)(2,1)S(1)}, f32[256,768]{1,0:T(8,...) custom-call(s32[12]{0:T(128)S(1)} %stack.66.place, ...), custom_call_target="tpu_custom_call" | custom-call | flops 1207959552 | bytes 2680344 | tf_op jit(solution)/shard_map/self_forward/pallas_call | solution.py:180
  132.1 6.8 %collective-permute-done.22.refs_6_ = bf16[48,3072]{1,0:T(8,128)(2,1)} collective-permute-done((bf16[48,3072]{1,0:T(8,128)(2,1)S(1)}, bf16[48,3072]{1,0:T(8,128)(2,1)}, u32[]{:S(2)}, u32[]{:S(2)}) %collective-permute-start.22) | collective-permute-done | bytes 294944 | tf_op jit(solution)/shard_map/ppermute | solution.py:92
  153.0 10.1 %cross_forward.1 = (bf16[256,768]{1,0:T(8,128)(2,1)S(1)}, bf16[256,1536]{1,0:T(8,128)(2,1)S(1)}, bf16[12,256,256]{2,1,0:T(8,128)(2,1)S(1)}, f32[256,768]{1,0:T(8...) custom-call(s32[12]{0:T(128)S(1)} %stack.66.place, ...), custom_call_target="tpu_custom_call" | custom-call | flops 1207959552 | bytes 4731928 | tf_op jit(solution)/shard_map/cross_forward/pallas_call | solution.py:180
  166.2 6.9 %hidden_first.1 = (bf16[256,3072]{1,0:T(8,128)(2,1)S(1)}, bf16[256,3072]{1,0:T(8,128)(2,1)S(1)}, bf16[4,96,256]{2,1,0:T(8,128)(2,1)S(1)}, bf16[4,96,256]{2,1,0:T...) custom-call(s32[12]{0:T(128)S(1)} %stack.66.place, ...), custom_call_target="tpu_custom_call", output_to_operand_aliasing={{6}: (4, {}), {7}: (5, {})} | custom-call | flops 2415919104 | bytes 6500376 | tf_op jit(solution)/shard_map/hidden_first/pallas_call | solution.py:180
  174.2 3.6 %hidden_second.1 = (bf16[256,768]{1,0:T(8,128)(2,1)}, f32[256,768]{1,0:T(8,128)S(1)}, f32[1,768]{1,0:T(1,128)S(1)}) custom-call(f32[256,768]{1,0:T(8,128)S(1)} %get-tuple-element.118.x, bf16[256,768]{1,0:T(8,128)(2,1)S(1)} %copy-done.4, f32[8,768]{1,0:T(8,128)S(1)} %copy-done.20, bf16[256,3072]{1,0:T(8,128)(2,1)S(1)} %get-tuple-element.124.act, ...), custom_call_target="tpu_custom_call" | custom-call | flops 2415919104 | bytes 6893568 | tf_op jit(solution)/shard_map/hidden_second/pallas_call | solution.py:180
  178.6 3.9 %weight_grads.3 = (bf16[2,96,3072]{2,1,0:T(8,128)(2,1)S(1)}, bf16[2,96,3072]{2,1,0:T(8,128)(2,1)S(1)}, bf16[2,384,768]{2,1,0:T(8,128)(2,1)S(1)}, bf16[2,384,768]{2,1,0:T(8,128)(2,1)S(1)}) custom-call(s32[12]{0:T(128)S(1)} %stack.66.place, bf16[4,96,256]{2,1,0:T(8,128)(2,1)S(1)} %get-tuple-element.131.refs_0_, ...), custom_call_target="tpu_custom_call" | custom-call | flops 1207959552 | bytes 2949144 | tf_op jit(solution)/shard_map/weight_grads/pallas_call | solution.py:180
  185.5 8.6 %cross_backward.1 = (bf16[256,1536]{1,0:T(8,128)(2,1)S(1)}, bf16[256,1536]{1,0:T(8,128)(2,1)S(1)}, f32[256,768]{1,0:T(8,128)}, f32[256,768]{1,0:T(8,128)S(1)}, f32[1,768]{1,0:T(1,128)S(1)}) custom-call(f32[256,768]{1,0:T(8,128)S(1)} %get-tuple-element.139.grad, f32[256,768]{1,0:T(8,128)S(1)} %copy-done.6, f32[8,768]{1,0:T(8,128)S(1)} %copy-done.20, ...), custom_call_target="tpu_custom_call" | custom-call | flops 1207959552 | bytes 4534272 | tf_op jit(solution)/shard_map/cross_backward/pallas_call | solution.py:180
  194.7 3.2 collective-permute-done.34.refs_1_
  203.6 7.0 %collective-permute-done.39.refs_1_ = bf16[2,96,3072]{2,1,0:T(8,128)(2,1)S(1)} collective-permute-done((bf16[2,96,3072]{2,1,0:T(8,128)(2,1)S(1)}, bf16[2,96,3072]{2,1,0:T(8,128)(2,1)S(1)}, u32[]{:S(2)}, u32[]{:S(2)}) %collective-permute-start.39) | collective-permute-done | bytes 1179680 | tf_op jit(solution)/shard_map/ppermute | solution.py:92
  213.0 9.4 %self_backward.1 = (bf16[256,3072]{1,0:T(8,128)(2,1)S(1)}, f32[256,768]{1,0:T(8,128)}, bf16[4,96,128]{2,1,0:T(8,128)(2,1)S(1)}, bf16[4,96,128]{2,1,0:T(8,128)(2,1)S(1)}) custom-call(s32[12]{0:T(128)S(1)} %stack.66.place, f32[256,768]{1,0:T(8,128)S(1)} %get-tuple-element.162.grad, bf16[256,768]{1,0:T(8,128)(2,1)S(1)} %copy-done.10, f32[8,768]{1,0:T(8,128)S(1)} %copy-done.20, ...), custom_call_target="tpu_custom_call" | custom-call | flops 1207959552 | bytes 4463640 | tf_op jit(solution)/shard_map/self_backward/pallas_call | solution.py:180
  226.4 12.1 %collective-permute-done.43.refs_1_ = bf16[2,96,1536]{2,1,0:T(8,128)(2,1)S(1)} collective-permute-done((bf16[2,96,1536]{2,1,0:T(8,128)(2,1)S(1)}, bf16[2,96,1536]{2,1,0:T(8,128)(2,1)S(1)}, u32[]{:S(2)}, u32[]{:S(2)}) %collective-permute-start.43) | collective-permute-done | bytes 589856 | tf_op jit(solution)/shard_map/ppermute | solution.py:92
  239.1 11.9 %collective-permute-done.41.refs_1_ = bf16[96,3072]{1,0:T(8,128)(2,1)S(1)} collective-permute-done((bf16[96,3072]{1,0:T(8,128)(2,1)S(1)}, bf16[96,3072]{1,0:T(8,128)(2,1)S(1)}, u32[]{:S(2)}, u32[]{:S(2)}) %collective-permute-start.41) | collective-permute-done | bytes 589856 | tf_op jit(solution)/shard_map/ppermute | solution.py:92
  253.7 3.5 %weight_grads.5 = (bf16[2,96,1664]{2,1,0:T(8,128)(2,1)S(1)}, bf16[2,96,1664]{2,1,0:T(8,128)(2,1)}, bf16[2,96,1536]{2,1,0:T(8,128)(2,1)S(1)}, bf16[2,96,1536]{2,1,0:T(8,128)(2,1)}) custom-call(s32[12]{0:T(128)S(1)} %stack.66.place, bf16[4,96,256]{2,1,0:T(8,128)(2,1)S(1)} %copy-done.39, bf16[4,96,256]{2,1,0:T(8,128)(2,1)S(1)} %collective-permute-done.45.refs_1_, ...), custom_call_target="tpu_custom_call" | custom-call | flops 603979776 | bytes 2064408 | tf_op jit(solution)/shard_map/weight_grads/pallas_call | solution.py:180
  265.0 15.9 %collective-permute-done.49 = bf16[96,1536]{1,0:T(8,128)(2,1)} collective-permute-done((bf16[96,1536]{1,0:T(8,128)(2,1)}, bf16[96,1536]{1,0:T(8,128)(2,1)}, u32[]{:S(2)}, u32[]{:S(2)}) %collective-permute-start.49) | collective-permute-done | bytes 294944 | tf_op jit(solution)/shard_map/ppermute | solution.py:92
  291.0 3.9 %collective-permute-done.58 = bf16[24,3072]{1,0:T(8,128)(2,1)S(1)} collective-permute-done((bf16[24,3072]{1,0:T(8,128)(2,1)S(1)}, bf16[24,3072]{1,0:T(8,128)(2,1)S(1)}, u32[]{:S(2)}, u32[]{:S(2)}) %collective-permute-start.58) | collective-permute-done | bytes 147488 | tf_op jit(solution)/shard_map/ppermute | solution.py:86
  294.9 6.6 %collective-permute-done.59 = bf16[24,3072]{1,0:T(8,128)(2,1)S(1)} collective-permute-done((bf16[24,3072]{1,0:T(8,128)(2,1)S(1)}, bf16[24,3072]{1,0:T(8,128)(2,1)S(1)}, u32[]{:S(2)}, u32[]{:S(2)}) %collective-permute-start.59) | collective-permute-done | bytes 147488 | tf_op jit(solution)/shard_map/ppermute | solution.py:86
  302.4 3.7 %collective-permute-start.55 = (bf16[24,3200]{1,0:T(8,128)(2,1)S(1)}, bf16[24,3200]{1,0:T(8,128)(2,1)S(1)}, u32[]{:S(2)}, u32[]{:S(2)}) collective-permute-start(bf16[24,3200]{1,0:T(8,128)(2,1)S(1)} %get-tuple-element.201), channel_id=1, source_target_pairs={{0,1},{1,2},{2,3},{3,0},{4,5},{5,6},{6,7},{7,4},{8,9},{9,10},{10,1... | collective-permute-start | bytes 460808 | tf_op jit(solution)/shard_map/ppermute | solution.py:86
  311.8 5.9 %collective-permute-done.56 = bf16[24,3200]{1,0:T(8,128)(2,1)S(1)} collective-permute-done((bf16[24,3200]{1,0:T(8,128)(2,1)S(1)}, bf16[24,3200]{1,0:T(8,128)(2,1)S(1)}, u32[]{:S(2)}, u32[]{:S(2)}) %collective-permute-start.56) | collective-permute-done | bytes 153632 | tf_op jit(solution)/shard_map/ppermute | solution.py:86
  (261 shorter events, 119.6 us)
Async XLA Ops:
  7.2 52.4 %all-gather.2.cloned.1.call-start = ((), (), s32[]{:S(2)}) async-start(), calls=%async_computation.1 | async-start | bytes 2211840 | tf_op jit(solution)/shard_map/all_gather | solution.py:767
  20.8 299.1 %reduce-scatter.2.cloned.1.call-start = ((), (), s32[]{:S(2)}) async-start(), calls=%async_computation.2 | async-start | bytes 1474560 | tf_op jit(solution)/shard_map/reduce_scatter | solution.py:874
  30.1 30.9 %collective-permute-start.3 = (bf16[96,3200]{1,0:T(8,128)(2,1)S(1)}, bf16[96,3200]{1,0:T(8,128)(2,1)S(1)}, u32[]{:S(2)}, u32[]{:S(2)}) collective-permute-start(bf16[96,3200]{1,0:T(8,128)(2,1)S(1)} %bitcast.75), channel_id=1, source_target_pairs={{0,4},{4,0},{8,12},{12,8},{16,20},{20,16},{24,28},{28,24},{1,5},{5... | collective-permute-start | bytes 1843208 | tf_op jit(solution)/shard_map/ppermute | solution.py:92
  52.2 20.3 %collective-permute-start.5 = (bf16[96,3200]{1,0:T(8,128)(2,1)}, bf16[96,3200]{1,0:T(8,128)(2,1)}, u32[]{:S(2)}, u32[]{:S(2)}) collective-permute-start(bf16[96,3200]{1,0:T(8,128)(2,1)} %collective-permute-done.4.refs_2_), channel_id=1, source_target_pairs={{0,4},{4,0},{8,12},{12,8},{16,20},{20,16},{24,28},{28,24},{1,5},{5... | collective-permute-start | bytes 1843208 | tf_op jit(solution)/shard_map/ppermute | solution.py:92
  52.7 20.3 %collective-permute-start.7 = (bf16[96,3200]{1,0:T(8,128)(2,1)}, bf16[96,3200]{1,0:T(8,128)(2,1)}, u32[]{:S(2)}, u32[]{:S(2)}) collective-permute-start(bf16[96,3200]{1,0:T(8,128)(2,1)} %collective-permute-done.6.refs_4_), channel_id=1, source_target_pairs={{0,4},{4,0},{8,12},{12,8},{16,20},{20,16},{24,28},{28,24},{1,5},{5... | collective-permute-start | bytes 1843208 | tf_op jit(solution)/shard_map/ppermute | solution.py:92
  61.9 43.5 %collective-permute-start.13 = (bf16[192,3072]{1,0:T(8,128)(2,1)S(1)}, bf16[192,3072]{1,0:T(8,128)(2,1)S(1)}, u32[]{:S(2)}, u32[]{:S(2)}) collective-permute-start(bf16[192,3072]{1,0:T(8,128)(2,1)S(1)} %bitcast.66), channel_id=1, source_target_pairs={{0,8},{4,12},{8,0},{12,4},{16,24},{20,28},{24,16},{28,20},{1,9},{5... | collective-permute-start | bytes 3538952 | tf_op jit(solution)/shard_map/ppermute | solution.py:92
  64.0 65.8 %collective-permute-start.15 = (bf16[192,3072]{1,0:T(8,128)(2,1)S(1)}, bf16[192,3072]{1,0:T(8,128)(2,1)S(1)}, u32[]{:S(2)}, u32[]{:S(2)}) collective-permute-start(bf16[192,3072]{1,0:T(8,128)(2,1)S(1)} %bitcast.67), channel_id=1, source_target_pairs={{0,16},{4,20},{8,24},{12,28},{16,0},{20,4},{24,8},{28,12},{1,17},{... | collective-permute-start | bytes 3538952 | tf_op jit(solution)/shard_map/ppermute | solution.py:92
  71.9 32.3 %collective-permute-start.20 = (bf16[384,768]{1,0:T(8,128)(2,1)}, bf16[384,768]{1,0:T(8,128)(2,1)}, u32[]{:S(2)}, u32[]{:S(2)}) collective-permute-start(bf16[384,768]{1,0:T(8,128)(2,1)} %bitcast.32.refs_6_), channel_id=1, source_target_pairs={{0,16},{4,20},{8,24},{12,28},{16,0},{20,4},{24,8},{28,12},{1,17},{... | collective-permute-start | bytes 1769480 | tf_op jit(solution)/shard_map/ppermute | solution.py:92
  72.5 59.0 %collective-permute-start.18 = (bf16[384,768]{1,0:T(8,128)(2,1)}, bf16[384,768]{1,0:T(8,128)(2,1)}, u32[]{:S(2)}, u32[]{:S(2)}) collective-permute-start(bf16[384,768]{1,0:T(8,128)(2,1)} %bitcast.32.refs_6_), channel_id=1, source_target_pairs={{0,8},{4,12},{8,0},{12,4},{16,24},{20,28},{24,16},{28,20},{1,9},{5... | collective-permute-start | bytes 1769480 | tf_op jit(solution)/shard_map/ppermute | solution.py:92
  73.0 58.5 %collective-permute-start.17 = (bf16[384,768]{1,0:T(8,128)(2,1)}, bf16[384,768]{1,0:T(8,128)(2,1)}, u32[]{:S(2)}, u32[]{:S(2)}) collective-permute-start(bf16[384,768]{1,0:T(8,128)(2,1)} %bitcast.32.refs_6_), channel_id=1, source_target_pairs={{0,4},{4,0},{8,12},{12,8},{16,20},{20,16},{24,28},{28,24},{1,5},{5... | collective-permute-start | bytes 1769480 | tf_op jit(solution)/shard_map/ppermute | solution.py:92
  104.2 36.8 %collective-permute-start.12 = (bf16[192,3072]{1,0:T(8,128)(2,1)S(1)}, bf16[192,3072]{1,0:T(8,128)(2,1)}, u32[]{:S(2)}, u32[]{:S(2)}) collective-permute-start(bf16[192,3072]{1,0:T(8,128)(2,1)S(1)} %bitcast.68), channel_id=1, source_target_pairs={{0,4},{4,0},{8,12},{12,8},{16,20},{20,16},{24,28},{28,24},{1,5},{5... | collective-permute-start | bytes 3538952 | tf_op jit(solution)/shard_map/ppermute | solution.py:92
  105.4 39.3 %collective-permute-start.14 = (bf16[192,3072]{1,0:T(8,128)(2,1)S(1)}, bf16[192,3072]{1,0:T(8,128)(2,1)S(1)}, u32[]{:S(2)}, u32[]{:S(2)}) collective-permute-start(bf16[192,3072]{1,0:T(8,128)(2,1)S(1)} %collective-permute-done.13.refs_2_), channel_id=1, source_target_pairs={{0,4},{4,0},{8,12},{12,8},{16,20},{20,16},{24,28},{28,24},{1,5},{5... | collective-permute-start | bytes 3538952 | tf_op jit(solution)/shard_map/ppermute | solution.py:92
  141.0 22.0 %collective-permute-start.28 = (bf16[384,768]{1,0:T(8,128)(2,1)}, bf16[384,768]{1,0:T(8,128)(2,1)}, u32[]{:S(2)}, u32[]{:S(2)}) collective-permute-start(bf16[384,768]{1,0:T(8,128)(2,1)} %collective-permute-done.20.refs_10_), channel_id=1, source_target_pairs={{0,8},{4,12},{8,0},{12,4},{16,24},{20,28},{24,16},{28,20},{1,9},{5... | collective-permute-start | bytes 1769480 | tf_op jit(solution)/shard_map/ppermute | solution.py:92
  143.3 19.9 %collective-permute-start.26 = (bf16[96,3072]{1,0:T(8,128)(2,1)}, bf16[96,3072]{1,0:T(8,128)(2,1)}, u32[]{:S(2)}, u32[]{:S(2)}) collective-permute-start(bf16[96,3072]{1,0:T(8,128)(2,1)} %slice.97), channel_id=1, source_target_pairs={{0,16},{4,20},{8,24},{12,28},{16,0},{20,4},{24,8},{28,12},{1,17},{... | collective-permute-start | bytes 1769480 | tf_op jit(solution)/shard_map/ppermute | solution.py:92
  182.5 28.1 %collective-permute-start.39 = (bf16[2,96,3072]{2,1,0:T(8,128)(2,1)S(1)}, bf16[2,96,3072]{2,1,0:T(8,128)(2,1)S(1)}, u32[]{:S(2)}, u32[]{:S(2)}) collective-permute-start(bf16[2,96,3072]{2,1,0:T(8,128)(2,1)S(1)} %get-tuple-element.136), channel_id=1, source_target_pairs={{0,16},{4,20},{8,24},{12,28},{16,0},{20,4},{24,8},{28,12},{1,17},{... | collective-permute-start | bytes 3538952 | tf_op jit(solution)/shard_map/ppermute | solution.py:92
  184.1 27.7 %collective-permute-start.40 = (bf16[2,384,768]{2,1,0:T(8,128)(2,1)S(1)}, bf16[2,384,768]{2,1,0:T(8,128)(2,1)S(1)}, u32[]{:S(2)}, u32[]{:S(2)}) collective-permute-start(bf16[2,384,768]{2,1,0:T(8,128)(2,1)S(1)} %get-tuple-element.138), channel_id=1, source_target_pairs={{0,8},{4,12},{8,0},{12,4},{16,24},{20,28},{24,16},{28,20},{1,9},{5... | collective-permute-start | bytes 3538952 | tf_op jit(solution)/shard_map/ppermute | solution.py:92
  222.4 31.1 %collective-permute-start.47 = (bf16[256,3072]{1,0:T(8,128)(2,1)S(1)}, bf16[256,3072]{1,0:T(8,128)(2,1)S(1)}, u32[]{:S(2)}, u32[]{:S(2)}) collective-permute-start(bf16[256,3072]{1,0:T(8,128)(2,1)S(1)} %get-tuple-element.172.refs_4_), channel_id=1, source_target_pairs={{0,4},{4,0},{8,12},{12,8},{16,20},{20,16},{24,28},{28,24},{1,5},{5... | collective-permute-start | bytes 4718600 | tf_op jit(solution)/shard_map/ppermute | solution.py:92
  224.4 26.6 %collective-permute-start.41 = (bf16[96,3072]{1,0:T(8,128)(2,1)S(1)}, bf16[96,3072]{1,0:T(8,128)(2,1)S(1)}, u32[]{:S(2)}, u32[]{:S(2)}) collective-permute-start(bf16[96,3072]{1,0:T(8,128)(2,1)S(1)} %get-tuple-element.159), channel_id=1, source_target_pairs={{0,8},{4,12},{8,0},{12,4},{16,24},{20,28},{24,16},{28,20},{1,9},{5... | collective-permute-start | bytes 1769480 | tf_op jit(solution)/shard_map/ppermute | solution.py:92
  225.0 27.6 %collective-permute-start.42 = (bf16[384,768]{1,0:T(8,128)(2,1)S(1)}, bf16[384,768]{1,0:T(8,128)(2,1)S(1)}, u32[]{:S(2)}, u32[]{:S(2)}) collective-permute-start(bf16[384,768]{1,0:T(8,128)(2,1)S(1)} %get-tuple-element.161), channel_id=1, source_target_pairs={{0,16},{4,20},{8,24},{12,28},{16,0},{20,4},{24,8},{28,12},{1,17},{... | collective-permute-start | bytes 1769480 | tf_op jit(solution)/shard_map/ppermute | solution.py:92
  257.3 30.0 %collective-permute-start.51 = (bf16[2,96,1664]{2,1,0:T(8,128)(2,1)}, bf16[2,96,1664]{2,1,0:T(8,128)(2,1)S(1)}, u32[]{:S(2)}, u32[]{:S(2)}) collective-permute-start(bf16[2,96,1664]{2,1,0:T(8,128)(2,1)} %get-tuple-element.187), channel_id=1, source_target_pairs={{0,16},{4,20},{8,24},{12,28},{16,0},{20,4},{24,8},{28,12},{1,17},{... | collective-permute-start | bytes 1916936 | tf_op jit(solution)/shard_map/ppermute | solution.py:92
  258.8 28.6 %collective-permute-start.52 = (bf16[2,96,1536]{2,1,0:T(8,128)(2,1)}, bf16[2,96,1536]{2,1,0:T(8,128)(2,1)S(1)}, u32[]{:S(2)}, u32[]{:S(2)}) collective-permute-start(bf16[2,96,1536]{2,1,0:T(8,128)(2,1)} %get-tuple-element.189), channel_id=1, source_target_pairs={{0,8},{4,12},{8,0},{12,4},{16,24},{20,28},{24,16},{28,20},{1,9},{5... | collective-permute-start | bytes 1769480 | tf_op jit(solution)/shard_map/ppermute | solution.py:92
  260.2 20.6 %collective-permute-start.49 = (bf16[96,1536]{1,0:T(8,128)(2,1)}, bf16[96,1536]{1,0:T(8,128)(2,1)}, u32[]{:S(2)}, u32[]{:S(2)}) collective-permute-start(bf16[96,1536]{1,0:T(8,128)(2,1)} %get-tuple-element.177), channel_id=1, source_target_pairs={{0,8},{4,12},{8,0},{12,4},{16,24},{20,28},{24,16},{28,20},{1,9},{5... | collective-permute-start | bytes 884744 | tf_op jit(solution)/shard_map/ppermute | solution.py:92
  260.8 20.1 %collective-permute-start.50 = (bf16[96,1536]{1,0:T(8,128)(2,1)}, bf16[96,1536]{1,0:T(8,128)(2,1)}, u32[]{:S(2)}, u32[]{:S(2)}) collective-permute-start(bf16[96,1536]{1,0:T(8,128)(2,1)} %get-tuple-element.179), channel_id=1, source_target_pairs={{0,16},{4,20},{8,24},{12,28},{16,0},{20,4},{24,8},{28,12},{1,17},{... | collective-permute-start | bytes 884744 | tf_op jit(solution)/shard_map/ppermute | solution.py:92
  283.2 18.3 %collective-permute-start.59 = (bf16[24,3072]{1,0:T(8,128)(2,1)S(1)}, bf16[24,3072]{1,0:T(8,128)(2,1)S(1)}, u32[]{:S(2)}, u32[]{:S(2)}) collective-permute-start(bf16[24,3072]{1,0:T(8,128)(2,1)S(1)} %get-tuple-element.193), channel_id=1, source_target_pairs={{0,2},{1,3},{2,0},{3,1},{4,6},{5,7},{6,4},{7,5},{8,10},{9,11},{10,... | collective-permute-start | bytes 442376 | tf_op jit(solution)/shard_map/ppermute | solution.py:86
  (90 other events, 727.2 us)
Sparse Core Ops, SparseCore 0:
  20.9 38.6 all-gather.1
  265.1 32.7 reduce-scatter.1
where the time goes:
time: 331 us; the launch traced here: 329 us
  waiting for transfers between devices  147 us (44%)
  Pallas kernels  67.9 us (21%)
  starting transfers between devices  49.1 us (15%)
  local copies, waits for them, and re-layouts  47 us (14%)
  between operations  14.7 us (4%)
  other arithmetic  3.68 us (1%)
    ppermute x52, waiting for transfers between devices, shifted(): return lax.ppermute(array, 'wide', pairs)  117 us
    pallas_call x16, Pallas kernels, run(): pl.pallas_call(kernel, name=name, in_specs=[pl.BlockSpec(memory_space=spa...  67.9 us
    ppermute x52, starting transfers between devices, shifted(): return lax.ppermute(array, 'wide', pairs)  31.7 us
    ppermute x9, waiting for transfers between devices, shifted(): lax.ppermute(array, 'narrow', [(i, (i + step) % count) for i in range(cou...  25 us
    unnamed x104, local copies, waits for them, and re-layouts  25 us
    ppermute x9, starting transfers between devices, shifted(): lax.ppermute(array, 'narrow', [(i, (i + step) % count) for i in range(cou...  17.4 us
  transfers between devices with their start and end apart: 63, of which 26 were waited for; matrix products, arithmetic and copies ran while one was open for 7% of the time, Pallas kernels for 13%

commit v1 on v0

v1 whole, which is shorter than its diff:
```python
import math

import jax
import jax.numpy as jnp
import numpy as np
from jax import lax
from jax.experimental import pallas as pl
from jax.experimental.pallas import tpu as pltpu
from jax.sharding import PartitionSpec as P

BUCKETS = 32
REACH = 128
LOW = jnp.bfloat16
F32 = jnp.float32
NN = (((1,), (0,)), ((), ()))
NT = (((1,), (1,)), ((), ()))
TN = (((0,), (0,)), ((), ()))
PAIRS = 6
LANES = 128
TABLE_LANE = 16
CHUNK = 384
MiB = 1024 * 1024
FIRST_AT = 4
ORDER_AT = 12
EARLY = 0.75
EARLY_GRAD = 0.5


def bucket_edges(bucket_count, far_reach):
    exact_span = bucket_count // 2
    edge_list = list(range(1, exact_span + 1))
    for target in range(exact_span + 1, bucket_count):
        distance = exact_span
        while (
            exact_span
            + int(
                math.log(distance / exact_span)
                / math.log(far_reach / exact_span)
                * (bucket_count - exact_span)
            )
            < target
        ):
            distance += 1
        edge_list.append(distance)
    return edge_list


def rolled_one_hot(rows):
    edges = np.array(bucket_edges(BUCKETS, REACH))
    distances = (rows - np.arange(rows)) % rows
    buckets = (distances[:, None] >= edges[None, :]).sum(axis=1)
    return (np.arange(BUCKETS)[:, None] == buckets[None, :]).astype(np.float32)


def table_hot(rows, blocks, share, table_rows):
    one_hot = rolled_one_hot(rows)
    groups = -(-table_rows // share)
    hot = np.zeros((groups, blocks * share, rows), np.float32)
    for block in range(blocks):
        for row in range(table_rows):
            hot[row // share, block * share + row % share] = one_hot[block * table_rows + row]
    return hot


def grid_sizes():
    wide = lax.axis_size("wide")
    inner = wide // 2
    across = 1
    while across * across < inner:
        across *= 2
    return {"y": inner // across, "x": across, "c": 2, "z": lax.axis_size("narrow")}


def grid_place():
    sizes = grid_sizes()
    wide = lax.axis_index("wide")
    return {
        "y": wide // (2 * sizes["x"]),
        "x": (wide // 2) % sizes["x"],
        "c": wide % 2,
        "z": lax.axis_index("narrow"),
    }


def shifted(array, dim, step):
    sizes = grid_sizes()
    count = sizes[dim]
    if dim == "z":
        return lax.ppermute(array, "narrow", [(i, (i + step) % count) for i in range(count)])
    stride = {"y": 2 * sizes["x"], "x": 2, "c": 1}[dim]
    pairs = []
    for source in range(lax.axis_size("wide")):
        place = (source // stride) % count
        pairs.append((source, source + ((place + step) % count - place) * stride))
    return lax.ppermute(array, "wide", pairs)


def after(value, *earlier):
    return lax.optimization_barrier((value, *earlier))[0]


def received(block, dim):
    count = grid_sizes()[dim]
    return [shifted(block, dim, count - step) for step in range(1, count)]


def swapped(array):
    return shifted(array, "c", 1)


def in_order(block, others, dim, axis):
    here = grid_place()[dim]
    cyclic = [block] + others
    count = len(cyclic)
    ordered = []
    for place in range(count):
        picked = cyclic[0]
        for step in range(1, count):
            picked = jnp.where((here + step) % count == place, cyclic[step], picked)
        ordered.append(picked)
    return jnp.stack(ordered, axis)


class Weights:
    def __init__(self, arrays, spots):
        self.arrays = arrays
        self.spots = spots

    def load(self, place, refs, matrices, sems, ranges=None):
        waits = []
        count = 0
        for low, high in ranges or [(0, None)]:
            copies = []
            for source, first, column, at, block, row, rows, matrix, there, cols in self.spots:
                start = row if at is None else pl.multiple_of(place[at] * block, block) + row
                from_column, to_column, size = column + low, there + low, (high or cols) - low
                copies.append(
                    pltpu.make_async_copy(
                        refs[source].at[pl.ds(first, rows), pl.ds(from_column, size)],
                        matrices[matrix].at[pl.ds(start, rows), pl.ds(to_column, size)],
                        sems.at[count],
                    )
                )
                count += 1
            for copy in copies:
                copy.start()
            waits.append(lambda copies=copies: [copy.wait() for copy in copies])
        return waits

    def sems(self, ranges=1):
        return [pltpu.SemaphoreType.DMA((max(len(self.spots) * ranges, 1),))]


def fetch(sources, targets, sems):
    copies = [pltpu.make_async_copy(a, b, sems.at[n]) for n, (a, b) in enumerate(zip(sources, targets))]
    for copy in copies:
        copy.start()
    return [copy.wait for copy in copies]


def in_pieces(block):
    sizes = grid_sizes()
    return sizes["y"] == 2 and sizes["x"] == 2 and block % 32 == 0


def from_neighbours(block):
    return [block, shifted(block, "x", 1), shifted(block, "y", 1)]


def from_corner(upper, lower):
    return [shifted(upper, "y", 1), shifted(lower, "x", 1)]


def gather_pieces(block, *earlier, near=None):
    near = near or from_neighbours(block)
    half = block.shape[0] // 2
    twins = [swapped(near[0])]
    near_x, near_y = (after(array, twins[0], *earlier) for array in near[1:])
    corner = [shifted(near_x[:half], "y", 1), shifted(near_y[half:], "x", 1)]
    twins += [swapped(near_x), swapped(near_y)]
    return near, twins, corner


def pairs(near, twins):
    return [array for pair in zip(near, twins) for array in pair]


def gather_whole(block):
    block = in_order(block, received(block, "x"), "x", 0)
    block = in_order(block, received(block, "y"), "y", 0)
    block = in_order(block, received(block, "c"), "c", 2)
    return block.reshape(-1, block.shape[-1])


def near_spots(sources, block, column, matrix, there, cols):
    return [
        (source, 0, column, FIRST_AT + n, block, 0, block, matrix, there, cols) for n, source in enumerate(sources)
    ]


def half_spots(sources, block, column, matrix, there, cols):
    half = block // 2
    return [
        (source, 0, column, FIRST_AT + 6 + n % 2, block, (n // 2) * half, half, matrix, there, cols)
        for n, source in enumerate(sources)
    ]


def folded_spots(spots, block, column, groups, width, matrix):
    return [
        (source, first, column + g * width, at, groups * block, g * block + row, rows, matrix, 0, width)
        for source, first, _, at, _, row, rows, *_ in spots
        for g in range(groups)
    ]


def with_twins(arrays):
    return [array for own in arrays for array in (own, swapped(own))]


def run(name, kernel, inputs, outputs, scratch=(), flops=0, weights=(), aliases=()):
    inputs = list(inputs)
    for group in weights:
        inputs += [(array, pltpu.HBM) for array in group.arrays]
    size = sum(math.prod(array.shape) * array.dtype.itemsize for array, _ in inputs)
    arrays = [
        array if space == pltpu.SMEM else pltpu.with_memory_space_constraint(array, space)
        for array, space in inputs
    ]
    shapes = [
        jax.ShapeDtypeStruct(*output[:2]) if len(output) > 2 else pltpu.VMEM(*output) for output in outputs
    ]
    return pl.pallas_call(
        kernel,
        name=name,
        in_specs=[pl.BlockSpec(memory_space=space) for _, space in inputs],
        out_specs=[pl.BlockSpec(memory_space=pltpu.VMEM) for _ in outputs],
        out_shape=shapes,
        scratch_shapes=list(scratch),
        input_output_aliases=dict(aliases),
        compiler_params=pltpu.CompilerParams(vmem_limit_bytes=24 * MiB),
        cost_estimate=pl.CostEstimate(flops=flops, bytes_accessed=size // 2, transcendentals=0),
    )(*arrays)


def vmem(*arrays):
    return [(array, pltpu.VMEM) for array in arrays]


def dot(left, right, dims=NN):
    return lax.dot_general(left, right, dims, preferred_element_type=F32)


def scale_of(values):
    return lax.rsqrt(jnp.mean(values * values, axis=-1, keepdims=True) + 1e-06)


def norm_back(values, gain, grad):
    scale = scale_of(values)
    weighted = grad * gain
    middle = jnp.mean(values * weighted, axis=-1, keepdims=True)
    return (
        scale * weighted - values * (scale * scale * scale * middle),
        jnp.sum(grad * values * scale, axis=0, keepdims=True),
    )


def split_rows(matrix, core, keep, send):
    count, rows, _ = keep.shape
    if rows % 16:
        matrix = matrix.astype(F32)
    pieces = [matrix[n * rows : (n + 1) * rows].astype(keep.dtype) for n in range(2 * count)]

    @pl.when(core == 0)
    def _():
        for n in range(count):
            keep[n] = pieces[2 * n]
            send[n] = pieces[2 * n + 1]

    @pl.when(core == 1)
    def _():
        for n in range(count):
            keep[n] = pieces[2 * n + 1]
            send[n] = pieces[2 * n]


def lanes_of(pair, column=0):
    return pl.ds(pl.multiple_of(column + pair * LANES, LANES), LANES)


def head_mask(rows, head):
    lanes = lax.broadcasted_iota(jnp.int32, (rows, LANES), 1)
    return (lanes >= 64) if head else (lanes < 64)


def attend(q_ref, k_ref, v_ref, columns, allowed, bias, prob_ref, out_ref):
    rows = q_ref.shape[0]
    cols = k_ref.shape[0]

    def step(pair, carry):
        q = q_ref[:, lanes_of(pair, columns[0])]
        k = k_ref[:, lanes_of(pair, columns[1])]
        v = v_ref[:, lanes_of(pair, columns[2])]
        result = None
        for head in range(2):
            mine = head_mask(rows, head)
            scores = dot(jnp.where(mine, q, jnp.zeros_like(q)), k, NT)
            if bias is not None:
                row = jnp.broadcast_to(bias[pl.ds(2 * pair + head, 1), :], (rows, cols))
                scores = scores + pltpu.roll(row, 0, 1, stride=1, stride_axis=0)
            scores = jnp.where(allowed[...] > 0, scores, -1e9)
            weights = jnp.exp(scores - jnp.max(scores, axis=1, keepdims=True))
            probs = (weights * (1.0 / jnp.sum(weights, axis=1, keepdims=True))).astype(LOW)
            prob_ref[2 * pair + head] = probs
            part = dot(probs, v)
            result = part if head == 0 else jnp.where(mine, part, result)
        out_ref[:, lanes_of(pair)] = result.astype(LOW)
        return carry

    lax.fori_loop(0, PAIRS, step, 0)


def attend_back(q_ref, k_ref, v_ref, columns, g_ref, prob_ref, outs, dist_ref):
    rows = q_ref.shape[0]
    cols = k_ref.shape[0]

    def step(pair, carry):
        q = q_ref[:, lanes_of(pair, columns[0])]
        k = k_ref[:, lanes_of(pair, columns[1])]
        v = v_ref[:, lanes_of(pair, columns[2])]
        g = g_ref[:, lanes_of(pair)]
        if dist_ref is not None:
            i = lax.broadcasted_iota(jnp.int32, (rows, rows), 0)
            j = lax.broadcasted_iota(jnp.int32, (rows, rows), 1)
            flip = (i + j == rows - 1).astype(LOW)
        grads = None
        for head in range(2):
            mine = head_mask(rows, head)
            low_probs = prob_ref[2 * pair + head]
            probs = low_probs.astype(F32)
            moved = probs * dot(jnp.where(mine, g, jnp.zeros_like(g)), v, NT)
            low_scores = (moved - probs * jnp.sum(moved, axis=1, keepdims=True)).astype(LOW)
            if dist_ref is not None:
                lined = pltpu.roll(dot(flip, low_scores), 1, 1, stride=1, stride_axis=0)
                dist_ref[pl.ds(2 * pair + head, 1), :] = jnp.sum(lined, axis=0, keepdims=True)
            new = (dot(low_scores, k), dot(low_scores, q, TN), dot(low_probs, g, TN))
            grads = new if head == 0 else tuple(jnp.where(mine, b, a) for a, b in zip(grads, new))
        for (ref, column), grad in zip(outs, grads):
            ref[:, lanes_of(pair, column)] = grad.astype(LOW)
        return carry

    lax.fori_loop(0, PAIRS, step, 0)


def head_lanes(group, heads):
    head = lax.broadcasted_iota(jnp.int32, (16, LANES), 0)
    lane = lax.broadcasted_iota(jnp.int32, (16, LANES), 1)
    return ((head < heads) & (lane == TABLE_LANE + group * heads + head)).astype(F32)


def self_forward(place, tokens, row_ids, col_ids, pad, hot, weights, cut, block):
    rows, width = tokens.shape
    count = len(weights.arrays)
    heads = 2 * PAIRS
    groups = hot.shape[0]
    blocks = (width // block) // 2

    def kernel(place, tok, row_ids, col_ids, pad, hot, *refs):
        pieces, refs = refs[:count], refs[count:]
        qk, v, probs, out, keep, send, gains, matrix, allowed, bias, att, sems = refs
        wait, wait_late = weights.load(place, pieces, [matrix], sems, [(0, cut), (cut, cut + 2 * width)])
        i = lax.broadcasted_iota(jnp.int32, (rows, rows), 0)
        j = lax.broadcasted_iota(jnp.int32, (rows, rows), 1)
        same = (row_ids[...] == col_ids[...]) & (j <= i) & ((pad[...] == 1) | (i == j))
        allowed[...] = same.astype(F32)
        residual = tok[...].astype(F32)
        scaled = residual * scale_of(residual)
        wait()
        extra = matrix[:, 2 * width : cut].astype(F32)
        gains[...] = extra.T[:8]
        normed = (scaled * gains[0:1, :]).astype(LOW)
        total = None
        for group in range(groups):
            table = dot(extra[: hot.shape[1]], head_lanes(group, heads), NT)
            part = dot(table.astype(LOW), hot[group], TN)
            total = part if total is None else total + part
        bias[...] = total
        split_rows(normed.T, place[2], keep.at[0], send.at[0])
        qk[...] = dot(normed, matrix[:, : 2 * width]).astype(LOW)
        wait_late()
        v[...] = dot(normed, matrix[:, cut : cut + width]).astype(LOW)
        attend(qk, qk, v, (0, width, 0), allowed, bias, probs, att)
        attended = att[...]
        split_rows(attended.T, place[2], keep.at[1], send.at[1])
        out[...] = residual + dot(attended, matrix[:, cut + width :])

    halves = ((2, blocks, block, rows), LOW)
    return run(
        "self_forward",
        kernel,
        [(place, pltpu.SMEM)] + vmem(tokens, row_ids, col_ids, pad, hot),
        [
            ((rows, 2 * width), LOW, None),
            ((rows, width), LOW, None),
            ((heads, rows, rows), LOW, None),
            ((rows, width), F32, None),
            halves,
            halves,
            ((8, width), F32),
        ],
        [
            pltpu.VMEM((width, cut + 2 * width), LOW),
            pltpu.VMEM((rows, rows), F32),
            pltpu.VMEM((16, rows), F32),
            pltpu.VMEM((rows, width), LOW),
        ]
        + weights.sems(2),
        flops=8 * rows * width * width,
        weights=[weights],
    )


def cross_forward(place, after_self, memory, gains, row_ids, col_ids, weights, block):
    rows, width = after_self.shape
    mem_rows = memory.shape[0]
    count = len(weights.arrays)
    blocks = (width // block) // 2

    def kernel(place, x, mem, gains, row_ids, col_ids, *refs):
        pieces, refs = refs[:count], refs[count:]
        q, kv, probs, out, keep, send, matrix, allowed, att, sems = refs
        wait, wait_late = weights.load(place, pieces, [matrix], sems, [(2 * width, 4 * width), (0, 2 * width)])
        allowed[...] = (row_ids[...] == col_ids[...]).astype(F32)
        residual = x[...]
        normed = (residual * scale_of(residual) * gains[1:2, :]).astype(LOW)
        split_rows(normed.T, place[2], keep.at[0], send.at[0])
        split_rows(mem[...].T, place[2], keep.at[2], send.at[2])
        wait()
        kv[...] = dot(mem[...], matrix[:, 2 * width :]).astype(LOW)
        wait_late()
        q[...] = dot(normed, matrix[:, :width]).astype(LOW)
        attend(q, kv, kv, (0, 0, width), allowed, None, probs, att)
        attended = att[...]
        split_rows(attended.T, place[2], keep.at[1], send.at[1])
        out[...] = residual + dot(attended, matrix[:, width : 2 * width])

    halves = ((3, blocks, block, rows), LOW)
    return run(
        "cross_forward",
        kernel,
        [(place, pltpu.SMEM)] + vmem(after_self, memory, gains, row_ids, col_ids),
        [
            ((rows, width), LOW, None),
            ((mem_rows, 2 * width), LOW, None),
            ((2 * PAIRS, rows, mem_rows), LOW, None),
            ((rows, width), F32),
            halves,
            halves,
        ],
        [
            pltpu.VMEM((width, 4 * width), LOW),
            pltpu.VMEM((rows, mem_rows), F32),
            pltpu.VMEM((rows, width), LOW),
        ]
        + weights.sems(2),
        flops=8 * rows * width * width,
        weights=[weights],
    )


def hidden_order(nz, share, groups):
    units = np.arange(CHUNK).reshape(-1, nz, groups, share)
    order = np.transpose(units, (0, 2, 1, 3)).reshape(-1)
    matrix = np.zeros((CHUNK, CHUNK), np.float32)
    matrix[order, np.arange(CHUNK)] = 1.0
    return jnp.asarray(matrix).astype(LOW)


def reorder(array, order, dims, kind):
    def kernel(array, order, out):
        for start in range(0, array.shape[1], CHUNK):
            out[:, start : start + CHUNK] = dot(array[:, start : start + CHUNK], order[...], dims).astype(kind)

    return run("reorder", kernel, vmem(array, order), [(array.shape, kind, None)])[0]


def hidden_early(place, weights, width, ff):
    count = len(weights.arrays)

    def kernel(place, *refs):
        weights.load(place, refs[:count], refs[count : count + 2], refs[count + 2])[0]()

    return run(
        "hidden_early",
        kernel,
        [(place, pltpu.SMEM)],
        [((width, ff), LOW), ((ff, width), LOW)],
        weights.sems(),
        weights=[weights],
    )


def hidden_first(place, after_cross, out_grad, gains, m_in, m_out, weights, block):
    rows, width = after_cross.shape
    ff = m_in.shape[1]
    count = len(weights.arrays)
    blocks = (width // block) // 2
    ff_block = ff // (2 * blocks)
    factor = math.sqrt(2.0 / math.pi)

    def kernel(place, x, og, gains, m_in_before, m_out_before, *refs):
        pieces, refs = refs[:count], refs[count:]
        act, gu, keep, send, m_in, m_out, sems = refs
        (wait,) = weights.load(place, pieces, [m_in, m_out], sems)
        residual = x[...]
        normed = (residual * scale_of(residual) * gains[2:3, :]).astype(LOW)
        split_rows(normed.T, place[2], keep.at[:, :block], send.at[:, :block])
        grad = og[...]
        wait()
        for start in range(0, ff, CHUNK):
            stop = start + CHUNK
            u = dot(normed, m_in[:, start:stop])
            ga = dot(grad, m_out[start:stop, :], NT).astype(LOW).astype(F32)
            square = u * u
            t = jnp.tanh(factor * u * (1.0 + 0.044715 * square))
            half = 0.5 * (1.0 + t)
            a = (u * half).astype(LOW)
            slope = half + (0.5 * factor) * u * (1.0 - t * t) * (1.0 + 3 * 0.044715 * square)
            gu[:, start:stop] = (slope * ga).astype(LOW)
            act[:, start:stop] = a
            turned = a.T
            for first in range(start, stop, ff_block):
                n = first // ff_block
                piece = turned[first - start : first - start + ff_block]

                @pl.when(place[2] == n % 2)
                def _(n=n, piece=piece):
                    keep[n // 2, block:] = piece

                @pl.when(place[2] != n % 2)
                def _(n=n, piece=piece):
                    send[n // 2, block:] = piece

    halves = ((blocks, block + ff_block, rows), LOW)
    return run(
        "hidden_first",
        kernel,
        [(place, pltpu.SMEM)] + vmem(after_cross, out_grad, gains, m_in, m_out),
        [
            ((rows, ff), LOW),
            ((rows, ff), LOW),
            halves,
            halves,
            (m_in.shape, LOW),
            (m_out.shape, LOW),
        ],
        weights.sems(),
        flops=4 * rows * width * ff,
        weights=[weights],
        aliases={4: 4, 5: 5},
    )


def hidden_second(after_cross, out_grad, gains, act, gu, m_in, m_out):
    rows, width = after_cross.shape
    ff = m_in.shape[1]

    def kernel(x, og, gains, act, gu, m_in, m_out, out, back_out, branch, gain_out):
        residual = x[...]
        back, gain = norm_back(residual, gains[2:3, :], dot(gu[...], m_in[...], NT))
        grad = og[...].astype(F32) + back
        back_out[...] = grad
        branch[...] = grad.astype(LOW)
        gain_out[...] = gain
        out[...] = (residual + dot(act[...], m_out[...])).astype(LOW)

    return run(
        "hidden_second",
        kernel,
        vmem(after_cross, out_grad, gains, act, gu, m_in, m_out),
        [((rows, width), LOW, None), ((rows, width), F32, None), ((rows, width), LOW, None), ((1, width), F32)],
        flops=4 * rows * width * ff,
    )


def cross_backward(place, grad, branch, after_self, gains, q, kv, probs, weights):
    rows, width = after_self.shape
    mem_rows = kv.shape[0]

    count = len(weights.arrays)

    def kernel(place, gains, *refs):
        far, refs = refs[:6], refs[6:]
        pieces, refs = refs[:count], refs[count:]
        out, mem_grad, back_out, gain_out, branch, grad, x, q, kv, probs, matrix, att, own_sems, sems = refs
        ranges = [(width, 2 * width), (0, width), (2 * width, 4 * width)]
        branch_wait = fetch(far[:1], (branch,), own_sems)
        loaded = weights.load(place, pieces, [matrix], sems, ranges)
        waits = fetch(far[1:], (kv, probs, q, x, grad), own_sems.at[pl.ds(1, 5)])
        branch_wait[0]()
        loaded[0]()
        att[...] = dot(branch[...], matrix[:, width : 2 * width], NT).astype(LOW)
        outs = ((out, 0), (out, width), (out, 2 * width))
        for wait in waits:
            wait()
        attend_back(q, kv, kv, (0, 0, width), att, probs, outs, None)
        loaded[1]()
        loaded[2]()
        back, gain = norm_back(x[...], gains[1:2, :], dot(out[:, :width], matrix[:, :width], NT))
        total = grad[...] + back
        back_out[...] = total
        out[:, 3 * width :] = total.astype(LOW)
        gain_out[...] = gain
        mem_grad[...] = dot(out[:, width : 3 * width], matrix[:, 2 * width :], NT)

    return run(
        "cross_backward",
        kernel,
        [(place, pltpu.SMEM)]
        + vmem(gains)
        + [(array, pltpu.HBM) for array in (branch, kv, probs, q, after_self, grad)],
        [
            ((rows, 4 * width), LOW),
            ((mem_rows, width), F32, None),
            ((rows, width), F32),
            ((1, width), F32),
        ],
        [
            pltpu.VMEM((rows, width), LOW),
            pltpu.VMEM((rows, width), F32),
            pltpu.VMEM((rows, width), F32),
            pltpu.VMEM((rows, width), LOW),
            pltpu.VMEM((mem_rows, 2 * width), LOW),
            pltpu.VMEM((2 * PAIRS, rows, mem_rows), LOW),
            pltpu.VMEM((width, 4 * width), LOW),
            pltpu.VMEM((rows, width), LOW),
            pltpu.SemaphoreType.DMA((6,)),
        ]
        + weights.sems(3),
        flops=8 * rows * width * width,
        weights=[weights],
    )


def self_backward(place, grad, cross_grads, tokens, gains, cross_gain, hidden_gain, qk, v, probs, hot, weights, cut, block):
    rows, width = tokens.shape
    count = len(weights.arrays)
    heads = 2 * PAIRS
    groups = hot.shape[0]
    blocks = (width // block) // 2

    def kernel(place, grad, before, tok, gains, cross_gain, hidden_gain, hot, qk_far, v_far, probs_far, *refs):
        pieces, refs = refs[:count], refs[count:]
        out, out_v, tok_grad, extra_keep, extra_send, qk, v, probs, matrix, att, dist, parts, own_sems, sems = refs
        ranges = [(cut + width, cut + 2 * width), (0, cut + width)]
        loaded = weights.load(place, pieces, [matrix], sems, ranges)
        waits = fetch((v_far, probs_far, qk_far), (v, probs, qk), own_sems)
        loaded[0]()
        att[...] = dot(before[:, 3 * width :], matrix[:, cut + width :], NT).astype(LOW)
        outs = ((out, 0), (out, width), (out_v, 0))
        dist[...] = jnp.zeros_like(dist)
        for wait in waits:
            wait()
        attend_back(qk, qk, v, (0, width, 0), att, probs, outs, dist)
        loaded[1]()
        normed_grad = dot(out[...], matrix[:, : 2 * width], NT)
        normed_grad = normed_grad + dot(out_v[...], matrix[:, cut : cut + width], NT)
        back, gain = norm_back(tok[...].astype(F32), gains[0:1, :], normed_grad)
        tok_grad[...] = grad[...] + back
        parts[...] = jnp.zeros_like(parts)
        parts[0:1, :] = gain
        parts[1:2, :] = cross_gain[...]
        parts[2:3, :] = hidden_gain[...]
        columns = parts[...].T
        table = None
        for group in range(groups):
            sums = lax.dot_general(
                hot[group].astype(F32), dist[...], NT, precision=lax.Precision.HIGHEST, preferred_element_type=F32
            )
            part = lax.dot_general(
                sums, head_lanes(group, heads), NN, precision=lax.Precision.HIGHEST, preferred_element_type=F32
            )
            table = part if table is None else table + part
        columns = columns + jnp.concatenate([table] * (2 * blocks), axis=0)
        split_rows(columns, place[2], extra_keep, extra_send)

    halves = ((blocks, block, LANES), LOW)
    return run(
        "self_backward",
        kernel,
        [(place, pltpu.SMEM)]
        + vmem(grad, cross_grads, tokens, gains, cross_gain, hidden_gain, hot)
        + [(array, pltpu.HBM) for array in (qk, v, probs)],
        [((rows, 2 * width), LOW), ((rows, width), LOW), ((rows, width), F32, None), halves, halves],
        [
            pltpu.VMEM((rows, 2 * width), LOW),
            pltpu.VMEM((rows, width), LOW),
            pltpu.VMEM((heads, rows, rows), LOW),
            pltpu.VMEM((width, cut + 2 * width), LOW),
            pltpu.VMEM((rows, width), LOW),
            pltpu.VMEM((16, rows), F32),
            pltpu.VMEM((LANES, width), F32),
            pltpu.SemaphoreType.DMA((3,)),
        ]
        + weights.sems(2),
        flops=8 * rows * width * width,
        weights=[weights],
    )


def weight_grads(place, lefts, rights, sections, cols, extras=(), straight=()):
    sizes = grid_sizes()
    counts = (sizes["y"], sizes["x"])
    blocks = counts[0] * counts[1]
    nz = sizes["z"]
    left_count, right_count = len(lefts), len(rights)
    block = min(section[0][3] for section in (*sections, *straight))
    across_z = sum(section[3] * (section[0][3] // block) for section in straight)
    tokens = rights[0][0].shape[0]
    most = max(section[0][3] for section in (*sections, *straight))

    def kernel(place, *refs):
        refs = list(refs)
        left = [(refs.pop(0), refs.pop(0)) for _ in range(left_count)]
        right = [(refs.pop(0), refs.pop(0)) for _ in range(right_count)]
        extra = [refs.pop(0) for _ in extras]
        gathered = refs.pop()
        outs = (refs[: counts[0]], refs[counts[0] : counts[0] + counts[1]])
        out_z = refs[-1]

        def place_of(half, n):
            step, other = n // counts[1 - half], n % counts[1 - half]
            there = (place[half] + step) % counts[half]
            return there * counts[1] + other if half == 0 else other * counts[1] + there

        def products(section, order):
            (l, n, row, rows), r, column, width = section[:4]
            joined = rows % 16 == 0 and row % 16 == 0
            if joined:
                for k in range(blocks):
                    for side in range(2):
                        gathered[k * rows : (k + 1) * rows, side * tokens : (side + 1) * tokens] = left[l][side][
                            n, order(k), row : row + rows, :
                        ]
            for first in range(0, width, 768):
                size = min(768, width - first)
                own, far = (ref[:, column + first : column + first + size] for ref in right[r])
                if joined:
                    total = dot(gathered[: blocks * rows, :tokens], own)
                    total = total + dot(gathered[: blocks * rows, tokens:], far)
                for k in range(blocks):
                    if joined:
                        yield first, size, k, total[k * rows : (k + 1) * rows]
                        continue
                    own_rows, far_rows = (ref[n, order(k), row : row + rows, :] for ref in left[l])
                    yield first, size, k, dot(own_rows, own) + dot(far_rows, far)

        for section in straight:
            for first, size, index, total in products(section, lambda k: k):
                for g in range(section[0][3] // block):
                    at = section[5] + g * section[3] + first
                    for z in range(nz):
                        row = g * block + z * block // nz
                        part = total[row : row + block // nz]
                        out_z[z, index, :, at : at + size] = part.astype(LOW)
        for section in sections:
            groups = section[0][3] // block
            half = section[4]
            for first, size, k, total in products(section, lambda k: place_of(half, k)):
                for g in range(groups):
                    at = section[5] + g * section[3] + first
                    part = total[g * block : (g + 1) * block].astype(LOW)
                    outs[half][k // counts[1 - half]][k % counts[1 - half], :, at : at + size] = part
        for k in range(blocks if extras else 0):
            index = place_of(0, k)
            both = extra[0][index].astype(F32) + extra[1][index].astype(F32)
            outs[0][k // counts[1]][k % counts[1], :, cols[0] - LANES :] = both.astype(LOW)

    arrays = [array for pair in lefts for array in pair] + [array for pair in rights for array in pair]
    outputs = []
    if sections:
        outputs += [((counts[1], block, cols[0]), LOW)] * counts[0]
        outputs += [((counts[0], block, cols[1]), LOW)] * counts[1]
    if straight:
        outputs.append(((nz, blocks, block // nz, across_z), LOW, None))
    return run(
        "weight_grads",
        kernel,
        [(place, pltpu.SMEM)] + vmem(*arrays, *extras),
        outputs,
        [pltpu.VMEM((blocks * most, 2 * tokens), LOW)],
        flops=sum(4 * s[0][3] * blocks * rights[0][0].shape[0] * s[3] for s in (*sections, *straight)),
    )


def add_stage(place, firsts, seconds):
    sizes = grid_sizes()
    counts = (sizes["x"], sizes["y"])

    def kernel(place, *refs):
        halves = (refs[: len(firsts)], refs[len(firsts) : len(firsts) + len(seconds)])
        outs = refs[len(firsts) + len(seconds) :]
        outs = (outs[: counts[0]], outs[counts[0] :])
        for half in range(2):
            here = place[1 - half]
            for step in range(counts[half]):
                index = (here + step) % counts[half]
                total = halves[half][0][index].astype(F32)
                for part in halves[half][1:]:
                    total = total + part[index].astype(F32)
                outs[half][step][...] = total.astype(LOW)

    outputs = [(firsts[0].shape[1:], LOW)] * counts[0] + [(seconds[0].shape[1:], LOW)] * counts[1]
    return run("add_stage", kernel, [(place, pltpu.SMEM)] + vmem(*firsts, *seconds), outputs)


def add_last(place, halves):
    count = grid_sizes()["z"]
    share = halves[0][0].shape[0] // count
    halves = [[part.reshape(count, share, part.shape[-1]) for part in parts] for parts in halves]
    cols = [parts[0].shape[-1] for parts in halves]

    def kernel(place, *refs):
        refs = list(refs)
        first = 0
        inputs = [[refs.pop(0) for _ in parts] for parts in halves]
        for parts, size in zip(inputs, cols):
            for step in range(count):
                index = (place[3] + step) % count
                total = parts[0][index].astype(F32)
                for part in parts[1:]:
                    total = total + part[index].astype(F32)
                refs[step][:, first : first + size] = total.astype(LOW)
            first += size

    return run(
        "add_last",
        kernel,
        [(place, pltpu.SMEM)] + vmem(*[part for parts in halves for part in parts]),
        [((share, sum(cols)), LOW)] * count,
    )


def mirrored(place, count):
    return place - place % count + count - 1 - place % count


def halving_order(place, count):
    order = [place]
    while len(order) < count:
        size = count // len(order)
        order += [mirrored(block, size) for block in order]
    return order


def halve(place, sides, count, first):
    have = sides[0][0].shape[0]
    half = have // 2
    cols = [parts[0].shape[2] for parts in sides]
    shape = (half, sides[0][0].shape[1], sum(cols))

    def kernel(place, *refs):
        refs = list(refs)
        inputs = [[refs.pop(0) for _ in parts] for parts in sides]
        order = halving_order(place[3], have) if first else range(have)
        for n in range(have):
            at = 0
            for parts, size in zip(inputs, cols):
                total = parts[0][order[n]].astype(F32)
                for part in parts[1:]:
                    total = total + part[order[n]].astype(F32)
                refs[n // half][n % half, :, at : at + size] = total.astype(LOW)
                at += size

    arrays = [part for parts in sides for part in parts]
    keep, send = run("halve", kernel, [(place, pltpu.SMEM)] + vmem(*arrays), [(shape, LOW), (shape, LOW)])
    pairs = [(i, mirrored(i, count)) for i in range(grid_sizes()["z"])]
    return keep, lax.ppermute(send, "narrow", pairs)


def by_blocks(parts):
    count = grid_sizes()["z"]
    return [part.reshape(count, part.shape[0] // count, part.shape[1]) for part in parts]


def total_of(parts):
    return sum(part.astype(F32) for part in parts)


def scatter_along(parts, dim):
    count, here = grid_sizes()[dim], grid_place()[dim]
    kept = [lax.dynamic_index_in_dim(part, here, 0, keepdims=False) for part in parts]
    for step in range(1, count):
        there = (here + step) % count
        part = total_of([lax.dynamic_index_in_dim(part, there, 0, keepdims=False) for part in parts])
        kept.append(shifted(part.astype(LOW), dim, step))
    return kept


def sent(parts, dim):
    return [parts[0]] + [shifted(part, dim, step) for step, part in enumerate(parts) if step]


def segment_ids(length_row, slot_count):
    ends = jnp.cumsum(length_row).astype(jnp.int32)
    places = jnp.arange(slot_count, dtype=jnp.int32)
    return jnp.sum((places[:, None] >= ends[None, :]).astype(jnp.int32), axis=1).astype(jnp.int32)


def local(
    tokens, memory, doc_lengths, mem_lengths, pad_mask,
    self_query, self_key, self_value, self_output, self_gain, bias_table,
    cross_query, cross_key, cross_value, cross_output, cross_gain,
    hidden_in, hidden_out, hidden_gain, out_grad,
):
    sizes = grid_sizes()
    here = grid_place()
    ny, nx, nz = sizes["y"], sizes["x"], sizes["z"]
    rows, width = tokens.shape
    mem_rows = memory.shape[0]
    ff = hidden_in.shape[1]
    share = self_query.shape[0]
    ff_share = hidden_out.shape[0]
    table_rows, heads = bias_table.shape
    block = nz * share
    ff_block = nz * ff_share
    cut = 2 * width + LANES

    spots = []
    for step in range(4):
        y = (here["y"] + step // 2) % ny
        x = (here["x"] + step % 2) % nx
        for core in range(2):
            spots.append((y * nx + x) * 2 + (here["c"] + core) % 2)
    for n in range(4):
        spots += [2 * n + here["c"], 2 * n + 1 - here["c"]]
    place = jnp.stack([here["y"], here["x"], here["c"], here["z"]] + spots).astype(jnp.int32)
    pieces = in_pieces(block)
    half = block // 2

    hot = jnp.asarray(table_hot(rows, nz, share, table_rows)).astype(LOW)
    groups = hot.shape[0]
    table = jnp.pad(bias_table, ((0, groups * share - table_rows), (0, 0)))
    table = jnp.transpose(table.reshape(groups, share, heads), (1, 0, 2)).reshape(share, groups * heads)
    extra = jnp.concatenate(
        [
            self_gain[:, None],
            cross_gain[:, None],
            hidden_gain[:, None],
            jnp.zeros((share, TABLE_LANE - 3), LOW),
            table,
            jnp.zeros((share, LANES - TABLE_LANE - groups * heads), LOW),
        ],
        axis=1,
    )
    self_own = jnp.concatenate([self_query, self_key, extra, self_value, self_output], axis=1)
    self_others = received(self_own, "z")
    self_z = in_order(self_own, self_others, "z", 0).reshape(block, -1)
    folds = ff // width
    order = hidden_order(nz, share, folds)
    wide_out = jnp.transpose(hidden_out.reshape(folds, share, width), (1, 0, 2)).reshape(share, ff)
    hidden_own = reorder(hidden_in, order, NN, LOW)
    early_cols = int(ff * EARLY) // LANES * LANES if pieces else 0
    rest = jnp.concatenate(
        [cross_query, cross_output, cross_key, cross_value, hidden_own[:, early_cols:], wide_out], axis=1
    )
    rest = lax.all_gather(after(rest, self_others[0]), "narrow", axis=0, tiled=True)

    seg_ids = segment_ids(doc_lengths[0], rows)
    mem_ids = segment_ids(mem_lengths[0], mem_rows)
    if pieces:
        in_own = hidden_own[:, :early_cols]
        in_x, in_y = shifted(in_own, "x", 1), shifted(in_own, "y", 1)
        in_xy = shifted(in_x, "y", 1)
        in_all = in_order(
            in_order(in_own, [in_x], "x", 0), [in_order(in_y, [in_xy], "x", 0)], "y", 0
        ).reshape(4, share, early_cols)
        near, twins, corner = gather_pieces(self_z)
        in_all = lax.all_gather(after(in_all, rest, *corner), "narrow", axis=0, tiled=False)
        w_self = Weights(
            pairs(near, twins) + with_twins(corner),
            near_spots(range(6), block, 0, 0, 0, cut + 2 * width)
            + half_spots(range(6, 10), block, 0, 0, 0, cut + 2 * width),
        )
        rest_near = from_neighbours(after(rest, *twins, *corner))
    else:
        w_self = Weights([gather_whole(self_z)], [(0, 0, 0, None, 0, 0, width, 0, 0, cut + 2 * width)])

    og_far = swapped(out_grad)
    qk, v, self_probs, after_self, s_keep, s_send, gains = self_forward(
        place, after(tokens, og_far), seg_ids[:, None], seg_ids[None], pad_mask[None], hot, w_self, cut, block
    )
    s_far = swapped(s_send)
    if pieces:
        twin = swapped(rest_near[0])
        rest_x, rest_y = (after(array, after_self, s_far, twin) for array in rest_near[1:])
        corner = from_corner(rest_x[:half, :ff], rest_y[half:, :ff])
        upper, lower = rest_x[:half, ff:], rest_y[half:, ff:]
        rest_arrays = [rest_near[0], twin] + with_twins([rest_x, rest_y])
        w_cross = Weights(
            rest_arrays + with_twins(corner),
            near_spots(range(6), block, 0, 0, 0, ff) + half_spots(range(6, 10), block, 0, 0, 0, ff),
        )
        last = from_corner(upper, lower)
        cross_in = after(after_self, s_far, upper, lower)
    else:
        rest = gather_whole(rest)
        w_cross = Weights([rest], [(0, 0, 0, None, 0, 0, width, 0, 0, ff)])
        m_in = rest[:, ff : 2 * ff]
        m_out = jnp.transpose(rest[:, 2 * ff :].reshape(-1, block, folds, width), (0, 2, 1, 3)).reshape(ff, width)
        cross_in = after_self
    q, kv, cross_probs, after_cross, c_keep, c_send = cross_forward(
        place, cross_in, memory, gains, seg_ids[:, None], mem_ids[None], w_cross, block
    )
    c_far = swapped(c_send)
    if pieces:
        late_cols = ff - early_cols
        spots = folded_spots(near_spots(range(6), block, 0, 1, 0, 0), block, ff + late_cols, folds, width, 1)
        if late_cols:
            spots += near_spots(range(6), block, ff, 0, early_cols, late_cols)
        early = list(rest_arrays)
        in_all = jnp.transpose(after(in_all, *corner), (1, 0, 2, 3)).reshape(4 * block, early_cols)
        for twin, array in enumerate((in_all, swapped(in_all))):
            spots += [
                (6 + twin, n * block, 0, ORDER_AT + 2 * n + twin, block, 0, block, 0, 0, early_cols) for n in range(4)
            ]
            early.append(array)
        m_in, m_out = hidden_early(after(place, after_cross, c_far), Weights(early, spots), width, ff)
        last = with_twins([after(array, after_cross) for array in last])
        spots = folded_spots(half_spots(range(4), block, 0, 1, 0, 0), block, late_cols, folds, width, 1)
        if late_cols:
            spots += half_spots(range(4), block, 0, 0, early_cols, late_cols)
        w_last = Weights(last, spots)
    else:
        w_last = Weights([], [])

    act, gu, h_keep, h_send, m_in, m_out = hidden_first(
        place, after(after_cross, c_far), out_grad, gains, m_in, m_out, w_last, block
    )
    h_far, gu_far = swapped(h_send), swapped(gu)
    layer_out, grad, branch, hidden_gain_part = hidden_second(after_cross, out_grad, gains, act, gu, m_in, m_out)
    h_keep = after(h_keep, grad)
    side = width // 2
    early_grads = int(ff * EARLY_GRAD) // LANES * LANES if pieces else 0
    late = (ff - early_grads) // 2
    if pieces:
        in_early = weight_grads(
            place,
            [(h_keep[None], h_far[None])],
            [(gu, gu_far), (out_grad, og_far)],
            [],
            (0, 0),
            straight=[
                ((0, 0, 0, block), 0, 0, early_grads, 2, 0),
                ((0, 0, block, ff_block), 1, 0, width, 2, early_grads),
            ],
        )[0]
        grad = after(grad, in_early)
        in_early = lax.psum_scatter(in_early, "narrow", scatter_dimension=0, tiled=True)
        out_sections = []
    else:
        out_sections = [
            ((2, 0, block, ff_block), 3, 0, side, 0, 2 * width + side + late),
            ((2, 0, block, ff_block), 3, side, side, 1, 2 * width + side + late),
        ]
    cross_cols = 2 * width + side + late + (folds * side if out_sections else 0)

    branch_far = swapped(branch)
    cross_grads, memory_grad, grad, cross_gain_part = cross_backward(
        place, grad, after(branch, branch_far), after_self, gains, q, kv, cross_probs, w_cross
    )
    cross_parts = weight_grads(
        place,
        [(c_keep, c_far), (s_keep, s_far), (h_keep[None], h_far[None])],
        [(cross_grads, swapped(cross_grads)), (branch, branch_far), (gu, gu_far), (out_grad, og_far)],
        [
            ((0, 0, 0, block), 0, 0, width, 0, 0),
            ((0, 1, 0, block), 1, 0, width, 0, width),
            ((1, 1, 0, block), 0, 3 * width, side, 0, 2 * width),
            ((2, 0, 0, block), 2, early_grads, late, 0, 2 * width + side),
            ((0, 2, 0, block), 0, width, 2 * width, 1, 0),
            ((1, 1, 0, block), 0, 3 * width + side, side, 1, 2 * width),
            ((2, 0, 0, block), 2, early_grads + late, late, 1, 2 * width + side),
            *out_sections,
        ],
        (cross_cols, cross_cols),
    )
    cross_first, cross_second = cross_parts[:ny], cross_parts[ny:]
    cross_first, cross_second = sent(cross_first, "y"), sent(cross_second, "x")

    grad = after(grad, *cross_parts)
    self_grads, self_dv, tokens_grad, extra_keep, extra_send = self_backward(
        place, grad, cross_grads, tokens, gains, cross_gain_part, hidden_gain_part, qk, v,
        self_probs, hot, w_self, cut, block,
    )
    self_parts = weight_grads(
        place,
        [(s_keep, s_far)],
        [(self_grads, swapped(self_grads)), (self_dv, swapped(self_dv))],
        [
            ((0, 0, 0, block), 0, 0, width, 0, 0),
            ((0, 0, 0, block), 0, width, side, 0, width),
            ((0, 0, 0, block), 0, width + side, side, 1, 0),
            ((0, 0, 0, block), 1, 0, width, 1, side),
        ],
        (width + side + LANES, width + side),
        (extra_keep, swapped(extra_send)),
    )
    self_first, self_second = self_parts[:ny], self_parts[ny:]
    self_first, self_second = sent(self_first, "y"), sent(self_second, "x")
    cross_first = [after(cross_first[0], *self_parts)] + cross_first[1:]
    cross_parts = add_stage(place, cross_first, cross_second)
    cross_first, cross_second = cross_parts[:nx], cross_parts[nx:]
    cross_first, cross_second = sent(cross_first, "x"), sent(cross_second, "y")
    cross_parts = halve(place, [by_blocks(cross_first), by_blocks(cross_second)], 2, True)
    self_first = [after(self_first[0], cross_parts[0])] + self_first[1:]
    self_parts = add_stage(place, self_first, self_second)
    self_first, self_second = self_parts[:nx], self_parts[nx:]
    self_first, self_second = sent(self_first, "x"), sent(self_second, "y")
    if pieces:
        in_early = after(in_early, *self_parts).reshape(ny, nx, share, early_grads + folds * width)
        in_early = scatter_along([in_early], "y")
    count = 2
    while count < nz:
        count *= 2
        earlier = (*self_parts, *in_early) if pieces else self_parts
        cross_parts = halve(place, [[after(part, *earlier) for part in cross_parts]], count, False)
    self_first = [after(self_first[0], cross_parts[0])] + self_first[1:]
    self_sums = add_last(place, (self_first, self_second))
    if pieces:
        in_early = total_of(scatter_along([after(part, cross_parts[0]) for part in in_early], "x"))
    cross_total = total_of([part[0] for part in cross_parts])
    self_total = total_of(sent(self_sums, "z"))

    at = 2 * width + side
    in_parts = [cross_total[:, n + at : n + at + late] for n in (0, cross_cols)]
    if pieces:
        in_parts = [in_early[:, :early_grads]] + in_parts
        out_part = in_early[:, early_grads:].reshape(share, folds, width)
    else:
        out_part = jnp.concatenate(
            [cross_total[:, n + at + late : n + cross_cols].reshape(share, folds, side) for n in (0, cross_cols)],
            axis=2,
        )
    in_grad = reorder(jnp.concatenate([part.astype(LOW) for part in in_parts], axis=1), order, NT, F32)
    out_part = jnp.transpose(out_part, (1, 0, 2)).reshape(ff_share, width)
    first_cols = width + side + LANES
    last = self_total[:, width + side : first_cols]
    table_grad = last[:, TABLE_LANE : TABLE_LANE + groups * heads].reshape(share, groups, heads)
    table_grad = jnp.transpose(table_grad, (1, 0, 2)).reshape(groups * share, heads)[:table_rows]
    key_grad = jnp.concatenate(
        [self_total[:, width : width + side], self_total[:, first_cols : first_cols + side]], axis=1
    )
    output_grad = jnp.concatenate(
        [cross_total[:, n + 2 * width : n + 2 * width + side] for n in (0, cross_cols)], axis=1
    )
    return (
        layer_out,
        tokens_grad,
        memory_grad,
        self_total[:, :width],
        key_grad,
        self_total[:, first_cols + side :],
        output_grad,
        last[:, 0],
        table_grad,
        cross_total[:, :width],
        cross_total[:, cross_cols : cross_cols + width],
        cross_total[:, cross_cols + width : cross_cols + 2 * width],
        cross_total[:, width : 2 * width],
        last[:, 1],
        in_grad,
        out_part.astype(F32),
        last[:, 2],
    )


def solution(mesh):
    rows = P(("wide", "narrow"), None)
    line = P(("wide", "narrow"))
    table = P("narrow", None)
    return jax.shard_map(
        local,
        mesh=mesh,
        in_specs=(
            (rows,) * 4 + (line,) + (rows,) * 4 + (line, table) + (rows,) * 4 + (line,) + (rows,) * 2 + (line, rows)
        ),
        out_specs=(rows,) * 7 + (line, table) + (rows,) * 4 + (line,) + (rows,) * 2 + (line,),
        check_vma=False,
    )
```

time: 331 us -> 282 us (0.85)
  waiting for transfers between devices: 147 us -> 107 us
  local copies, waits for them, and re-layouts: 47 us -> 32.4 us
  Pallas kernels: 67.9 us -> 81.1 us
  starting transfers between devices: 49.1 us -> 40.2 us
    ppermute x52 -> x46, waiting for transfers between devices: 117 us -> 87.6 us  [shifted(): return lax.ppermute(array, 'wide', pairs)]
    pallas_call x16 -> x17, Pallas kernels: 67.9 us -> 81.1 us  [run(): pl.pallas_call(kernel, name=name, in_specs=[pl.BlockSpec(memory_space=spa...]
    ppermute x9 -> x6, starting transfers between devices: 17.4 us -> 9.01 us  [shifted(): lax.ppermute(array, 'narrow', [(i, (i + step) % count) for i in range(cou...]
    unnamed x104 -> x122, local copies, waits for them, and re-layouts: 25 us -> 16.9 us
    ppermute x9 -> x6, waiting for transfers between devices: 25 us -> 18.6 us  [shifted(): lax.ppermute(array, 'narrow', [(i, (i + step) % count) for i in range(cou...]
    all_gather x1 -> x2, waiting for transfers between devices: 4.98 us -> 1.19 us  [the longest x1 1.19 us: local(): lax.all_gather(after(rest, self_others[0]), 'narrow', axis=0, tiled=True)]
    slice x9 -> x12, local copies, waits for them, and re-layouts: 7.38 us -> 4.1 us  [the longest x2 2.02 us: local(): upper, lower = (rest_x[:half, ff:], rest_y[half:, ff:])]
    ppermute x52 -> x46, starting transfers between devices: 31.7 us -> 29.4 us  [shifted(): return lax.ppermute(array, 'wide', pairs)]
  transfers between devices with their start and end apart: 63 -> 57, of which waited for: 26 -> 31; matrix products, arithmetic and copies ran while one was open for 7% -> 7% of each run, Pallas kernels for 13% -> 24%
where the time goes in v1:
time: 282 us; the launch traced here: 281 us
  waiting for transfers between devices  107 us (38%)
  Pallas kernels  81.1 us (29%)
  starting transfers between devices  40.2 us (14%)
  local copies, waits for them, and re-layouts  32.4 us (11%)
  between operations  14.7 us (5%)
  other arithmetic  5.17 us (2%)
    ppermute x46, waiting for transfers between devices, shifted(): return lax.ppermute(array, 'wide', pairs)  87.6 us
    pallas_call x17, Pallas kernels, run(): pl.pallas_call(kernel, name=name, in_specs=[pl.BlockSpec(memory_space=spa...  81.1 us
    ppermute x46, starting transfers between devices, shifted(): return lax.ppermute(array, 'wide', pairs)  29.4 us
    ppermute x6, waiting for transfers between devices, shifted(): lax.ppermute(array, 'narrow', [(i, (i + step) % count) for i in range(cou...  18.6 us
    unnamed x122, local copies, waits for them, and re-layouts  16.9 us
    ppermute x6, starting transfers between devices, shifted(): lax.ppermute(array, 'narrow', [(i, (i + step) % count) for i in range(cou...  9.01 us
  transfers between devices with their start and end apart: 57, of which 31 were waited for; matrix products, arithmetic and copies ran while one was open for 7% of the time, Pallas kernels for 24%

profile of v1, /device:TPU:0, one launch (start us, length us, event | category | flops | bytes accessed | tf_op | source)
XLA Modules:
  0.0 280.9 jit_solution(16514071085216511442)
XLA Ops:
  9.6 3.0 %collective-permute-start.26 = (bf16[24,2304]{1,0:T(8,128)(2,1)S(1)}, bf16[24,2304]{1,0:T(8,128)(2,1)S(1)}, u32[]{:S(2)}, u32[]{:S(2)}) collective-permute-start(bf16[24,2304]{1,0:T(8,128)(2,1)S(1)} %slice.115), channel_id=1, source_target_pairs={{0,16},{4,20},{8,24},{12,28},{16,0},{20,4},{24,8},{28,12},{1,17},{... | collective-permute-start | bytes 331784 | tf_op jit(solution)/shard_map/ppermute | solution.py:95
  18.0 3.6 %collective-permute-start.3 = (bf16[24,3200]{1,0:T(8,128)(2,1)S(1)}, bf16[24,3200]{1,0:T(8,128)(2,1)S(1)}, u32[]{:S(2)}, u32[]{:S(2)}) collective-permute-start(bf16[24,3200]{1,0:T(8,128)(2,1)S(1)} %concatenate.43), channel_id=1, source_target_pairs={{0,3},{1,0},{2,1},{3,2},{4,7},{5,4},{6,5},{7,6},{8,11},{9,8},{10,9... | collective-permute-start | bytes 460808 | tf_op jit(solution)/shard_map/ppermute | solution.py:89
  26.1 8.0 %collective-permute-done.2 = bf16[24,3200]{1,0:T(8,128)(2,1)S(1)} collective-permute-done((bf16[24,3200]{1,0:T(8,128)(2,1)S(1)}, bf16[24,3200]{1,0:T(8,128)(2,1)S(1)}, u32[]{:S(2)}, u32[]{:S(2)}) %collective-permute-start.2) | collective-permute-done | bytes 153632 | tf_op jit(solution)/shard_map/ppermute | solution.py:89
  35.6 14.1 %collective-permute-done.7.refs_4_ = bf16[96,3200]{1,0:T(8,128)(2,1)S(1)} collective-permute-done((bf16[96,3200]{1,0:T(8,128)(2,1)S(1)}, bf16[96,3200]{1,0:T(8,128)(2,1)S(1)}, u32[]{:S(2)}, u32[]{:S(2)}) %collective-permute-start.7) | collective-permute-done | bytes 614432 | tf_op jit(solution)/shard_map/ppermute | solution.py:95
  52.9 4.8 %collective-permute-done.11.refs_8_ = bf16[48,3200]{1,0:T(8,128)(2,1)S(1)} collective-permute-done((bf16[48,3200]{1,0:T(8,128)(2,1)S(1)}, bf16[48,3200]{1,0:T(8,128)(2,1)S(1)}, u32[]{:S(2)}, u32[]{:S(2)}) %collective-permute-start.11) | collective-permute-done | bytes 307232 | tf_op jit(solution)/shard_map/ppermute | solution.py:95
  70.6 10.4 %self_forward.1 = (bf16[256,1536]{1,0:T(8,128)(2,1)S(1)}, bf16[256,768]{1,0:T(8,128)(2,1)S(1)}, bf16[12,256,256]{2,1,0:T(8,128)(2,1)S(1)}, f32[256,768]{1,0:T(8,...) custom-call(s32[20]{0:T(128)S(1)} %stack.118.place, ...), custom_call_target="tpu_custom_call" | custom-call | flops 1207959552 | bytes 2680360 | tf_op jit(solution)/shard_map/self_forward/pallas_call | solution.py:233
  87.1 6.7 %collective-permute-done.16.refs_4_.refs_10_ = bf16[96,6912]{1,0:T(8,128)(2,1)} collective-permute-done((bf16[96,6912]{1,0:T(8,128)(2,1)}, bf16[96,6912]{1,0:T(8,128)(2,1)}, u32[]{:S(2)}, u32[]{:S(2)}) %collective-permute-start.16) | collective-permute-done | bytes 1327136 | tf_op jit(solution)/shard_map/ppermute | solution.py:95
  100.2 6.2 %collective-permute-done.21.refs_8_.refs_14_ = bf16[48,3072]{1,0:T(8,128)(2,1)} collective-permute-done((bf16[48,3072]{1,0:T(8,128)(2,1)S(1)}, bf16[48,3072]{1,0:T(8,128)(2,1)}, u32[]{:S(2)}, u32[]{:S(2)}) %collective-permute-start.21) | collective-permute-done | bytes 294944 | tf_op jit(solution)/shard_map/ppermute | solution.py:95
  107.6 2.8 %copy.68 = bf16[4,4,24,2304]{3,2,1,0:T(8,128)(2,1)} copy(bf16[4,4,24,2304]{3,2,0,1:T(8,128)(2,1)} %bitcast.101) | data formatting | bytes 3538944 | tf_op jit(solution)/shard_map/transpose | solution.py:1022
  117.0 10.2 %cross_forward.1 = (bf16[256,768]{1,0:T(8,128)(2,1)S(1)}, bf16[256,1536]{1,0:T(8,128)(2,1)S(1)}, bf16[12,256,256]{2,1,0:T(8,128)(2,1)S(1)}, f32[256,768]{1,0:T(8...) custom-call(s32[20]{0:T(128)S(1)} %stack.118.place, ...), custom_call_target="tpu_custom_call" | custom-call | flops 1207959552 | bytes 5174312 | tf_op jit(solution)/shard_map/cross_forward/pallas_call | solution.py:233
  132.9 4.3 %hidden_early.1 = (bf16[768,3072]{1,0:T(8,128)(2,1)S(1)}, bf16[3072,768]{1,0:T(8,128)(2,1)S(1)}) custom-call(s32[20]{0:T(128)S(1)} %stack.118.place, bf16[96,6912]{1,0:T(8,128)(2,1)} %all-gather.4.cloned.1.call-done.refs_0_.refs_6_, bf16[96,6912]{1,0:T(8,128)(2,1)} %collective-permute-done.15.refs_1_.refs_7_, ...), custom_call_target="tpu_custom_call" | custom-call | bytes 5750824 | tf_op jit(solution)/shard_map/hidden_early/pallas_call | solution.py:233
  138.2 7.7 %hidden_first.1 = (bf16[256,3072]{1,0:T(8,128)(2,1)S(1)}, bf16[256,3072]{1,0:T(8,128)(2,1)S(1)}, bf16[4,480,256]{2,1,0:T(8,128)(2,1)S(1)}, bf16[4,480,256]{2,1,0...) custom-call(s32[20]{0:T(128)S(1)} %stack.118.place, ...), custom_call_target="tpu_custom_call", output_to_operand_aliasing={{4}: (4, {}), {5}: (5, {})} | custom-call | flops 2415919104 | bytes 6058024 | tf_op jit(solution)/shard_map/hidden_first/pallas_call | solution.py:233
  147.2 3.5 %hidden_second.1 = (bf16[256,768]{1,0:T(8,128)(2,1)}, f32[256,768]{1,0:T(8,128)S(1)}, bf16[256,768]{1,0:T(8,128)(2,1)S(1)}, f32[1,768]{1,0:T(1,128)S(1)}) custom-call(f32[256,768]{1,0:T(8,128)S(1)} %get-tuple-element.114.x, bf16[256,768]{1,0:T(8,128)(2,1)S(1)} %copy-done, f32[8,768]{1,0:T(8,128)S(1)} %copy-done.21, ...), custom_call_target="tpu_custom_call" | custom-call | flops 2415919104 | bytes 6893568 | tf_op jit(solution)/shard_map/hidden_second/pallas_call | solution.py:233
  152.3 4.3 %weight_grads.3 = bf16[4,4,24,4608]{3,2,1,0:T(8,128)(2,1)} custom-call(s32[20]{0:T(128)S(1)} %stack.118.place, bf16[1,4,480,256]{3,2,1,0:T(8,128)(2,1)S(1)} %bitcast.80, bf16[1,4,480,256]{3,2,1,0:T(8,128)(2,1)S(1)} %bitcast.82, bf16[256,3072]{1,0:T(8,128)(2,1)S(1)} %get-tuple-element.123.gu.refs_2_.refs_10_, ...), custom_call_target="tpu_custom_call" | custom-call | flops 1811939328 | bytes 2949160 | tf_op jit(solution)/shard_map/weight_grads/pallas_call | solution.py:233
  160.5 13.5 %cross_backward.1 = (bf16[256,3072]{1,0:T(8,128)(2,1)S(1)}, f32[256,768]{1,0:T(8,128)}, f32[256,768]{1,0:T(8,128)S(1)}, f32[1,768]{1,0:T(1,128)S(1)}) custom-call(s32[20]{0:T(128)S(1)} %stack.118.place, f32[8,768]{1,0:T(8,128)S(1)} %copy-done.22, bf16[256,768]{1,0:T(8,128)(2,1)} %copy-done.9, bf16[256,1536]{1,0:T(8,128)(2,1)} %copy-done.18, ...), custom_call_target="tpu_custom_call" | custom-call | flops 1207959552 | bytes 6942760 | tf_op jit(solution)/shard_map/cross_backward/pallas_call | solution.py:233
  174.2 3.3 %collective-permute-done.35.refs_7_ = bf16[256,3072]{1,0:T(8,128)(2,1)S(1)} collective-permute-done((bf16[256,3072]{1,0:T(8,128)(2,1)S(1)}, bf16[256,3072]{1,0:T(8,128)(2,1)S(1)}, u32[]{:S(2)}, u32[]{:S(2)}) %collective-permute-start.35) | collective-permute-done | bytes 1572896 | tf_op jit(solution)/shard_map/ppermute | solution.py:95
  177.5 3.0 %weight_grads.4 = (bf16[2,96,2688]{2,1,0:T(8,128)(2,1)S(1)}, bf16[2,96,2688]{2,1,0:T(8,128)(2,1)S(1)}, bf16[2,96,2688]{2,1,0:T(8,128)(2,1)S(1)}, bf16[2,96,2688]{2,1,0:T(8,128)(2,1)S(1)}) custom-call(s32[20]{0:T(128)S(1)} %stack.118.place, bf16[3,4,96,256]{3,2,1,0:T(8,128)(2,1)S(1)} %copy-done.25, bf16[3,4,96,256]{3,2,1,0:T(8,128)(2,1)S(1)} %copy-done.27, ...), custom_call_target="tpu_custom_call" | custom-call | flops 2113929216 | bytes 5898280 | tf_op jit(solution)/shard_map/weight_grads/pallas_call | solution.py:233
  183.8 12.9 %self_backward.1 = (bf16[256,1536]{1,0:T(8,128)(2,1)S(1)}, bf16[256,768]{1,0:T(8,128)(2,1)S(1)}, f32[256,768]{1,0:T(8,128)}, bf16[4,96,128]{2,1,0:T(8,128)(2,1)S(1)}, bf16[4,96,128]{2,1,0:T(8,128)(2,1)S(1)}) custom-call(s32[20]{0:T(128)S(1)} %stack.118.place, f32[256,768]{1,0:T(8,128)S(1)} %get-tuple-element.145.grad, ...), custom_call_target="tpu_custom_call" | custom-call | flops 1207959552 | bytes 5250088 | tf_op jit(solution)/shard_map/self_backward/pallas_call | solution.py:233
  202.4 3.0 %collective-permute-done.39.refs_1_ = bf16[2,96,2688]{2,1,0:T(8,128)(2,1)S(1)} collective-permute-done((bf16[2,96,2688]{2,1,0:T(8,128)(2,1)S(1)}, bf16[2,96,2688]{2,1,0:T(8,128)(2,1)S(1)}, u32[]{:S(2)}, u32[]{:S(2)}) %collective-permute-start.39) | collective-permute-done | bytes 1032224 | tf_op jit(solution)/shard_map/ppermute | solution.py:95
  212.7 10.8 %collective-permute-done.41 = bf16[96,2688]{1,0:T(8,128)(2,1)S(1)} collective-permute-done((bf16[96,2688]{1,0:T(8,128)(2,1)}, bf16[96,2688]{1,0:T(8,128)(2,1)S(1)}, u32[]{:S(2)}, u32[]{:S(2)}) %collective-permute-start.41) | collective-permute-done | bytes 516128 | tf_op jit(solution)/shard_map/ppermute | solution.py:95
  227.1 4.1 %collective-permute-done.44.refs_3_ = bf16[2,96,1152]{2,1,0:T(8,128)(2,1)} collective-permute-done((bf16[2,96,1152]{2,1,0:T(8,128)(2,1)}, bf16[2,96,1152]{2,1,0:T(8,128)(2,1)}, u32[]{:S(2)}, u32[]{:S(2)}) %collective-permute-start.44) | collective-permute-done | bytes 442400 | tf_op jit(solution)/shard_map/ppermute | solution.py:95
  239.1 9.9 %collective-permute-done.45 = bf16[2,24,4608]{2,1,0:T(8,128)(2,1)} collective-permute-done((bf16[2,24,4608]{2,1,0:T(8,128)(2,1)S(1)}, bf16[2,24,4608]{2,1,0:T(8,128)(2,1)}, u32[]{:S(2)}, u32[]{:S(2)}) %collective-permute-start.45) | collective-permute-done | bytes 442400 | tf_op jit(solution)/shard_map/ppermute | solution.py:95
  253.4 2.8 %collective-permute-start.51 = (bf16[24,2432]{1,0:T(8,128)(2,1)S(1)}, bf16[24,2432]{1,0:T(8,128)(2,1)S(1)}, u32[]{:S(2)}, u32[]{:S(2)}) collective-permute-start(bf16[24,2432]{1,0:T(8,128)(2,1)S(1)} %get-tuple-element.181), channel_id=1, source_target_pairs={{0,3},{1,0},{2,1},{3,2},{4,7},{5,4},{6,5},{7,6},{8,11},{9,8},{10,9... | collective-permute-start | bytes 350216 | tf_op jit(solution)/shard_map/ppermute | solution.py:89
  259.2 8.6 %collective-permute-done.50 = bf16[24,2432]{1,0:T(8,128)(2,1)S(1)} collective-permute-done((bf16[24,2432]{1,0:T(8,128)(2,1)S(1)}, bf16[24,2432]{1,0:T(8,128)(2,1)S(1)}, u32[]{:S(2)}, u32[]{:S(2)}) %collective-permute-start.50) | collective-permute-done | bytes 116768 | tf_op jit(solution)/shard_map/ppermute | solution.py:89
  (278 shorter events, 104.5 us)
Async XLA Ops:
  7.2 52.1 %all-gather.4.cloned.1.call-start = ((), (), s32[]{:S(2)}) async-start(), calls=%async_computation.1 | async-start | bytes 1658880 | tf_op jit(solution)/shard_map/all_gather | solution.py:967
  9.6 25.8 %collective-permute-start.26 = (bf16[24,2304]{1,0:T(8,128)(2,1)S(1)}, bf16[24,2304]{1,0:T(8,128)(2,1)S(1)}, u32[]{:S(2)}, u32[]{:S(2)}) collective-permute-start(bf16[24,2304]{1,0:T(8,128)(2,1)S(1)} %slice.115), channel_id=1, source_target_pairs={{0,16},{4,20},{8,24},{12,28},{16,0},{20,4},{24,8},{28,12},{1,17},{... | collective-permute-start | bytes 331784 | tf_op jit(solution)/shard_map/ppermute | solution.py:95
  26.1 81.5 %all-gather.6.cloned.1.call-start = ((), (), s32[]{:S(2)}) async-start(), calls=%async_computation.3 | async-start | bytes 2211840 | tf_op jit(solution)/shard_map/all_gather | solution.py:979
  34.3 15.4 %collective-permute-start.7 = (bf16[96,3200]{1,0:T(8,128)(2,1)S(1)}, bf16[96,3200]{1,0:T(8,128)(2,1)S(1)}, u32[]{:S(2)}, u32[]{:S(2)}) collective-permute-start(bf16[96,3200]{1,0:T(8,128)(2,1)S(1)} %bitcast.96), channel_id=1, source_target_pairs={{0,16},{4,20},{8,24},{12,28},{16,0},{20,4},{24,8},{28,12},{1,17},{... | collective-permute-start | bytes 1843208 | tf_op jit(solution)/shard_map/ppermute | solution.py:95
  34.9 15.0 %collective-permute-start.5 = (bf16[96,3200]{1,0:T(8,128)(2,1)S(1)}, bf16[96,3200]{1,0:T(8,128)(2,1)S(1)}, u32[]{:S(2)}, u32[]{:S(2)}) collective-permute-start(bf16[96,3200]{1,0:T(8,128)(2,1)S(1)} %bitcast.97), channel_id=1, source_target_pairs={{0,8},{4,12},{8,0},{12,4},{16,24},{20,28},{24,16},{28,20},{1,9},{5... | collective-permute-start | bytes 1843208 | tf_op jit(solution)/shard_map/ppermute | solution.py:95
  35.4 14.3 %collective-permute-start.4 = (bf16[96,3200]{1,0:T(8,128)(2,1)S(1)}, bf16[96,3200]{1,0:T(8,128)(2,1)S(1)}, u32[]{:S(2)}, u32[]{:S(2)}) collective-permute-start(bf16[96,3200]{1,0:T(8,128)(2,1)S(1)} %bitcast.98), channel_id=1, source_target_pairs={{0,4},{4,0},{8,12},{12,8},{16,20},{20,16},{24,28},{28,24},{1,5},{5... | collective-permute-start | bytes 1843208 | tf_op jit(solution)/shard_map/ppermute | solution.py:95
  59.3 176.0 %reduce-scatter.2.cloned.1.call-start = ((), (), s32[]{:S(2)}) async-start(), calls=%async_computation.2 | async-start | bytes 4423680 | tf_op jit(solution)/shard_map/reduce_scatter | solution.py:1059
  62.3 31.5 %collective-permute-start.16 = (bf16[96,6912]{1,0:T(8,128)(2,1)}, bf16[96,6912]{1,0:T(8,128)(2,1)}, u32[]{:S(2)}, u32[]{:S(2)}) collective-permute-start(bf16[96,6912]{1,0:T(8,128)(2,1)} %all-gather.4.cloned.1.call-done.refs_0_.refs_6_), channel_id=1, source_target_pairs={{0,16},{4,20},{8,24},{12,28},{16,0},{20,4},{24,8},{28,12},{1,17},{... | collective-permute-start | bytes 3981320 | tf_op jit(solution)/shard_map/ppermute | solution.py:95
  63.8 30.0 %collective-permute-start.15 = (bf16[96,6912]{1,0:T(8,128)(2,1)}, bf16[96,6912]{1,0:T(8,128)(2,1)}, u32[]{:S(2)}, u32[]{:S(2)}) collective-permute-start(bf16[96,6912]{1,0:T(8,128)(2,1)} %all-gather.4.cloned.1.call-done.refs_0_.refs_6_), channel_id=1, source_target_pairs={{0,4},{4,0},{8,12},{12,8},{16,20},{20,16},{24,28},{28,24},{1,5},{5... | collective-permute-start | bytes 3981320 | tf_op jit(solution)/shard_map/ppermute | solution.py:95
  63.8 31.9 %collective-permute-start.14 = (bf16[96,6912]{1,0:T(8,128)(2,1)}, bf16[96,6912]{1,0:T(8,128)(2,1)}, u32[]{:S(2)}, u32[]{:S(2)}) collective-permute-start(bf16[96,6912]{1,0:T(8,128)(2,1)} %all-gather.4.cloned.1.call-done.refs_0_.refs_6_), channel_id=1, source_target_pairs={{0,8},{4,12},{8,0},{12,4},{16,24},{20,28},{24,16},{28,20},{1,9},{5... | collective-permute-start | bytes 3981320 | tf_op jit(solution)/shard_map/ppermute | solution.py:95
  99.7 16.1 %collective-permute-start.17 = (bf16[96,6912]{1,0:T(8,128)(2,1)}, bf16[96,6912]{1,0:T(8,128)(2,1)S(1)}, u32[]{:S(2)}, u32[]{:S(2)}) collective-permute-start(bf16[96,6912]{1,0:T(8,128)(2,1)} %collective-permute-done.14.refs_2_.refs_8_), channel_id=1, source_target_pairs={{0,4},{4,0},{8,12},{12,8},{16,20},{20,16},{24,28},{28,24},{1,5},{5... | collective-permute-start | bytes 3981320 | tf_op jit(solution)/shard_map/ppermute | solution.py:95
  99.7 16.1 %collective-permute-start.18 = (bf16[96,6912]{1,0:T(8,128)(2,1)}, bf16[96,6912]{1,0:T(8,128)(2,1)}, u32[]{:S(2)}, u32[]{:S(2)}) collective-permute-start(bf16[96,6912]{1,0:T(8,128)(2,1)} %collective-permute-done.16.refs_4_.refs_10_), channel_id=1, source_target_pairs={{0,4},{4,0},{8,12},{12,8},{16,20},{20,16},{24,28},{28,24},{1,5},{5... | collective-permute-start | bytes 3981320 | tf_op jit(solution)/shard_map/ppermute | solution.py:95
  110.5 22.5 %collective-permute-start.27 = (bf16[384,2304]{1,0:T(8,128)(2,1)}, bf16[384,2304]{1,0:T(8,128)(2,1)}, u32[]{:S(2)}, u32[]{:S(2)}) collective-permute-start(bf16[384,2304]{1,0:T(8,128)(2,1)} %bitcast.44.refs_6_), channel_id=1, source_target_pairs={{0,4},{4,0},{8,12},{12,8},{16,20},{20,16},{24,28},{28,24},{1,5},{5... | collective-permute-start | bytes 5308424 | tf_op jit(solution)/shard_map/ppermute | solution.py:95
  114.9 16.0 %collective-permute-start.30 = (bf16[48,3840]{1,0:T(8,128)(2,1)S(1)}, bf16[48,3840]{1,0:T(8,128)(2,1)S(1)}, u32[]{:S(2)}, u32[]{:S(2)}) collective-permute-start(bf16[48,3840]{1,0:T(8,128)(2,1)S(1)} %slice.92), channel_id=1, source_target_pairs={{0,8},{4,12},{8,0},{12,4},{16,24},{20,28},{24,16},{28,20},{1,9},{5... | collective-permute-start | bytes 1105928 | tf_op jit(solution)/shard_map/ppermute | solution.py:95
  115.5 15.4 %collective-permute-start.28 = (bf16[48,3840]{1,0:T(8,128)(2,1)S(1)}, bf16[48,3840]{1,0:T(8,128)(2,1)S(1)}, u32[]{:S(2)}, u32[]{:S(2)}) collective-permute-start(bf16[48,3840]{1,0:T(8,128)(2,1)S(1)} %slice.91), channel_id=1, source_target_pairs={{0,16},{4,20},{8,24},{12,28},{16,0},{20,4},{24,8},{28,12},{1,17},{... | collective-permute-start | bytes 1105928 | tf_op jit(solution)/shard_map/ppermute | solution.py:95
  180.5 24.9 %collective-permute-start.39 = (bf16[2,96,2688]{2,1,0:T(8,128)(2,1)S(1)}, bf16[2,96,2688]{2,1,0:T(8,128)(2,1)S(1)}, u32[]{:S(2)}, u32[]{:S(2)}) collective-permute-start(bf16[2,96,2688]{2,1,0:T(8,128)(2,1)S(1)} %get-tuple-element.142), channel_id=1, source_target_pairs={{0,16},{4,20},{8,24},{12,28},{16,0},{20,4},{24,8},{28,12},{1,17},{... | collective-permute-start | bytes 3096584 | tf_op jit(solution)/shard_map/ppermute | solution.py:95
  182.3 24.6 %collective-permute-start.40 = (bf16[2,96,2688]{2,1,0:T(8,128)(2,1)S(1)}, bf16[2,96,2688]{2,1,0:T(8,128)(2,1)S(1)}, u32[]{:S(2)}, u32[]{:S(2)}) collective-permute-start(bf16[2,96,2688]{2,1,0:T(8,128)(2,1)S(1)} %get-tuple-element.144), channel_id=1, source_target_pairs={{0,8},{4,12},{8,0},{12,4},{16,24},{20,28},{24,16},{28,20},{1,9},{5... | collective-permute-start | bytes 3096584 | tf_op jit(solution)/shard_map/ppermute | solution.py:95
  208.7 14.9 %collective-permute-start.41 = (bf16[96,2688]{1,0:T(8,128)(2,1)}, bf16[96,2688]{1,0:T(8,128)(2,1)S(1)}, u32[]{:S(2)}, u32[]{:S(2)}) collective-permute-start(bf16[96,2688]{1,0:T(8,128)(2,1)} %get-tuple-element.163), channel_id=1, source_target_pairs={{0,8},{4,12},{8,0},{12,4},{16,24},{20,28},{24,16},{28,20},{1,9},{5... | collective-permute-start | bytes 1548296 | tf_op jit(solution)/shard_map/ppermute | solution.py:95
  210.2 14.7 %collective-permute-start.42 = (bf16[96,2688]{1,0:T(8,128)(2,1)S(1)}, bf16[96,2688]{1,0:T(8,128)(2,1)S(1)}, u32[]{:S(2)}, u32[]{:S(2)}) collective-permute-start(bf16[96,2688]{1,0:T(8,128)(2,1)S(1)} %get-tuple-element.165), channel_id=1, source_target_pairs={{0,16},{4,20},{8,24},{12,28},{16,0},{20,4},{24,8},{28,12},{1,17},{... | collective-permute-start | bytes 1548296 | tf_op jit(solution)/shard_map/ppermute | solution.py:95
  210.5 22.7 %collective-permute-start.43 = (bf16[2,96,1280]{2,1,0:T(8,128)(2,1)}, bf16[2,96,1280]{2,1,0:T(8,128)(2,1)}, u32[]{:S(2)}, u32[]{:S(2)}) collective-permute-start(bf16[2,96,1280]{2,1,0:T(8,128)(2,1)} %get-tuple-element.158), channel_id=1, source_target_pairs={{0,16},{4,20},{8,24},{12,28},{16,0},{20,4},{24,8},{28,12},{1,17},{... | collective-permute-start | bytes 1474568 | tf_op jit(solution)/shard_map/ppermute | solution.py:95
  212.2 19.0 %collective-permute-start.44 = (bf16[2,96,1152]{2,1,0:T(8,128)(2,1)}, bf16[2,96,1152]{2,1,0:T(8,128)(2,1)}, u32[]{:S(2)}, u32[]{:S(2)}) collective-permute-start(bf16[2,96,1152]{2,1,0:T(8,128)(2,1)} %get-tuple-element.160), channel_id=1, source_target_pairs={{0,8},{4,12},{8,0},{12,4},{16,24},{20,28},{24,16},{28,20},{1,9},{5... | collective-permute-start | bytes 1327112 | tf_op jit(solution)/shard_map/ppermute | solution.py:95
  226.4 22.6 %collective-permute-start.46 = (bf16[2,24,5376]{2,1,0:T(8,128)(2,1)}, bf16[2,24,5376]{2,1,0:T(8,128)(2,1)S(1)}, u32[]{:S(2)}, u32[]{:S(2)}) collective-permute-start(bf16[2,24,5376]{2,1,0:T(8,128)(2,1)} %get-tuple-element.174), channel_id=1, source_target_pairs={{0,1},{1,0},{2,3},{3,2},{4,5},{5,4},{6,7},{7,6},{8,9},{9,8},{10,11... | collective-permute-start | bytes 1548296 | tf_op jit(solution)/shard_map/ppermute | solution.py:878
  252.7 15.1 %collective-permute-start.50 = (bf16[24,2432]{1,0:T(8,128)(2,1)S(1)}, bf16[24,2432]{1,0:T(8,128)(2,1)S(1)}, u32[]{:S(2)}, u32[]{:S(2)}) collective-permute-start(bf16[24,2432]{1,0:T(8,128)(2,1)S(1)} %get-tuple-element.180), channel_id=1, source_target_pairs={{0,2},{1,3},{2,0},{3,1},{4,6},{5,7},{6,4},{7,5},{8,10},{9,11},{10,... | collective-permute-start | bytes 350216 | tf_op jit(solution)/shard_map/ppermute | solution.py:89
  253.4 14.4 %collective-permute-start.51 = (bf16[24,2432]{1,0:T(8,128)(2,1)S(1)}, bf16[24,2432]{1,0:T(8,128)(2,1)S(1)}, u32[]{:S(2)}, u32[]{:S(2)}) collective-permute-start(bf16[24,2432]{1,0:T(8,128)(2,1)S(1)} %get-tuple-element.181), channel_id=1, source_target_pairs={{0,3},{1,0},{2,1},{3,2},{4,7},{5,4},{6,5},{7,6},{8,11},{9,8},{10,9... | collective-permute-start | bytes 350216 | tf_op jit(solution)/shard_map/ppermute | solution.py:89
  (91 other events, 843.8 us)
Sparse Core Ops, SparseCore 0:
  26.2 33.0 all-gather.3
  61.4 39.2 all-gather.5
  157.8 65.6 reduce-scatter.1

commit v2 on v1

--- a/solution.py
+++ b/solution.py
@@ -22,7 +22,7 @@
 MiB = 1024 * 1024
 FIRST_AT = 4
 ORDER_AT = 12
-EARLY = 0.75
+EARLY = 0.5
 EARLY_GRAD = 0.5
 
 
@@ -45,15 +45,14 @@
     return edge_list
 
 
-def rolled_one_hot(rows):
+def distance_one_hot(rows):
     edges = np.array(bucket_edges(BUCKETS, REACH))
-    distances = (rows - np.arange(rows)) % rows
-    buckets = (distances[:, None] >= edges[None, :]).sum(axis=1)
+    buckets = (np.arange(rows)[:, None] >= edges[None, :]).sum(axis=1)
     return (np.arange(BUCKETS)[:, None] == buckets[None, :]).astype(np.float32)
 
 
 def table_hot(rows, blocks, share, table_rows):
-    one_hot = rolled_one_hot(rows)
+    one_hot = distance_one_hot(rows)
     groups = -(-table_rows // share)
     hot = np.zeros((groups, blocks * share, rows), np.float32)
     for block in range(blocks):
@@ -126,7 +125,7 @@
         self.arrays = arrays
         self.spots = spots
 
-    def load(self, place, refs, matrices, sems, ranges=None):
+    def load(self, place, refs, matrices, sems, ranges=None, lazy=False):
         waits = []
         count = 0
         for low, high in ranges or [(0, None)]:
@@ -142,10 +141,13 @@
                     )
                 )
                 count += 1
-            for copy in copies:
-                copy.start()
-            waits.append(lambda copies=copies: [copy.wait() for copy in copies])
-        return waits
+            waits.append((copies, lambda copies=copies: [copy.wait() for copy in copies]))
+            if not lazy:
+                for copy in copies:
+                    copy.start()
+        if lazy:
+            return waits
+        return [wait for _, wait in waits]
 
     def sems(self, ranges=1):
         return [pltpu.SemaphoreType.DMA((max(len(self.spots) * ranges, 1),))]
@@ -300,21 +302,20 @@
     def step(pair, carry):
         q = q_ref[:, lanes_of(pair, columns[0])]
         k = k_ref[:, lanes_of(pair, columns[1])]
-        v = v_ref[:, lanes_of(pair, columns[2])]
-        result = None
+        v_turned = v_ref[:, lanes_of(pair, columns[2])].T
         for head in range(2):
             mine = head_mask(rows, head)
-            scores = dot(jnp.where(mine, q, jnp.zeros_like(q)), k, NT)
+            scores = dot(k, jnp.where(mine, q, jnp.zeros_like(q)), NT)
             if bias is not None:
-                row = jnp.broadcast_to(bias[pl.ds(2 * pair + head, 1), :], (rows, cols))
+                row = jnp.broadcast_to(bias[pl.ds(2 * pair + head, 1), :], (cols, rows))
                 scores = scores + pltpu.roll(row, 0, 1, stride=1, stride_axis=0)
             scores = jnp.where(allowed[...] > 0, scores, -1e9)
-            weights = jnp.exp(scores - jnp.max(scores, axis=1, keepdims=True))
-            probs = (weights * (1.0 / jnp.sum(weights, axis=1, keepdims=True))).astype(LOW)
+            weights = jnp.exp(scores - jnp.max(scores, axis=0, keepdims=True))
+            probs = (weights * (1.0 / jnp.sum(weights, axis=0, keepdims=True))).astype(LOW)
             prob_ref[2 * pair + head] = probs
-            part = dot(probs, v)
-            result = part if head == 0 else jnp.where(mine, part, result)
-        out_ref[:, lanes_of(pair)] = result.astype(LOW)
+            part = dot(v_turned[head * 64 : head * 64 + 64], probs)
+            first = pl.multiple_of(pair * LANES + head * 64, 64)
+            out_ref[pl.ds(first, 64), :] = part.astype(LOW)
         return carry
 
     lax.fori_loop(0, PAIRS, step, 0)
@@ -329,23 +330,27 @@
         k = k_ref[:, lanes_of(pair, columns[1])]
         v = v_ref[:, lanes_of(pair, columns[2])]
         g = g_ref[:, lanes_of(pair)]
+        k_turned = k.T
         if dist_ref is not None:
-            i = lax.broadcasted_iota(jnp.int32, (rows, rows), 0)
-            j = lax.broadcasted_iota(jnp.int32, (rows, rows), 1)
-            flip = (i + j == rows - 1).astype(LOW)
+            i = lax.broadcasted_iota(jnp.int32, (cols, cols), 0)
+            j = lax.broadcasted_iota(jnp.int32, (cols, cols), 1)
+            flip = (i + j == cols - 1).astype(LOW)
         grads = None
+        query_parts = []
         for head in range(2):
-            mine = head_mask(rows, head)
+            mine = head_mask(cols, head)
             low_probs = prob_ref[2 * pair + head]
             probs = low_probs.astype(F32)
-            moved = probs * dot(jnp.where(mine, g, jnp.zeros_like(g)), v, NT)
-            low_scores = (moved - probs * jnp.sum(moved, axis=1, keepdims=True)).astype(LOW)
+            moved = probs * dot(v, jnp.where(head_mask(rows, head), g, jnp.zeros_like(g)), NT)
+            low_scores = (moved - probs * jnp.sum(moved, axis=0, keepdims=True)).astype(LOW)
             if dist_ref is not None:
                 lined = pltpu.roll(dot(flip, low_scores), 1, 1, stride=1, stride_axis=0)
                 dist_ref[pl.ds(2 * pair + head, 1), :] = jnp.sum(lined, axis=0, keepdims=True)
-            new = (dot(low_scores, k), dot(low_scores, q, TN), dot(low_probs, g, TN))
+            query_parts.append(dot(k_turned[head * 64 : head * 64 + 64], low_scores))
+            new = (dot(low_scores, q), dot(low_probs, g))
             grads = new if head == 0 else tuple(jnp.where(mine, b, a) for a, b in zip(grads, new))
-        for (ref, column), grad in zip(outs, grads):
+        query_grad = jnp.concatenate(query_parts, axis=0).T
+        for (ref, column), grad in zip(outs, (query_grad, *grads)):
             ref[:, lanes_of(pair, column)] = grad.astype(LOW)
         return carry
 
@@ -371,7 +376,7 @@
         wait, wait_late = weights.load(place, pieces, [matrix], sems, [(0, cut), (cut, cut + 2 * width)])
         i = lax.broadcasted_iota(jnp.int32, (rows, rows), 0)
         j = lax.broadcasted_iota(jnp.int32, (rows, rows), 1)
-        same = (row_ids[...] == col_ids[...]) & (j <= i) & ((pad[...] == 1) | (i == j))
+        same = (row_ids[...] == col_ids[...]) & (i <= j) & ((pad[...] == 1) | (i == j))
         allowed[...] = same.astype(F32)
         residual = tok[...].astype(F32)
         scaled = residual * scale_of(residual)
@@ -391,8 +396,8 @@
         v[...] = dot(normed, matrix[:, cut : cut + width]).astype(LOW)
         attend(qk, qk, v, (0, width, 0), allowed, bias, probs, att)
         attended = att[...]
-        split_rows(attended.T, place[2], keep.at[1], send.at[1])
-        out[...] = residual + dot(attended, matrix[:, cut + width :])
+        split_rows(attended, place[2], keep.at[1], send.at[1])
+        out[...] = residual + dot(attended, matrix[:, cut + width :], TN)
 
     halves = ((2, blocks, block, rows), LOW)
     return run(
@@ -412,7 +417,7 @@
             pltpu.VMEM((width, cut + 2 * width), LOW),
             pltpu.VMEM((rows, rows), F32),
             pltpu.VMEM((16, rows), F32),
-            pltpu.VMEM((rows, width), LOW),
+            pltpu.VMEM((width, rows), LOW),
         ]
         + weights.sems(2),
         flops=8 * rows * width * width,
@@ -441,8 +446,8 @@
         q[...] = dot(normed, matrix[:, :width]).astype(LOW)
         attend(q, kv, kv, (0, 0, width), allowed, None, probs, att)
         attended = att[...]
-        split_rows(attended.T, place[2], keep.at[1], send.at[1])
-        out[...] = residual + dot(attended, matrix[:, width : 2 * width])
+        split_rows(attended, place[2], keep.at[1], send.at[1])
+        out[...] = residual + dot(attended, matrix[:, width : 2 * width], TN)
 
     halves = ((3, blocks, block, rows), LOW)
     return run(
@@ -452,15 +457,15 @@
         [
             ((rows, width), LOW, None),
             ((mem_rows, 2 * width), LOW, None),
-            ((2 * PAIRS, rows, mem_rows), LOW, None),
+            ((2 * PAIRS, mem_rows, rows), LOW, None),
             ((rows, width), F32),
             halves,
             halves,
         ],
         [
             pltpu.VMEM((width, 4 * width), LOW),
-            pltpu.VMEM((rows, mem_rows), F32),
-            pltpu.VMEM((rows, width), LOW),
+            pltpu.VMEM((mem_rows, rows), F32),
+            pltpu.VMEM((width, rows), LOW),
         ]
         + weights.sems(2),
         flops=8 * rows * width * width,
@@ -520,7 +525,7 @@
         for start in range(0, ff, CHUNK):
             stop = start + CHUNK
             u = dot(normed, m_in[:, start:stop])
-            ga = dot(grad, m_out[start:stop, :], NT).astype(LOW).astype(F32)
+            ga = dot(grad, m_out[start:stop, :], NT)
             square = u * u
             t = jnp.tanh(factor * u * (1.0 + 0.044715 * square))
             half = 0.5 * (1.0 + t)
@@ -595,17 +600,24 @@
         out, mem_grad, back_out, gain_out, branch, grad, x, q, kv, probs, matrix, att, own_sems, sems = refs
         ranges = [(width, 2 * width), (0, width), (2 * width, 4 * width)]
         branch_wait = fetch(far[:1], (branch,), own_sems)
-        loaded = weights.load(place, pieces, [matrix], sems, ranges)
-        waits = fetch(far[1:], (kv, probs, q, x, grad), own_sems.at[pl.ds(1, 5)])
+        loaded = weights.load(place, pieces, [matrix], sems, ranges, True)
+        for copy in loaded[0][0]:
+            copy.start()
+        waits = fetch(far[1:4], (kv, probs, q), own_sems.at[pl.ds(1, 3)])
+        for copy in loaded[1][0] + loaded[2][0]:
+            copy.start()
+        late_waits = fetch(far[4:], (x, grad), own_sems.at[pl.ds(4, 2)])
         branch_wait[0]()
-        loaded[0]()
+        loaded[0][1]()
         att[...] = dot(branch[...], matrix[:, width : 2 * width], NT).astype(LOW)
         outs = ((out, 0), (out, width), (out, 2 * width))
         for wait in waits:
             wait()
         attend_back(q, kv, kv, (0, 0, width), att, probs, outs, None)
-        loaded[1]()
-        loaded[2]()
+        loaded[1][1]()
+        loaded[2][1]()
+        for wait in late_waits:
+            wait()
         back, gain = norm_back(x[...], gains[1:2, :], dot(out[:, :width], matrix[:, :width], NT))
         total = grad[...] + back
         back_out[...] = total
@@ -631,7 +643,7 @@
             pltpu.VMEM((rows, width), F32),
             pltpu.VMEM((rows, width), LOW),
             pltpu.VMEM((mem_rows, 2 * width), LOW),
-            pltpu.VMEM((2 * PAIRS, rows, mem_rows), LOW),
+            pltpu.VMEM((2 * PAIRS, mem_rows, rows), LOW),
             pltpu.VMEM((width, 4 * width), LOW),
             pltpu.VMEM((rows, width), LOW),
             pltpu.SemaphoreType.DMA((6,)),
@@ -648,23 +660,28 @@
     heads = 2 * PAIRS
     groups = hot.shape[0]
     blocks = (width // block) // 2
+    under = width // 2 * LANES // width
 
     def kernel(place, grad, before, tok, gains, cross_gain, hidden_gain, hot, qk_far, v_far, probs_far, *refs):
         pieces, refs = refs[:count], refs[count:]
-        out, out_v, tok_grad, extra_keep, extra_send, qk, v, probs, matrix, att, dist, parts, own_sems, sems = refs
+        out_q, out_k, out_v, tok_grad, extra_keep, extra_send, qk, v, probs, matrix, att, dist, parts, own_sems, sems = refs
         ranges = [(cut + width, cut + 2 * width), (0, cut + width)]
-        loaded = weights.load(place, pieces, [matrix], sems, ranges)
+        loaded = weights.load(place, pieces, [matrix], sems, ranges, True)
+        for copy in loaded[0][0]:
+            copy.start()
         waits = fetch((v_far, probs_far, qk_far), (v, probs, qk), own_sems)
-        loaded[0]()
+        for copy in loaded[1][0]:
+            copy.start()
+        loaded[0][1]()
         att[...] = dot(before[:, 3 * width :], matrix[:, cut + width :], NT).astype(LOW)
-        outs = ((out, 0), (out, width), (out_v, 0))
+        outs = ((out_q, 0), (out_k, 0), (out_v.at[:rows], 0))
         dist[...] = jnp.zeros_like(dist)
         for wait in waits:
             wait()
         attend_back(qk, qk, v, (0, width, 0), att, probs, outs, dist)
-        loaded[1]()
-        normed_grad = dot(out[...], matrix[:, : 2 * width], NT)
-        normed_grad = normed_grad + dot(out_v[...], matrix[:, cut : cut + width], NT)
+        loaded[1][1]()
+        normed_grad = dot(out_q[...], matrix[:, :width], NT) + dot(out_k[...], matrix[:, width : 2 * width], NT)
+        normed_grad = normed_grad + dot(out_v[:rows, :], matrix[:, cut : cut + width], NT)
         back, gain = norm_back(tok[...].astype(F32), gains[0:1, :], normed_grad)
         tok_grad[...] = grad[...] + back
         parts[...] = jnp.zeros_like(parts)
@@ -683,6 +700,9 @@
             table = part if table is None else table + part
         columns = columns + jnp.concatenate([table] * (2 * blocks), axis=0)
         split_rows(columns, place[2], extra_keep, extra_send)
+        sending = extra_send[...].astype(F32).reshape(width // 2, LANES)
+        for n in range(width // LANES):
+            out_v[rows:, n * LANES : (n + 1) * LANES] = sending[n * under : (n + 1) * under].astype(LOW)
 
     halves = ((blocks, block, LANES), LOW)
     return run(
@@ -691,8 +711,9 @@
         [(place, pltpu.SMEM)]
         + vmem(grad, cross_grads, tokens, gains, cross_gain, hidden_gain, hot)
         + [(array, pltpu.HBM) for array in (qk, v, probs)],
-        [((rows, 2 * width), LOW), ((rows, width), LOW), ((rows, width), F32, None), halves, halves],
+        [((rows, width), LOW)] * 2 + [((rows + under, width), LOW), ((rows, width), F32, None), halves],
         [
+            pltpu.VMEM(halves[0], LOW),
             pltpu.VMEM((rows, 2 * width), LOW),
             pltpu.VMEM((rows, width), LOW),
             pltpu.VMEM((heads, rows, rows), LOW),
@@ -724,7 +745,7 @@
         left = [(refs.pop(0), refs.pop(0)) for _ in range(left_count)]
         right = [(refs.pop(0), refs.pop(0)) for _ in range(right_count)]
         extra = [refs.pop(0) for _ in extras]
-        gathered = refs.pop()
+        far_extra, gathered = refs.pop(), refs.pop()
         outs = (refs[: counts[0]], refs[counts[0] : counts[0] + counts[1]])
         out_z = refs[-1]
 
@@ -744,7 +765,7 @@
                         ]
             for first in range(0, width, 768):
                 size = min(768, width - first)
-                own, far = (ref[:, column + first : column + first + size] for ref in right[r])
+                own, far = (ref[:tokens, column + first : column + first + size] for ref in right[r])
                 if joined:
                     total = dot(gathered[: blocks * rows, :tokens], own)
                     total = total + dot(gathered[: blocks * rows, tokens:], far)
@@ -771,9 +792,15 @@
                     at = section[5] + g * section[3] + first
                     part = total[g * block : (g + 1) * block].astype(LOW)
                     outs[half][k // counts[1 - half]][k % counts[1 - half], :, at : at + size] = part
+        if extras:
+            sent_ref = right[-1][1]
+            under = sent_ref.shape[0] - tokens
+            for n in range(blocks * block // under):
+                far_extra[n * under : (n + 1) * under, :] = sent_ref[tokens:, n * LANES : (n + 1) * LANES].astype(F32)
         for k in range(blocks if extras else 0):
             index = place_of(0, k)
-            both = extra[0][index].astype(F32) + extra[1][index].astype(F32)
+            start = pl.multiple_of(index * block, 8)
+            both = extra[0][index].astype(F32) + far_extra[pl.ds(start, block), :]
             outs[0][k // counts[1]][k % counts[1], :, cols[0] - LANES :] = both.astype(LOW)
 
     arrays = [array for pair in lefts for array in pair] + [array for pair in rights for array in pair]
@@ -788,7 +815,7 @@
         kernel,
         [(place, pltpu.SMEM)] + vmem(*arrays, *extras),
         outputs,
-        [pltpu.VMEM((blocks * most, 2 * tokens), LOW)],
+        [pltpu.VMEM((blocks * most, 2 * tokens), LOW), pltpu.VMEM((blocks * block, LANES), F32)],
         flops=sum(4 * s[0][3] * blocks * rights[0][0].shape[0] * s[3] for s in (*sections, *straight)),
     )
 
@@ -881,6 +908,62 @@
 def by_blocks(parts):
     count = grid_sizes()["z"]
     return [part.reshape(count, part.shape[0] // count, part.shape[1]) for part in parts]
+
+
+def finish_first(place, cross, early, order, early_cols, late, width, ff):
+    share, cols = cross[0].shape[1:]
+    cols = cols // 2
+    side = width // 2
+    folds = ff // width
+
+    def kernel(place, near, far, kept, kept_far, other, order, c_query, c_key, c_value, c_output, s_output, h_in, h_out):
+        total = near[0].astype(F32) + far[0].astype(F32)
+        c_query[...] = total[:, :width]
+        c_output[...] = total[:, width : 2 * width]
+        s_output[:, :side] = total[:, 2 * width : 2 * width + side]
+        c_key[...] = total[:, cols : cols + width]
+        c_value[...] = total[:, cols + width : cols + 2 * width]
+        s_output[:, side:] = total[:, cols + 2 * width : cols + 2 * width + side]
+        x = place[1]
+        first = kept[x].astype(F32) + kept_far[x].astype(F32) + other[...].astype(F32)
+        for n in range(folds):
+            h_out[n * share : (n + 1) * share, :] = first[:, early_cols + n * width : early_cols + (n + 1) * width]
+        at = 2 * width + side
+        pieces = [(first, 0, early_cols), (total, at, late), (total, cols + at, late)]
+        start = 0
+        for source, column, count in pieces:
+            for n in range(0, count, CHUNK):
+                part = source[:, column + n : column + n + CHUNK].astype(LOW)
+                h_in[:, start : start + CHUNK] = dot(part, order[...], NT)
+                start += CHUNK
+
+    square = ((share, width), F32, None)
+    return run(
+        "finish_first",
+        kernel,
+        [(place, pltpu.SMEM)] + vmem(*cross, *early, order),
+        [square] * 5 + [((share, ff), F32, None), ((share * folds, width), F32, None)],
+    )
+
+
+def finish_second(parts, width):
+    share = parts[0].shape[0]
+    side = width // 2
+    cut = width + side + LANES
+
+    def kernel(*refs):
+        parts, (query, key, value, small) = refs[:-4], refs[-4:]
+        total = parts[0][...].astype(F32)
+        for part in parts[1:]:
+            total = total + part[...].astype(F32)
+        query[...] = total[:, :width]
+        key[:, :side] = total[:, width : width + side]
+        key[:, side:] = total[:, cut : cut + side]
+        value[...] = total[:, cut + side :]
+        small[...] = total[:, width + side : cut]
+
+    square = ((share, width), F32, None)
+    return run("finish_second", kernel, vmem(*parts), [square] * 3 + [((share, LANES), F32, None)])
 
 
 def total_of(parts):
@@ -988,7 +1071,7 @@
 
     og_far = swapped(out_grad)
     qk, v, self_probs, after_self, s_keep, s_send, gains = self_forward(
-        place, after(tokens, og_far), seg_ids[:, None], seg_ids[None], pad_mask[None], hot, w_self, cut, block
+        place, after(tokens, og_far), seg_ids[:, None], seg_ids[None], pad_mask[:, None], hot, w_self, cut, block
     )
     s_far = swapped(s_send)
     if pieces:
@@ -996,6 +1079,8 @@
         rest_x, rest_y = (after(array, after_self, s_far, twin) for array in rest_near[1:])
         corner = from_corner(rest_x[:half, :ff], rest_y[half:, :ff])
         upper, lower = rest_x[:half, ff:], rest_y[half:, ff:]
+        in_all = jnp.transpose(after(in_all, twin), (1, 0, 2, 3)).reshape(4 * block, early_cols)
+        corner = [after(array, upper, lower, in_all) for array in corner]
         rest_arrays = [rest_near[0], twin] + with_twins([rest_x, rest_y])
         w_cross = Weights(
             rest_arrays + with_twins(corner),
@@ -1010,7 +1095,7 @@
         m_out = jnp.transpose(rest[:, 2 * ff :].reshape(-1, block, folds, width), (0, 2, 1, 3)).reshape(ff, width)
         cross_in = after_self
     q, kv, cross_probs, after_cross, c_keep, c_send = cross_forward(
-        place, cross_in, memory, gains, seg_ids[:, None], mem_ids[None], w_cross, block
+        place, cross_in, memory, gains, mem_ids[:, None], seg_ids[None], w_cross, block
     )
     c_far = swapped(c_send)
     if pieces:
@@ -1019,13 +1104,12 @@
         if late_cols:
             spots += near_spots(range(6), block, ff, 0, early_cols, late_cols)
         early = list(rest_arrays)
-        in_all = jnp.transpose(after(in_all, *corner), (1, 0, 2, 3)).reshape(4 * block, early_cols)
         for twin, array in enumerate((in_all, swapped(in_all))):
             spots += [
                 (6 + twin, n * block, 0, ORDER_AT + 2 * n + twin, block, 0, block, 0, 0, early_cols) for n in range(4)
             ]
             early.append(array)
-        m_in, m_out = hidden_early(after(place, after_cross, c_far), Weights(early, spots), width, ff)
+        m_in, m_out = hidden_early(after(place, after_cross), Weights(early, spots), width, ff)
         last = with_twins([after(array, after_cross) for array in last])
         spots = folded_spots(half_spots(range(4), block, 0, 1, 0, 0), block, late_cols, folds, width, 1)
         if late_cols:
@@ -1089,22 +1173,22 @@
     cross_first, cross_second = sent(cross_first, "y"), sent(cross_second, "x")
 
     grad = after(grad, *cross_parts)
-    self_grads, self_dv, tokens_grad, extra_keep, extra_send = self_backward(
+    self_dq, self_dk, self_dv, tokens_grad, extra_keep = self_backward(
         place, grad, cross_grads, tokens, gains, cross_gain_part, hidden_gain_part, qk, v,
         self_probs, hot, w_self, cut, block,
     )
     self_parts = weight_grads(
         place,
         [(s_keep, s_far)],
-        [(self_grads, swapped(self_grads)), (self_dv, swapped(self_dv))],
+        [(self_dq, swapped(self_dq)), (self_dk, swapped(self_dk)), (self_dv, swapped(self_dv))],
         [
             ((0, 0, 0, block), 0, 0, width, 0, 0),
-            ((0, 0, 0, block), 0, width, side, 0, width),
-            ((0, 0, 0, block), 0, width + side, side, 1, 0),
-            ((0, 0, 0, block), 1, 0, width, 1, side),
+            ((0, 0, 0, block), 1, 0, side, 0, width),
+            ((0, 0, 0, block), 1, side, side, 1, 0),
+            ((0, 0, 0, block), 2, 0, width, 1, side),
         ],
         (width + side + LANES, width + side),
-        (extra_keep, swapped(extra_send)),
+        (extra_keep,),
     )
     self_first, self_second = self_parts[:ny], self_parts[ny:]
     self_first, self_second = sent(self_first, "y"), sent(self_second, "x")
@@ -1127,50 +1211,47 @@
         cross_parts = halve(place, [[after(part, *earlier) for part in cross_parts]], count, False)
     self_first = [after(self_first[0], cross_parts[0])] + self_first[1:]
     self_sums = add_last(place, (self_first, self_second))
+    self_parts = sent(self_sums, "z")
     if pieces:
-        in_early = total_of(scatter_along([after(part, cross_parts[0]) for part in in_early], "x"))
-    cross_total = total_of([part[0] for part in cross_parts])
-    self_total = total_of(sent(self_sums, "z"))
-
-    at = 2 * width + side
-    in_parts = [cross_total[:, n + at : n + at + late] for n in (0, cross_cols)]
-    if pieces:
-        in_parts = [in_early[:, :early_grads]] + in_parts
-        out_part = in_early[:, early_grads:].reshape(share, folds, width)
+        in_early = [after(part, cross_parts[0]) for part in in_early]
+        there = total_of([lax.dynamic_index_in_dim(part, 1 - here["x"], 0, keepdims=False) for part in in_early])
+        in_early.append(shifted(there.astype(LOW), "x", 1))
+        *cross_grads, in_grad, out_part = finish_first(
+            place, cross_parts, in_early, order, early_grads, late, width, ff
+        )
+        self_parts = [after(self_parts[0], in_grad)] + self_parts[1:]
     else:
-        out_part = jnp.concatenate(
-            [cross_total[:, n + at + late : n + cross_cols].reshape(share, folds, side) for n in (0, cross_cols)],
-            axis=2,
-        )
-    in_grad = reorder(jnp.concatenate([part.astype(LOW) for part in in_parts], axis=1), order, NT, F32)
-    out_part = jnp.transpose(out_part, (1, 0, 2)).reshape(ff_share, width)
-    first_cols = width + side + LANES
-    last = self_total[:, width + side : first_cols]
+        cross_total = total_of([part[0] for part in cross_parts])
+        at = 2 * width + side
+        halves = [cross_total[:, n : n + cross_cols] for n in (0, cross_cols)]
+        in_grad = jnp.concatenate([part[:, at : at + late].astype(LOW) for part in halves], axis=1)
+        in_grad = reorder(in_grad, order, NT, F32)
+        out_part = jnp.concatenate([part[:, at + late :].reshape(share, folds, side) for part in halves], axis=2)
+        out_part = jnp.transpose(out_part, (1, 0, 2)).reshape(ff_share, width)
+        cross_grads = [
+            halves[0][:, :width],
+            halves[1][:, :width],
+            halves[1][:, width : 2 * width],
+            halves[0][:, width : 2 * width],
+            jnp.concatenate([part[:, 2 * width : at] for part in halves], axis=1),
+        ]
+    query_grad, key_grad, value_grad, last = finish_second(self_parts, width)
     table_grad = last[:, TABLE_LANE : TABLE_LANE + groups * heads].reshape(share, groups, heads)
     table_grad = jnp.transpose(table_grad, (1, 0, 2)).reshape(groups * share, heads)[:table_rows]
-    key_grad = jnp.concatenate(
-        [self_total[:, width : width + side], self_total[:, first_cols : first_cols + side]], axis=1
-    )
-    output_grad = jnp.concatenate(
-        [cross_total[:, n + 2 * width : n + 2 * width + side] for n in (0, cross_cols)], axis=1
-    )
     return (
         layer_out,
         tokens_grad,
         memory_grad,
-        self_total[:, :width],
+        query_grad,
         key_grad,
-        self_total[:, first_cols + side :],
-        output_grad,
+        value_grad,
+        cross_grads[4],
         last[:, 0],
         table_grad,
-        cross_total[:, :width],
-        cross_total[:, cross_cols : cross_cols + width],
-        cross_total[:, cross_cols + width : cross_cols + 2 * width],
-        cross_total[:, width : 2 * width],
+        *cross_grads[:4],
         last[:, 1],
         in_grad,
-        out_part.astype(F32),
+        out_part,
         last[:, 2],
     )
 

time: 282 us -> 272 us (0.965)
  waiting for transfers between devices: 107 us -> 97.7 us
  starting transfers between devices: 40.2 us -> 43.2 us
    ppermute x6, waiting for transfers between devices: 18.6 us -> 6.74 us  [shifted(): lax.ppermute(array, 'narrow', [(i, (i + step) % count) for i in range(cou...]
    ppermute x2, waiting for transfers between devices: 0.01 us -> 3.07 us  [halve(): return (keep, lax.ppermute(send, 'narrow', pairs))]
    pallas_call x17 -> x18, Pallas kernels: 81.1 us -> 78.9 us  [run(): pl.pallas_call(kernel, name=name, in_specs=[pl.BlockSpec(memory_space=spa...]
    unnamed x122 -> x121, local copies, waits for them, and re-layouts: 16.9 us -> 15.4 us
  transfers between devices with their start and end apart: 57 -> 57, of which waited for: 31 -> 28; matrix products, arithmetic and copies ran while one was open for 7% -> 6% of each run, Pallas kernels for 24% -> 24%
where the time goes in v2:
time: 272 us
  waiting for transfers between devices  97.7 us (36%)
  Pallas kernels  78.9 us (29%)
  starting transfers between devices  43.2 us (16%)
  local copies, waits for them, and re-layouts  32.3 us (12%)
  between operations  14.6 us (5%)
  other arithmetic  4.9 us (2%)
    ppermute x46, waiting for transfers between devices, shifted(): return lax.ppermute(array, 'wide', pairs)  84.8 us
    pallas_call x18, Pallas kernels, run(): pl.pallas_call(kernel, name=name, in_specs=[pl.BlockSpec(memory_space=spa...  78.9 us
    ppermute x46, starting transfers between devices, shifted(): return lax.ppermute(array, 'wide', pairs)  30.8 us
    unnamed x121, local copies, waits for them, and re-layouts  15.4 us
    ppermute x6, starting transfers between devices, shifted(): lax.ppermute(array, 'narrow', [(i, (i + step) % count) for i in range(cou...  10.1 us
    ppermute x6, waiting for transfers between devices, shifted(): lax.ppermute(array, 'narrow', [(i, (i + step) % count) for i in range(cou...  6.74 us
  transfers between devices with their start and end apart: 57, of which 28 were waited for; matrix products, arithmetic and copies ran while one was open for 6% of the time, Pallas kernels for 24%

profile of v2, /device:TPU:0, one launch (start us, length us, event | category | flops | bytes accessed | tf_op | source)
XLA Modules:
  0.0 271.5 jit_solution(2066576895266768235)
XLA Ops:
  11.1 5.1 %collective-permute-start.3 = (bf16[24,3200]{1,0:T(8,128)(2,1)S(1)}, bf16[24,3200]{1,0:T(8,128)(2,1)S(1)}, u32[]{:S(2)}, u32[]{:S(2)}) collective-permute-start(bf16[24,3200]{1,0:T(8,128)(2,1)S(1)} %concatenate.34), channel_id=1, source_target_pairs={{0,3},{1,0},{2,1},{3,2},{4,7},{5,4},{6,5},{7,6},{8,11},{9,8},{10,9... | collective-permute-start | bytes 460808 | tf_op jit(solution)/shard_map/ppermute | solution.py:88
  32.5 12.2 %collective-permute-done.7.refs_4_ = bf16[96,3200]{1,0:T(8,128)(2,1)S(1)} collective-permute-done((bf16[96,3200]{1,0:T(8,128)(2,1)S(1)}, bf16[96,3200]{1,0:T(8,128)(2,1)S(1)}, u32[]{:S(2)}, u32[]{:S(2)}) %collective-permute-start.7) | collective-permute-done | bytes 614432 | tf_op jit(solution)/shard_map/ppermute | solution.py:94
  44.8 2.6 collective-permute-done.5.refs_2_
  51.6 5.7 %collective-permute-done.11.refs_8_ = bf16[48,3200]{1,0:T(8,128)(2,1)} collective-permute-done((bf16[48,3200]{1,0:T(8,128)(2,1)S(1)}, bf16[48,3200]{1,0:T(8,128)(2,1)}, u32[]{:S(2)}, u32[]{:S(2)}) %collective-permute-start.11) | collective-permute-done | bytes 307232 | tf_op jit(solution)/shard_map/ppermute | solution.py:94
  60.3 3.0 %all-gather.4.cloned.1.call-done.refs_0_.refs_6_ = bf16[96,7680]{1,0:T(8,128)(2,1)} async-done(((bf16[24,7680]{1,0:T(8,128)(2,1)}), bf16[96,7680]{1,0:T(8,128)(2,1)}) %all-gather.4.cloned.1.call-update) | async-done | bytes 1474576 | tf_op jit(solution)/shard_map/all_gather | solution.py:1050
  70.6 9.5 %self_forward.1 = (bf16[256,1536]{1,0:T(8,128)(2,1)S(1)}, bf16[256,768]{1,0:T(8,128)(2,1)S(1)}, bf16[12,256,256]{2,1,0:T(8,128)(2,1)S(1)}, f32[256,768]{1,0:T(8,...) custom-call(s32[20]{0:T(128)S(1)} %stack.118.place, ...), custom_call_target="tpu_custom_call" | custom-call | flops 1207959552 | bytes 2680360 | tf_op jit(solution)/shard_map/self_forward/pallas_call | solution.py:235
  85.4 11.4 %collective-permute-done.16.refs_4_.refs_10_ = bf16[96,7680]{1,0:T(8,128)(2,1)S(1)} collective-permute-done((bf16[96,7680]{1,0:T(8,128)(2,1)}, bf16[96,7680]{1,0:T(8,128)(2,1)S(1)}, u32[]{:S(2)}, u32[]{:S(2)}) %collective-permute-start.16) | collective-permute-done | bytes 1474592 | tf_op jit(solution)/shard_map/ppermute | solution.py:94
  96.8 3.0 %collective-permute-done.14.refs_2_.refs_8_ = bf16[96,7680]{1,0:T(8,128)(2,1)} collective-permute-done((bf16[96,7680]{1,0:T(8,128)(2,1)}, bf16[96,7680]{1,0:T(8,128)(2,1)}, u32[]{:S(2)}, u32[]{:S(2)}) %collective-permute-start.14) | collective-permute-done | bytes 1474592 | tf_op jit(solution)/shard_map/ppermute | solution.py:94
  116.2 9.4 %cross_forward.1 = (bf16[256,768]{1,0:T(8,128)(2,1)S(1)}, bf16[256,1536]{1,0:T(8,128)(2,1)S(1)}, bf16[12,256,256]{2,1,0:T(8,128)(2,1)S(1)}, f32[256,768]{1,0:T(8...) custom-call(s32[20]{0:T(128)S(1)} %stack.118.place, ...), custom_call_target="tpu_custom_call" | custom-call | flops 1207959552 | bytes 5616680 | tf_op jit(solution)/shard_map/cross_forward/pallas_call | solution.py:235
  128.6 4.2 %hidden_early.1 = (bf16[768,3072]{1,0:T(8,128)(2,1)S(1)}, bf16[3072,768]{1,0:T(8,128)(2,1)S(1)}) custom-call(s32[20]{0:T(128)S(1)} %stack.118.place, bf16[96,7680]{1,0:T(8,128)(2,1)} %all-gather.4.cloned.1.call-done.refs_0_.refs_6_, bf16[96,7680]{1,0:T(8,128)(2,1)} %collective-permute-done.15.refs_1_.refs_7_, ...), custom_call_target="tpu_custom_call" | custom-call | bytes 5603368 | tf_op jit(solution)/shard_map/hidden_early/pallas_call | solution.py:235
  134.6 7.5 %hidden_first.1 = (bf16[256,3072]{1,0:T(8,128)(2,1)S(1)}, bf16[256,3072]{1,0:T(8,128)(2,1)S(1)}, bf16[4,480,256]{2,1,0:T(8,128)(2,1)S(1)}, bf16[4,480,256]{2,1,0...) custom-call(s32[20]{0:T(128)S(1)} %stack.118.place, ...), custom_call_target="tpu_custom_call", output_to_operand_aliasing={{4}: (4, {}), {5}: (5, {})} | custom-call | flops 2415919104 | bytes 6205480 | tf_op jit(solution)/shard_map/hidden_first/pallas_call | solution.py:235
  143.4 3.5 %hidden_second.1 = (bf16[256,768]{1,0:T(8,128)(2,1)}, f32[256,768]{1,0:T(8,128)S(1)}, bf16[256,768]{1,0:T(8,128)(2,1)S(1)}, f32[1,768]{1,0:T(1,128)S(1)}) custom-call(f32[256,768]{1,0:T(8,128)S(1)} %get-tuple-element.132.x, bf16[256,768]{1,0:T(8,128)(2,1)S(1)} %copy-done, f32[8,768]{1,0:T(8,128)S(1)} %copy-done.25, ...), custom_call_target="tpu_custom_call" | custom-call | flops 2415919104 | bytes 6893568 | tf_op jit(solution)/shard_map/hidden_second/pallas_call | solution.py:235
  148.6 4.4 %weight_grads.3 = bf16[4,4,24,4608]{3,2,1,0:T(8,128)(2,1)} custom-call(s32[20]{0:T(128)S(1)} %stack.118.place, bf16[1,4,480,256]{3,2,1,0:T(8,128)(2,1)S(1)} %bitcast.72, bf16[1,4,480,256]{3,2,1,0:T(8,128)(2,1)S(1)} %bitcast.74, bf16[256,3072]{1,0:T(8,128)(2,1)S(1)} %get-tuple-element.139.gu.refs_2_.refs_10_, ...), custom_call_target="tpu_custom_call" | custom-call | flops 1811939328 | bytes 2949160 | tf_op jit(solution)/shard_map/weight_grads/pallas_call | solution.py:235
  156.8 12.3 %cross_backward.1 = (bf16[256,3072]{1,0:T(8,128)(2,1)S(1)}, f32[256,768]{1,0:T(8,128)}, f32[256,768]{1,0:T(8,128)S(1)}, f32[1,768]{1,0:T(1,128)S(1)}) custom-call(s32[20]{0:T(128)S(1)} %stack.118.place, f32[8,768]{1,0:T(8,128)S(1)} %copy-done.26, bf16[256,768]{1,0:T(8,128)(2,1)} %copy-done.17, bf16[256,1536]{1,0:T(8,128)(2,1)} %copy-done.21, ...), custom_call_target="tpu_custom_call" | custom-call | flops 1207959552 | bytes 7385128 | tf_op jit(solution)/shard_map/cross_backward/pallas_call | solution.py:235
  169.5 3.0 %collective-permute-done.35.refs_7_ = bf16[256,3072]{1,0:T(8,128)(2,1)S(1)} collective-permute-done((bf16[256,3072]{1,0:T(8,128)(2,1)S(1)}, bf16[256,3072]{1,0:T(8,128)(2,1)S(1)}, u32[]{:S(2)}, u32[]{:S(2)}) %collective-permute-start.35) | collective-permute-done | bytes 1572896 | tf_op jit(solution)/shard_map/ppermute | solution.py:94
  172.6 3.0 %weight_grads.4 = (bf16[2,96,2688]{2,1,0:T(8,128)(2,1)S(1)}, bf16[2,96,2688]{2,1,0:T(8,128)(2,1)S(1)}, bf16[2,96,2688]{2,1,0:T(8,128)(2,1)S(1)}, bf16[2,96,2688]{2,1,0:T(8,128)(2,1)S(1)}) custom-call(s32[20]{0:T(128)S(1)} %stack.118.place, bf16[3,4,96,256]{3,2,1,0:T(8,128)(2,1)S(1)} %copy-done.29, bf16[3,4,96,256]{3,2,1,0:T(8,128)(2,1)S(1)} %copy-done.31, ...), custom_call_target="tpu_custom_call" | custom-call | flops 2113929216 | bytes 5898280 | tf_op jit(solution)/shard_map/weight_grads/pallas_call | solution.py:235
  177.7 12.6 %self_backward.1 = (bf16[256,768]{1,0:T(8,128)(2,1)S(1)}, bf16[256,768]{1,0:T(8,128)(2,1)S(1)}, bf16[320,768]{1,0:T(8,128)(2,1)S(1)}, f32[256,768]{1,0:T(8,128)}, bf16[4,96,128]{2,1,0:T(8,128)(2,1)S(1)}) custom-call(s32[20]{0:T(128)S(1)} %stack.118.place, f32[256,768]{1,0:T(8,128)S(1)} %get-tuple-element.161.grad, ...), custom_call_target="tpu_custom_call" | custom-call | flops 1207959552 | bytes 5250088 | tf_op jit(solution)/shard_map/self_backward/pallas_call | solution.py:235
  193.3 2.6 weight_grads.5
  195.9 4.8 %collective-permute-done.39.refs_1_ = bf16[2,96,2688]{2,1,0:T(8,128)(2,1)S(1)} collective-permute-done((bf16[2,96,2688]{2,1,0:T(8,128)(2,1)S(1)}, bf16[2,96,2688]{2,1,0:T(8,128)(2,1)S(1)}, u32[]{:S(2)}, u32[]{:S(2)}) %collective-permute-start.39) | collective-permute-done | bytes 1032224 | tf_op jit(solution)/shard_map/ppermute | solution.py:94
  207.3 10.8 %collective-permute-done.41 = bf16[96,2688]{1,0:T(8,128)(2,1)S(1)} collective-permute-done((bf16[96,2688]{1,0:T(8,128)(2,1)}, bf16[96,2688]{1,0:T(8,128)(2,1)S(1)}, u32[]{:S(2)}, u32[]{:S(2)}) %collective-permute-start.41) | collective-permute-done | bytes 516128 | tf_op jit(solution)/shard_map/ppermute | solution.py:94
  221.0 5.0 %collective-permute-done.44.refs_3_ = bf16[2,96,1152]{2,1,0:T(8,128)(2,1)} collective-permute-done((bf16[2,96,1152]{2,1,0:T(8,128)(2,1)}, bf16[2,96,1152]{2,1,0:T(8,128)(2,1)}, u32[]{:S(2)}, u32[]{:S(2)}) %collective-permute-start.44) | collective-permute-done | bytes 442400 | tf_op jit(solution)/shard_map/ppermute | solution.py:94
  234.6 9.9 %collective-permute-done.45.kept_far = bf16[2,24,4608]{2,1,0:T(8,128)(2,1)S(1)} collective-permute-done((bf16[2,24,4608]{2,1,0:T(8,128)(2,1)}, bf16[2,24,4608]{2,1,0:T(8,128)(2,1)S(1)}, u32[]{:S(2)}, u32[]{:S(2)}) %collective-permute-start.45) | collective-permute-done | bytes 442400 | tf_op jit(solution)/shard_map/ppermute | solution.py:94
  252.8 3.1 %collective-permute-done.49.far = bf16[1,24,5376]{2,1,0:T(8,128)(2,1)S(1)} collective-permute-done((bf16[1,24,5376]{2,1,0:T(8,128)(2,1)S(1)}, bf16[1,24,5376]{2,1,0:T(8,128)(2,1)S(1)}, u32[]{:S(2)}, u32[]{:S(2)}) %collective-permute-start.49) | collective-permute-done | bytes 258080 | tf_op jit(solution)/shard_map/ppermute | solution.py:905
  258.1 4.8 %collective-permute-done.52.refs_2_ = bf16[24,2432]{1,0:T(8,128)(2,1)S(1)} collective-permute-done((bf16[24,2432]{1,0:T(8,128)(2,1)S(1)}, bf16[24,2432]{1,0:T(8,128)(2,1)S(1)}, u32[]{:S(2)}, u32[]{:S(2)}) %collective-permute-start.52) | collective-permute-done | bytes 116768 | tf_op jit(solution)/shard_map/ppermute | solution.py:88
  (267 shorter events, 103.6 us)
Async XLA Ops:
  7.2 56.1 %all-gather.4.cloned.1.call-start = ((), (), s32[]{:S(2)}) async-start(), calls=%async_computation.1 | async-start | bytes 1843200 | tf_op jit(solution)/shard_map/all_gather | solution.py:1050
  11.1 15.3 %collective-permute-start.3 = (bf16[24,3200]{1,0:T(8,128)(2,1)S(1)}, bf16[24,3200]{1,0:T(8,128)(2,1)S(1)}, u32[]{:S(2)}, u32[]{:S(2)}) collective-permute-start(bf16[24,3200]{1,0:T(8,128)(2,1)S(1)} %concatenate.34), channel_id=1, source_target_pairs={{0,3},{1,0},{2,1},{3,2},{4,7},{5,4},{6,5},{7,6},{8,11},{9,8},{10,9... | collective-permute-start | bytes 460808 | tf_op jit(solution)/shard_map/ppermute | solution.py:88
  27.2 80.1 %all-gather.6.cloned.1.call-start = ((), (), s32[]{:S(2)}) async-start(), calls=%async_computation.3 | async-start | bytes 1474560 | tf_op jit(solution)/shard_map/all_gather | solution.py:1062
  29.5 15.3 %collective-permute-start.7 = (bf16[96,3200]{1,0:T(8,128)(2,1)S(1)}, bf16[96,3200]{1,0:T(8,128)(2,1)S(1)}, u32[]{:S(2)}, u32[]{:S(2)}) collective-permute-start(bf16[96,3200]{1,0:T(8,128)(2,1)S(1)} %bitcast.87), channel_id=1, source_target_pairs={{0,16},{4,20},{8,24},{12,28},{16,0},{20,4},{24,8},{28,12},{1,17},{... | collective-permute-start | bytes 1843208 | tf_op jit(solution)/shard_map/ppermute | solution.py:94
  31.0 13.7 %collective-permute-start.4 = (bf16[96,3200]{1,0:T(8,128)(2,1)S(1)}, bf16[96,3200]{1,0:T(8,128)(2,1)S(1)}, u32[]{:S(2)}, u32[]{:S(2)}) collective-permute-start(bf16[96,3200]{1,0:T(8,128)(2,1)S(1)} %bitcast.88), channel_id=1, source_target_pairs={{0,4},{4,0},{8,12},{12,8},{16,20},{20,16},{24,28},{28,24},{1,5},{5... | collective-permute-start | bytes 1843208 | tf_op jit(solution)/shard_map/ppermute | solution.py:94
  31.1 16.3 %collective-permute-start.5 = (bf16[96,3200]{1,0:T(8,128)(2,1)S(1)}, bf16[96,3200]{1,0:T(8,128)(2,1)S(1)}, u32[]{:S(2)}, u32[]{:S(2)}) collective-permute-start(bf16[96,3200]{1,0:T(8,128)(2,1)S(1)} %bitcast.89), channel_id=1, source_target_pairs={{0,8},{4,12},{8,0},{12,4},{16,24},{20,28},{24,16},{28,20},{1,9},{5... | collective-permute-start | bytes 1843208 | tf_op jit(solution)/shard_map/ppermute | solution.py:94
  50.0 14.7 %collective-permute-start.22 = (bf16[24,1536]{1,0:T(8,128)(2,1)}, bf16[24,1536]{1,0:T(8,128)(2,1)}, u32[]{:S(2)}, u32[]{:S(2)}) collective-permute-start(bf16[24,1536]{1,0:T(8,128)(2,1)} %slice.51), channel_id=1, source_target_pairs={{0,16},{4,20},{8,24},{12,28},{16,0},{20,4},{24,8},{28,12},{1,17},{... | collective-permute-start | bytes 221192 | tf_op jit(solution)/shard_map/ppermute | solution.py:94
  63.3 33.5 %collective-permute-start.16 = (bf16[96,7680]{1,0:T(8,128)(2,1)}, bf16[96,7680]{1,0:T(8,128)(2,1)S(1)}, u32[]{:S(2)}, u32[]{:S(2)}) collective-permute-start(bf16[96,7680]{1,0:T(8,128)(2,1)} %all-gather.4.cloned.1.call-done.refs_0_.refs_6_), channel_id=1, source_target_pairs={{0,16},{4,20},{8,24},{12,28},{16,0},{20,4},{24,8},{28,12},{1,17},{... | collective-permute-start | bytes 4423688 | tf_op jit(solution)/shard_map/ppermute | solution.py:94
  64.8 32.0 %collective-permute-start.15 = (bf16[96,7680]{1,0:T(8,128)(2,1)}, bf16[96,7680]{1,0:T(8,128)(2,1)}, u32[]{:S(2)}, u32[]{:S(2)}) collective-permute-start(bf16[96,7680]{1,0:T(8,128)(2,1)} %all-gather.4.cloned.1.call-done.refs_0_.refs_6_), channel_id=1, source_target_pairs={{0,4},{4,0},{8,12},{12,8},{16,20},{20,16},{24,28},{28,24},{1,5},{5... | collective-permute-start | bytes 4423688 | tf_op jit(solution)/shard_map/ppermute | solution.py:94
  64.8 35.0 %collective-permute-start.14 = (bf16[96,7680]{1,0:T(8,128)(2,1)}, bf16[96,7680]{1,0:T(8,128)(2,1)}, u32[]{:S(2)}, u32[]{:S(2)}) collective-permute-start(bf16[96,7680]{1,0:T(8,128)(2,1)} %all-gather.4.cloned.1.call-done.refs_0_.refs_6_), channel_id=1, source_target_pairs={{0,8},{4,12},{8,0},{12,4},{16,24},{20,28},{24,16},{28,20},{1,9},{5... | collective-permute-start | bytes 4423688 | tf_op jit(solution)/shard_map/ppermute | solution.py:94
  69.5 160.2 %reduce-scatter.2.cloned.1.call-start = ((), (), s32[]{:S(2)}) async-start(), calls=%async_computation.2 | async-start | bytes 4423680 | tf_op jit(solution)/shard_map/reduce_scatter | solution.py:1143
  99.8 16.3 %collective-permute-start.17 = (bf16[96,7680]{1,0:T(8,128)(2,1)}, bf16[96,7680]{1,0:T(8,128)(2,1)}, u32[]{:S(2)}, u32[]{:S(2)}) collective-permute-start(bf16[96,7680]{1,0:T(8,128)(2,1)} %collective-permute-done.14.refs_2_.refs_8_), channel_id=1, source_target_pairs={{0,4},{4,0},{8,12},{12,8},{16,20},{20,16},{24,28},{28,24},{1,5},{5... | collective-permute-start | bytes 4423688 | tf_op jit(solution)/shard_map/ppermute | solution.py:94
  99.8 16.3 %collective-permute-start.18 = (bf16[96,7680]{1,0:T(8,128)(2,1)S(1)}, bf16[96,7680]{1,0:T(8,128)(2,1)}, u32[]{:S(2)}, u32[]{:S(2)}) collective-permute-start(bf16[96,7680]{1,0:T(8,128)(2,1)S(1)} %collective-permute-done.16.refs_4_.refs_10_), channel_id=1, source_target_pairs={{0,4},{4,0},{8,12},{12,8},{16,20},{20,16},{24,28},{28,24},{1,5},{5... | collective-permute-start | bytes 4423688 | tf_op jit(solution)/shard_map/ppermute | solution.py:94
  112.3 16.4 %collective-permute-start.27 = (bf16[384,1536]{1,0:T(8,128)(2,1)}, bf16[384,1536]{1,0:T(8,128)(2,1)}, u32[]{:S(2)}, u32[]{:S(2)}) collective-permute-start(bf16[384,1536]{1,0:T(8,128)(2,1)} %bitcast.44.refs_6_), channel_id=1, source_target_pairs={{0,4},{4,0},{8,12},{12,8},{16,20},{20,16},{24,28},{28,24},{1,5},{5... | collective-permute-start | bytes 3538952 | tf_op jit(solution)/shard_map/ppermute | solution.py:94
  113.2 14.9 %collective-permute-start.30 = (bf16[48,4608]{1,0:T(8,128)(2,1)}, bf16[48,4608]{1,0:T(8,128)(2,1)}, u32[]{:S(2)}, u32[]{:S(2)}) collective-permute-start(bf16[48,4608]{1,0:T(8,128)(2,1)} %slice.42), channel_id=1, source_target_pairs={{0,8},{4,12},{8,0},{12,4},{16,24},{20,28},{24,16},{28,20},{1,9},{5... | collective-permute-start | bytes 1327112 | tf_op jit(solution)/shard_map/ppermute | solution.py:94
  175.6 25.2 %collective-permute-start.39 = (bf16[2,96,2688]{2,1,0:T(8,128)(2,1)S(1)}, bf16[2,96,2688]{2,1,0:T(8,128)(2,1)S(1)}, u32[]{:S(2)}, u32[]{:S(2)}) collective-permute-start(bf16[2,96,2688]{2,1,0:T(8,128)(2,1)S(1)} %get-tuple-element.158), channel_id=1, source_target_pairs={{0,16},{4,20},{8,24},{12,28},{16,0},{20,4},{24,8},{28,12},{1,17},{... | collective-permute-start | bytes 3096584 | tf_op jit(solution)/shard_map/ppermute | solution.py:94
  176.6 24.8 %collective-permute-start.40 = (bf16[2,96,2688]{2,1,0:T(8,128)(2,1)S(1)}, bf16[2,96,2688]{2,1,0:T(8,128)(2,1)S(1)}, u32[]{:S(2)}, u32[]{:S(2)}) collective-permute-start(bf16[2,96,2688]{2,1,0:T(8,128)(2,1)S(1)} %get-tuple-element.160), channel_id=1, source_target_pairs={{0,8},{4,12},{8,0},{12,4},{16,24},{20,28},{24,16},{28,20},{1,9},{5... | collective-permute-start | bytes 3096584 | tf_op jit(solution)/shard_map/ppermute | solution.py:94
  203.2 14.9 %collective-permute-start.41 = (bf16[96,2688]{1,0:T(8,128)(2,1)}, bf16[96,2688]{1,0:T(8,128)(2,1)S(1)}, u32[]{:S(2)}, u32[]{:S(2)}) collective-permute-start(bf16[96,2688]{1,0:T(8,128)(2,1)} %get-tuple-element.179), channel_id=1, source_target_pairs={{0,8},{4,12},{8,0},{12,4},{16,24},{20,28},{24,16},{28,20},{1,9},{5... | collective-permute-start | bytes 1548296 | tf_op jit(solution)/shard_map/ppermute | solution.py:94
  204.2 14.7 %collective-permute-start.42 = (bf16[96,2688]{1,0:T(8,128)(2,1)S(1)}, bf16[96,2688]{1,0:T(8,128)(2,1)S(1)}, u32[]{:S(2)}, u32[]{:S(2)}) collective-permute-start(bf16[96,2688]{1,0:T(8,128)(2,1)S(1)} %get-tuple-element.181), channel_id=1, source_target_pairs={{0,16},{4,20},{8,24},{12,28},{16,0},{20,4},{24,8},{28,12},{1,17},{... | collective-permute-start | bytes 1548296 | tf_op jit(solution)/shard_map/ppermute | solution.py:94
  205.7 21.9 %collective-permute-start.43 = (bf16[2,96,1280]{2,1,0:T(8,128)(2,1)}, bf16[2,96,1280]{2,1,0:T(8,128)(2,1)}, u32[]{:S(2)}, u32[]{:S(2)}) collective-permute-start(bf16[2,96,1280]{2,1,0:T(8,128)(2,1)} %get-tuple-element.174), channel_id=1, source_target_pairs={{0,16},{4,20},{8,24},{12,28},{16,0},{20,4},{24,8},{28,12},{1,17},{... | collective-permute-start | bytes 1474568 | tf_op jit(solution)/shard_map/ppermute | solution.py:94
  206.2 19.8 %collective-permute-start.44 = (bf16[2,96,1152]{2,1,0:T(8,128)(2,1)}, bf16[2,96,1152]{2,1,0:T(8,128)(2,1)}, u32[]{:S(2)}, u32[]{:S(2)}) collective-permute-start(bf16[2,96,1152]{2,1,0:T(8,128)(2,1)} %get-tuple-element.176), channel_id=1, source_target_pairs={{0,8},{4,12},{8,0},{12,4},{16,24},{20,28},{24,16},{28,20},{1,9},{5... | collective-permute-start | bytes 1327112 | tf_op jit(solution)/shard_map/ppermute | solution.py:94
  220.4 24.1 %collective-permute-start.46 = (bf16[2,24,5376]{2,1,0:T(8,128)(2,1)}, bf16[2,24,5376]{2,1,0:T(8,128)(2,1)S(1)}, u32[]{:S(2)}, u32[]{:S(2)}) collective-permute-start(bf16[2,24,5376]{2,1,0:T(8,128)(2,1)} %get-tuple-element.190), channel_id=1, source_target_pairs={{0,1},{1,0},{2,3},{3,2},{4,5},{5,4},{6,7},{7,6},{8,9},{9,8},{10,11... | collective-permute-start | bytes 1548296 | tf_op jit(solution)/shard_map/ppermute | solution.py:905
  233.1 14.2 %collective-permute-start.48 = (bf16[96,1152]{1,0:T(8,128)(2,1)}, bf16[96,1152]{1,0:T(8,128)(2,1)S(1)}, u32[]{:S(2)}, u32[]{:S(2)}) collective-permute-start(bf16[96,1152]{1,0:T(8,128)(2,1)} %get-tuple-element.187), channel_id=1, source_target_pairs={{0,16},{4,20},{8,24},{12,28},{16,0},{20,4},{24,8},{28,12},{1,17},{... | collective-permute-start | bytes 663560 | tf_op jit(solution)/shard_map/ppermute | solution.py:94
  248.9 14.0 %collective-permute-start.52 = (bf16[24,2432]{1,0:T(8,128)(2,1)S(1)}, bf16[24,2432]{1,0:T(8,128)(2,1)S(1)}, u32[]{:S(2)}, u32[]{:S(2)}) collective-permute-start(bf16[24,2432]{1,0:T(8,128)(2,1)S(1)} %get-tuple-element.201), channel_id=1, source_target_pairs={{0,2},{1,3},{2,0},{3,1},{4,6},{5,7},{6,4},{7,5},{8,10},{9,11},{10,... | collective-permute-start | bytes 350216 | tf_op jit(solution)/shard_map/ppermute | solution.py:88
  (91 other events, 913.5 us)
Sparse Core Ops, SparseCore 0:
  27.3 35.9 all-gather.3
  69.6 27.0 all-gather.5
  154.0 64.3 reduce-scatter.1

commit v3 on v2

--- a/solution.py
+++ b/solution.py
@@ -23,7 +23,7 @@
 FIRST_AT = 4
 ORDER_AT = 12
 EARLY = 0.5
-EARLY_GRAD = 0.5
+EARLY_GRAD = 0.25
 
 
 def bucket_edges(bucket_count, far_reach):
@@ -502,6 +502,82 @@
         [((width, ff), LOW), ((ff, width), LOW)],
         weights.sems(),
         weights=[weights],
+    )
+
+
+def fetching(kernel, arrays):
+    count = len(arrays)
+
+    def fetched(*refs):
+        sources, outs, refs = refs[:count], refs[count : -count - 1], refs[-count - 1 :]
+        for wait in fetch(sources, refs[:-1], refs[-1]):
+            wait()
+        kernel(*refs[:-1], *outs)
+
+    scratch = [pltpu.VMEM(array.shape, array.dtype) for array in arrays]
+    return fetched, scratch + [pltpu.SemaphoreType.DMA((count,))]
+
+
+def pack_first(squares, gains, table, cut):
+    share, width = squares[0].shape
+    table_rows, heads = table.shape
+
+    def kernel(query, key, value, output, *refs):
+        gains, (table, out, lanes) = refs[:3], refs[3:]
+        lanes[...] = jnp.zeros_like(lanes)
+        rows = jnp.concatenate([gain[...].astype(F32) for gain in gains] + [jnp.zeros((5, share), F32)], axis=0)
+        lanes[:, :8] = rows.T
+        for group in range(-(-table_rows // share)):
+            part = table[...].astype(F32)[group * share : (group + 1) * share]
+            at = TABLE_LANE + group * heads
+            lanes[: part.shape[0], at : at + heads] = part
+        out[:, :width] = query[...]
+        out[:, width : 2 * width] = key[...]
+        out[:, 2 * width : cut] = lanes[...].astype(LOW)
+        out[:, cut : cut + width] = value[...]
+        out[:, cut + width :] = output[...]
+
+    arrays = [*squares, *[gain.reshape(1, share) for gain in gains], table]
+    fetched, scratch = fetching(kernel, arrays)
+    return run(
+        "pack_first",
+        fetched,
+        [(array, pltpu.HBM) for array in arrays],
+        [((share, cut + 2 * width), LOW)],
+        [pltpu.VMEM((share, LANES), F32), *scratch],
+    )[0]
+
+
+def pack_rest(squares, hidden_in, hidden_out, order, early_cols):
+    share, width = squares[0].shape
+    ff = hidden_in.shape[1]
+    folds = ff // width
+    late = ff - early_cols
+
+    def kernel(*refs):
+        squares, (h_in, h_out, order, rest, early) = refs[:4], refs[4:]
+        for start in range(0, ff, CHUNK):
+            part = dot(h_in[:, start : start + CHUNK], order[...]).astype(LOW)
+            if start < early_cols:
+                early[:, start : start + CHUNK] = part
+            else:
+                at = 4 * width + start - early_cols
+                rest[:, at : at + CHUNK] = part
+        for n, square in enumerate(squares):
+            rest[:, n * width : (n + 1) * width] = square[...]
+        rows = h_out[...].astype(F32)
+        for n in range(folds):
+            at = 4 * width + late + n * width
+            rest[:, at : at + width] = rows[n * share : (n + 1) * share].astype(LOW)
+
+    arrays = [*squares, hidden_in, hidden_out, order]
+    fetched, scratch = fetching(kernel, arrays)
+    return run(
+        "pack_rest",
+        fetched,
+        [(array, pltpu.HBM) for array in arrays],
+        [((share, 4 * width + late + ff), LOW, None), ((share, early_cols), LOW, None)],
+        scratch,
     )
 
 
@@ -825,20 +901,26 @@
     counts = (sizes["x"], sizes["y"])
 
     def kernel(place, *refs):
-        halves = (refs[: len(firsts)], refs[len(firsts) : len(firsts) + len(seconds)])
-        outs = refs[len(firsts) + len(seconds) :]
-        outs = (outs[: counts[0]], outs[counts[0] :])
+        refs = list(refs)
+        halves = [[[refs.pop(0) for _ in parts] for parts in groups] for groups in (firsts, seconds)]
+        outs = (refs[: counts[0]], refs[counts[0] :])
         for half in range(2):
             here = place[1 - half]
             for step in range(counts[half]):
                 index = (here + step) % counts[half]
-                total = halves[half][0][index].astype(F32)
-                for part in halves[half][1:]:
-                    total = total + part[index].astype(F32)
-                outs[half][step][...] = total.astype(LOW)
-
-    outputs = [(firsts[0].shape[1:], LOW)] * counts[0] + [(seconds[0].shape[1:], LOW)] * counts[1]
-    return run("add_stage", kernel, [(place, pltpu.SMEM)] + vmem(*firsts, *seconds), outputs)
+                at = 0
+                for parts in halves[half]:
+                    total = parts[0][index].astype(F32)
+                    for part in parts[1:]:
+                        total = total + part[index].astype(F32)
+                    outs[half][step][:, at : at + total.shape[1]] = total.astype(LOW)
+                    at += total.shape[1]
+
+    outputs = []
+    for groups, count in zip((firsts, seconds), counts):
+        outputs += [((groups[0][0].shape[1], sum(parts[0].shape[2] for parts in groups)), LOW)] * count
+    arrays = [part for groups in (firsts, seconds) for parts in groups for part in parts]
+    return run("add_stage", kernel, [(place, pltpu.SMEM)] + vmem(*arrays), outputs)
 
 
 def add_last(place, halves):
@@ -1023,42 +1105,46 @@
 
     hot = jnp.asarray(table_hot(rows, nz, share, table_rows)).astype(LOW)
     groups = hot.shape[0]
-    table = jnp.pad(bias_table, ((0, groups * share - table_rows), (0, 0)))
-    table = jnp.transpose(table.reshape(groups, share, heads), (1, 0, 2)).reshape(share, groups * heads)
-    extra = jnp.concatenate(
-        [
-            self_gain[:, None],
-            cross_gain[:, None],
-            hidden_gain[:, None],
-            jnp.zeros((share, TABLE_LANE - 3), LOW),
-            table,
-            jnp.zeros((share, LANES - TABLE_LANE - groups * heads), LOW),
-        ],
-        axis=1,
-    )
-    self_own = jnp.concatenate([self_query, self_key, extra, self_value, self_output], axis=1)
+    folds = ff // width
+    order = hidden_order(nz, share, folds)
+    early_cols = int(ff * EARLY) // LANES * LANES if pieces else 0
+    cross_squares = (cross_query, cross_output, cross_key, cross_value)
+    if pieces:
+        self_own = pack_first(
+            (self_query, self_key, self_value, self_output), (self_gain, cross_gain, hidden_gain), bias_table, cut
+        )
+        rest, in_own = pack_rest(cross_squares, hidden_in, hidden_out, order, early_cols)
+    else:
+        table = jnp.pad(bias_table, ((0, groups * share - table_rows), (0, 0)))
+        table = jnp.transpose(table.reshape(groups, share, heads), (1, 0, 2)).reshape(share, groups * heads)
+        extra = jnp.concatenate(
+            [
+                self_gain[:, None],
+                cross_gain[:, None],
+                hidden_gain[:, None],
+                jnp.zeros((share, TABLE_LANE - 3), LOW),
+                table,
+                jnp.zeros((share, LANES - TABLE_LANE - groups * heads), LOW),
+            ],
+            axis=1,
+        )
+        self_own = jnp.concatenate([self_query, self_key, extra, self_value, self_output], axis=1)
+        wide_out = jnp.transpose(hidden_out.reshape(folds, share, width), (1, 0, 2)).reshape(share, ff)
+        rest = jnp.concatenate([*cross_squares, reorder(hidden_in, order, NN, LOW), wide_out], axis=1)
     self_others = received(self_own, "z")
     self_z = in_order(self_own, self_others, "z", 0).reshape(block, -1)
-    folds = ff // width
-    order = hidden_order(nz, share, folds)
-    wide_out = jnp.transpose(hidden_out.reshape(folds, share, width), (1, 0, 2)).reshape(share, ff)
-    hidden_own = reorder(hidden_in, order, NN, LOW)
-    early_cols = int(ff * EARLY) // LANES * LANES if pieces else 0
-    rest = jnp.concatenate(
-        [cross_query, cross_output, cross_key, cross_value, hidden_own[:, early_cols:], wide_out], axis=1
-    )
-    rest = lax.all_gather(after(rest, self_others[0]), "narrow", axis=0, tiled=True)
+    rest = after(rest, self_others[0])
+    rest = lax.all_gather(rest, "narrow", axis=0, tiled=True)
 
     seg_ids = segment_ids(doc_lengths[0], rows)
     mem_ids = segment_ids(mem_lengths[0], mem_rows)
     if pieces:
-        in_own = hidden_own[:, :early_cols]
         in_x, in_y = shifted(in_own, "x", 1), shifted(in_own, "y", 1)
         in_xy = shifted(in_x, "y", 1)
         in_all = in_order(
             in_order(in_own, [in_x], "x", 0), [in_order(in_y, [in_xy], "x", 0)], "y", 0
         ).reshape(4, share, early_cols)
-        near, twins, corner = gather_pieces(self_z)
+        near, twins, corner = gather_pieces(after(self_z, in_xy))
         in_all = lax.all_gather(after(in_all, rest, *corner), "narrow", axis=0, tiled=False)
         w_self = Weights(
             pairs(near, twins) + with_twins(corner),
@@ -1127,27 +1213,30 @@
     side = width // 2
     early_grads = int(ff * EARLY_GRAD) // LANES * LANES if pieces else 0
     late = (ff - early_grads) // 2
+    ff_cols = late + (0 if pieces else folds * side)
+    ff_sections = [((0, 0, 0, block), 0, early_grads + n * late, late, n, 0) for n in range(2)]
+    straight = []
     if pieces:
-        in_early = weight_grads(
-            place,
-            [(h_keep[None], h_far[None])],
-            [(gu, gu_far), (out_grad, og_far)],
-            [],
-            (0, 0),
-            straight=[
-                ((0, 0, 0, block), 0, 0, early_grads, 2, 0),
-                ((0, 0, block, ff_block), 1, 0, width, 2, early_grads),
-            ],
-        )[0]
-        grad = after(grad, in_early)
+        straight = [
+            ((0, 0, 0, block), 0, 0, early_grads, 2, 0),
+            ((0, 0, block, ff_block), 1, 0, width, 2, early_grads),
+        ]
+    else:
+        ff_sections += [((0, 0, block, ff_block), 1, n * side, side, n, late) for n in range(2)]
+    ff_parts = weight_grads(
+        place,
+        [(h_keep[None], h_far[None])],
+        [(gu, gu_far), (out_grad, og_far)],
+        ff_sections,
+        (ff_cols, ff_cols),
+        straight=straight,
+    )
+    if pieces:
+        *ff_parts, in_early = ff_parts
         in_early = lax.psum_scatter(in_early, "narrow", scatter_dimension=0, tiled=True)
-        out_sections = []
-    else:
-        out_sections = [
-            ((2, 0, block, ff_block), 3, 0, side, 0, 2 * width + side + late),
-            ((2, 0, block, ff_block), 3, side, side, 1, 2 * width + side + late),
-        ]
-    cross_cols = 2 * width + side + late + (folds * side if out_sections else 0)
+    grad = after(grad, *ff_parts)
+    ff_first, ff_second = sent(ff_parts[:ny], "y"), sent(ff_parts[ny:], "x")
+    cross_cols = 2 * width + side + ff_cols
 
     branch_far = swapped(branch)
     cross_grads, memory_grad, grad, cross_gain_part = cross_backward(
@@ -1155,19 +1244,16 @@
     )
     cross_parts = weight_grads(
         place,
-        [(c_keep, c_far), (s_keep, s_far), (h_keep[None], h_far[None])],
-        [(cross_grads, swapped(cross_grads)), (branch, branch_far), (gu, gu_far), (out_grad, og_far)],
+        [(c_keep, c_far), (s_keep, s_far)],
+        [(cross_grads, swapped(after(cross_grads, *ff_first, *ff_second))), (branch, branch_far)],
         [
             ((0, 0, 0, block), 0, 0, width, 0, 0),
             ((0, 1, 0, block), 1, 0, width, 0, width),
             ((1, 1, 0, block), 0, 3 * width, side, 0, 2 * width),
-            ((2, 0, 0, block), 2, early_grads, late, 0, 2 * width + side),
             ((0, 2, 0, block), 0, width, 2 * width, 1, 0),
             ((1, 1, 0, block), 0, 3 * width + side, side, 1, 2 * width),
-            ((2, 0, 0, block), 2, early_grads + late, late, 1, 2 * width + side),
-            *out_sections,
         ],
-        (cross_cols, cross_cols),
+        (2 * width + side, 2 * width + side),
     )
     cross_first, cross_second = cross_parts[:ny], cross_parts[ny:]
     cross_first, cross_second = sent(cross_first, "y"), sent(cross_second, "x")
@@ -1193,16 +1279,16 @@
     self_first, self_second = self_parts[:ny], self_parts[ny:]
     self_first, self_second = sent(self_first, "y"), sent(self_second, "x")
     cross_first = [after(cross_first[0], *self_parts)] + cross_first[1:]
-    cross_parts = add_stage(place, cross_first, cross_second)
+    cross_parts = add_stage(place, [cross_first, ff_first], [cross_second, ff_second])
     cross_first, cross_second = cross_parts[:nx], cross_parts[nx:]
     cross_first, cross_second = sent(cross_first, "x"), sent(cross_second, "y")
     cross_parts = halve(place, [by_blocks(cross_first), by_blocks(cross_second)], 2, True)
     self_first = [after(self_first[0], cross_parts[0])] + self_first[1:]
-    self_parts = add_stage(place, self_first, self_second)
+    self_parts = add_stage(place, [self_first], [self_second])
     self_first, self_second = self_parts[:nx], self_parts[nx:]
     self_first, self_second = sent(self_first, "x"), sent(self_second, "y")
     if pieces:
-        in_early = after(in_early, *self_parts).reshape(ny, nx, share, early_grads + folds * width)
+        in_early = after(in_early, cross_parts[0]).reshape(ny, nx, share, early_grads + folds * width)
         in_early = scatter_along([in_early], "y")
     count = 2
     while count < nz:

time: 272 us -> 259 us (0.952)
  local copies, waits for them, and re-layouts: 32.3 us -> 21.7 us
  waiting for transfers between devices: 97.7 us -> 93.5 us
  starting transfers between devices: 43.2 us -> 46.6 us
  other arithmetic: 4.9 us -> 2.13 us
    unnamed x121 -> x84, local copies, waits for them, and re-layouts: 15.4 us -> 7.53 us
    ppermute x46 -> x48, waiting for transfers between devices: 84.8 us -> 77 us  [shifted(): return lax.ppermute(array, 'wide', pairs)]
    ppermute x6, waiting for transfers between devices: 6.74 us -> 12.8 us  [shifted(): lax.ppermute(array, 'narrow', [(i, (i + step) % count) for i in range(cou...]
    ppermute x46 -> x48, starting transfers between devices: 30.8 us -> 34.5 us  [shifted(): return lax.ppermute(array, 'wide', pairs)]
    pallas_call x18 -> x19, Pallas kernels: 78.9 us -> 80.2 us  [run(): pl.pallas_call(kernel, name=name, in_specs=[pl.BlockSpec(memory_space=spa...]
  transfers between devices with their start and end apart: 57 -> 59, of which waited for: 28 -> 27; matrix products, arithmetic and copies ran while one was open for 6% -> 6% of each run, Pallas kernels for 24% -> 26%
where the time goes in v3:
time: 259 us; the launch traced here: 258 us
  waiting for transfers between devices  93.5 us (36%)
  Pallas kernels  80.2 us (31%)
  starting transfers between devices  46.6 us (18%)
  local copies, waits for them, and re-layouts  21.7 us (8%)
  between operations  14.4 us (6%)
    pallas_call x19, Pallas kernels, run(): pl.pallas_call(kernel, name=name, in_specs=[pl.BlockSpec(memory_space=spa...  80.2 us
    ppermute x48, waiting for transfers between devices, shifted(): return lax.ppermute(array, 'wide', pairs)  77 us
    ppermute x48, starting transfers between devices, shifted(): return lax.ppermute(array, 'wide', pairs)  34.5 us
    ppermute x6, waiting for transfers between devices, shifted(): lax.ppermute(array, 'narrow', [(i, (i + step) % count) for i in range(cou...  12.8 us
    ppermute x6, starting transfers between devices, shifted(): lax.ppermute(array, 'narrow', [(i, (i + step) % count) for i in range(cou...  10.3 us
    unnamed x84, local copies, waits for them, and re-layouts  7.53 us
  transfers between devices with their start and end apart: 59, of which 27 were waited for; matrix products, arithmetic and copies ran while one was open for 6% of the time, Pallas kernels for 26%

profile of v3, /device:TPU:0, one launch (start us, length us, event | category | flops | bytes accessed | tf_op | source)
XLA Modules:
  0.0 258.5 jit_solution(16130185619120212282)
XLA Ops:
  8.2 5.1 %collective-permute-start.3 = (bf16[24,3200]{1,0:T(8,128)(2,1)S(1)}, bf16[24,3200]{1,0:T(8,128)(2,1)S(1)}, u32[]{:S(2)}, u32[]{:S(2)}) collective-permute-start(bf16[24,3200]{1,0:T(8,128)(2,1)S(1)} %pack_first.1), channel_id=1, source_target_pairs={{0,3},{1,0},{2,1},{3,2},{4,7},{5,4},{6,5},{7,6},{8,11},{9,8},{10,9... | collective-permute-start | bytes 460808 | tf_op jit(solution)/shard_map/ppermute | solution.py:88
  14.4 2.4 pack_rest.1
  18.4 2.9 %collective-permute-done.4 = bf16[24,1536]{1,0:T(8,128)(2,1)S(1)} collective-permute-done((bf16[24,1536]{1,0:T(8,128)(2,1)S(1)}, bf16[24,1536]{1,0:T(8,128)(2,1)S(1)}, u32[]{:S(2)}, u32[]{:S(2)}) %collective-permute-start.4) | collective-permute-done | bytes 73760 | tf_op jit(solution)/shard_map/ppermute | solution.py:94
  22.8 3.5 %collective-permute-done.2 = bf16[24,3200]{1,0:T(8,128)(2,1)S(1)} collective-permute-done((bf16[24,3200]{1,0:T(8,128)(2,1)S(1)}, bf16[24,3200]{1,0:T(8,128)(2,1)S(1)}, u32[]{:S(2)}, u32[]{:S(2)}) %collective-permute-start.2) | collective-permute-done | bytes 153632 | tf_op jit(solution)/shard_map/ppermute | solution.py:88
  29.7 12.2 %collective-permute-done.9.refs_4_ = bf16[96,3200]{1,0:T(8,128)(2,1)S(1)} collective-permute-done((bf16[96,3200]{1,0:T(8,128)(2,1)S(1)}, bf16[96,3200]{1,0:T(8,128)(2,1)S(1)}, u32[]{:S(2)}, u32[]{:S(2)}) %collective-permute-start.9) | collective-permute-done | bytes 614432 | tf_op jit(solution)/shard_map/ppermute | solution.py:94
  41.9 2.7 %collective-permute-done.7.refs_2_ = bf16[96,3200]{1,0:T(8,128)(2,1)} collective-permute-done((bf16[96,3200]{1,0:T(8,128)(2,1)S(1)}, bf16[96,3200]{1,0:T(8,128)(2,1)}, u32[]{:S(2)}, u32[]{:S(2)}) %collective-permute-start.7) | collective-permute-done | bytes 614432 | tf_op jit(solution)/shard_map/ppermute | solution.py:94
  49.7 5.9 %collective-permute-done.13.refs_8_ = bf16[48,3200]{1,0:T(8,128)(2,1)S(1)} collective-permute-done((bf16[48,3200]{1,0:T(8,128)(2,1)S(1)}, bf16[48,3200]{1,0:T(8,128)(2,1)S(1)}, u32[]{:S(2)}, u32[]{:S(2)}) %collective-permute-start.13) | collective-permute-done | bytes 307232 | tf_op jit(solution)/shard_map/ppermute | solution.py:94
  63.9 9.5 %self_forward.1 = (bf16[256,1536]{1,0:T(8,128)(2,1)S(1)}, bf16[256,768]{1,0:T(8,128)(2,1)S(1)}, bf16[12,256,256]{2,1,0:T(8,128)(2,1)S(1)}, f32[256,768]{1,0:T(8,...) custom-call(s32[20]{0:T(128)S(1)} %stack.118.place, ...), custom_call_target="tpu_custom_call" | custom-call | flops 1207959552 | bytes 2680360 | tf_op jit(solution)/shard_map/self_forward/pallas_call | solution.py:235
  78.0 13.5 %collective-permute-done.18.refs_4_.refs_10_ = bf16[96,7680]{1,0:T(8,128)(2,1)} collective-permute-done((bf16[96,7680]{1,0:T(8,128)(2,1)}, bf16[96,7680]{1,0:T(8,128)(2,1)}, u32[]{:S(2)}, u32[]{:S(2)}) %collective-permute-start.18) | collective-permute-done | bytes 1474592 | tf_op jit(solution)/shard_map/ppermute | solution.py:94
  91.5 2.9 %collective-permute-done.16.refs_2_.refs_8_ = bf16[96,7680]{1,0:T(8,128)(2,1)} collective-permute-done((bf16[96,7680]{1,0:T(8,128)(2,1)}, bf16[96,7680]{1,0:T(8,128)(2,1)}, u32[]{:S(2)}, u32[]{:S(2)}) %collective-permute-start.16) | collective-permute-done | bytes 1474592 | tf_op jit(solution)/shard_map/ppermute | solution.py:94
  113.0 9.4 %cross_forward.1 = (bf16[256,768]{1,0:T(8,128)(2,1)S(1)}, bf16[256,1536]{1,0:T(8,128)(2,1)S(1)}, bf16[12,256,256]{2,1,0:T(8,128)(2,1)S(1)}, f32[256,768]{1,0:T(8...) custom-call(s32[20]{0:T(128)S(1)} %stack.118.place, ...), custom_call_target="tpu_custom_call" | custom-call | flops 1207959552 | bytes 5616680 | tf_op jit(solution)/shard_map/cross_forward/pallas_call | solution.py:235
  123.1 4.2 %hidden_early.1 = (bf16[768,3072]{1,0:T(8,128)(2,1)S(1)}, bf16[3072,768]{1,0:T(8,128)(2,1)S(1)}) custom-call(s32[20]{0:T(128)S(1)} %stack.118.place, bf16[96,7680]{1,0:T(8,128)(2,1)} %all-gather.4.cloned.1.call-done.refs_0_.refs_6_, bf16[96,7680]{1,0:T(8,128)(2,1)} %collective-permute-done.17.refs_1_.refs_7_, ...), custom_call_target="tpu_custom_call" | custom-call | bytes 5603368 | tf_op jit(solution)/shard_map/hidden_early/pallas_call | solution.py:235
  129.1 7.5 %hidden_first.1 = (bf16[256,3072]{1,0:T(8,128)(2,1)S(1)}, bf16[256,3072]{1,0:T(8,128)(2,1)S(1)}, bf16[4,480,256]{2,1,0:T(8,128)(2,1)S(1)}, bf16[4,480,256]{2,1,0...) custom-call(s32[20]{0:T(128)S(1)} %stack.118.place, ...), custom_call_target="tpu_custom_call", output_to_operand_aliasing={{4}: (4, {}), {5}: (5, {})} | custom-call | flops 2415919104 | bytes 6205480 | tf_op jit(solution)/shard_map/hidden_first/pallas_call | solution.py:235
  137.2 3.6 %hidden_second.1 = (bf16[256,768]{1,0:T(8,128)(2,1)}, f32[256,768]{1,0:T(8,128)S(1)}, bf16[256,768]{1,0:T(8,128)(2,1)S(1)}, f32[1,768]{1,0:T(1,128)S(1)}) custom-call(f32[256,768]{1,0:T(8,128)S(1)} %get-tuple-element.144.x, bf16[256,768]{1,0:T(8,128)(2,1)S(1)} %copy-done.1, f32[8,768]{1,0:T(8,128)S(1)} %get-tuple-element.137.gains, ...), custom_call_target="tpu_custom_call" | custom-call | flops 2415919104 | bytes 6893568 | tf_op jit(solution)/shard_map/hidden_second/pallas_call | solution.py:235
  141.6 4.6 %weight_grads.3 = (bf16[2,96,1152]{2,1,0:T(8,128)(2,1)S(1)}, bf16[2,96,1152]{2,1,0:T(8,128)(2,1)S(1)}, bf16[2,96,1152]{2,1,0:T(8,128)(2,1)S(1)}, bf16[2,96,1152]...) custom-call(s32[20]{0:T(128)S(1)} %stack.118.place, bf16[1,4,480,256]{3,2,1,0:T(8,128)(2,1)S(1)} %bitcast.79, ...), custom_call_target="tpu_custom_call" | custom-call | flops 2415919104 | bytes 2949160 | tf_op jit(solution)/shard_map/weight_grads/pallas_call | solution.py:235
  152.0 11.8 %cross_backward.1 = (bf16[256,3072]{1,0:T(8,128)(2,1)S(1)}, f32[256,768]{1,0:T(8,128)}, f32[256,768]{1,0:T(8,128)S(1)}, f32[1,768]{1,0:T(1,128)S(1)}) custom-call(s32[20]{0:T(128)S(1)} %stack.118.place, f32[8,768]{1,0:T(8,128)S(1)} %get-tuple-element.137.gains, bf16[256,768]{1,0:T(8,128)(2,1)} %copy-done.5, bf16[256,1536]{1,0:T(8,128)(2,1)} %copy-done.8, ...), custom_call_target="tpu_custom_call" | custom-call | flops 1207959552 | bytes 7385128 | tf_op jit(solution)/shard_map/cross_backward/pallas_call | solution.py:235
  163.9 3.4 %collective-permute-done.37.refs_5_ = bf16[256,3072]{1,0:T(8,128)(2,1)S(1)} collective-permute-done((bf16[256,3072]{1,0:T(8,128)(2,1)S(1)}, bf16[256,3072]{1,0:T(8,128)(2,1)S(1)}, u32[]{:S(2)}, u32[]{:S(2)}) %collective-permute-start.37) | collective-permute-done | bytes 1572896 | tf_op jit(solution)/shard_map/ppermute | solution.py:94
  171.4 12.7 %self_backward.1 = (bf16[256,768]{1,0:T(8,128)(2,1)S(1)}, bf16[256,768]{1,0:T(8,128)(2,1)S(1)}, bf16[320,768]{1,0:T(8,128)(2,1)S(1)}, f32[256,768]{1,0:T(8,128)}, bf16[4,96,128]{2,1,0:T(8,128)(2,1)S(1)}) custom-call(s32[20]{0:T(128)S(1)} %stack.118.place, f32[256,768]{1,0:T(8,128)S(1)} %get-tuple-element.178.grad, ...), custom_call_target="tpu_custom_call" | custom-call | flops 1207959552 | bytes 5250088 | tf_op jit(solution)/shard_map/self_backward/pallas_call | solution.py:235
  195.1 12.3 %collective-permute-done.43 = bf16[96,3072]{1,0:T(8,128)(2,1)S(1)} collective-permute-done((bf16[96,3072]{1,0:T(8,128)(2,1)}, bf16[96,3072]{1,0:T(8,128)(2,1)S(1)}, u32[]{:S(2)}, u32[]{:S(2)}) %collective-permute-start.43) | collective-permute-done | bytes 589856 | tf_op jit(solution)/shard_map/ppermute | solution.py:94
  213.3 2.9 %collective-permute-done.46.refs_3_ = bf16[2,96,1152]{2,1,0:T(8,128)(2,1)} collective-permute-done((bf16[2,96,1152]{2,1,0:T(8,128)(2,1)}, bf16[2,96,1152]{2,1,0:T(8,128)(2,1)}, u32[]{:S(2)}, u32[]{:S(2)}) %collective-permute-start.46) | collective-permute-done | bytes 442400 | tf_op jit(solution)/shard_map/ppermute | solution.py:94
  216.2 3.3 %collective-permute-done.45.refs_1_ = bf16[2,96,1280]{2,1,0:T(8,128)(2,1)} collective-permute-done((bf16[2,96,1280]{2,1,0:T(8,128)(2,1)}, bf16[2,96,1280]{2,1,0:T(8,128)(2,1)}, u32[]{:S(2)}, u32[]{:S(2)}) %collective-permute-start.45) | collective-permute-done | bytes 491552 | tf_op jit(solution)/shard_map/ppermute | solution.py:94
  222.7 4.6 %collective-permute-done.47.kept_far = bf16[2,24,3840]{2,1,0:T(8,128)(2,1)S(1)} collective-permute-done((bf16[2,24,3840]{2,1,0:T(8,128)(2,1)S(1)}, bf16[2,24,3840]{2,1,0:T(8,128)(2,1)S(1)}, u32[]{:S(2)}, u32[]{:S(2)}) %collective-permute-start.47) | collective-permute-done | bytes 368672 | tf_op jit(solution)/shard_map/ppermute | solution.py:94
  235.7 2.6 %collective-permute-done.51.far = bf16[1,24,6144]{2,1,0:T(8,128)(2,1)S(1)} collective-permute-done((bf16[1,24,6144]{2,1,0:T(8,128)(2,1)S(1)}, bf16[1,24,6144]{2,1,0:T(8,128)(2,1)S(1)}, u32[]{:S(2)}, u32[]{:S(2)}) %collective-permute-start.51) | collective-permute-done | bytes 294944 | tf_op jit(solution)/shard_map/ppermute | solution.py:987
  240.8 9.1 %collective-permute-done.54.refs_2_ = bf16[24,2432]{1,0:T(8,128)(2,1)S(1)} collective-permute-done((bf16[24,2432]{1,0:T(8,128)(2,1)S(1)}, bf16[24,2432]{1,0:T(8,128)(2,1)S(1)}, u32[]{:S(2)}, u32[]{:S(2)}) %collective-permute-start.54) | collective-permute-done | bytes 116768 | tf_op jit(solution)/shard_map/ppermute | solution.py:88
  (225 shorter events, 91.4 us)
Async XLA Ops:
  7.2 50.7 %all-gather.4.cloned.1.call-start = ((), (), s32[]{:S(2)}) async-start(), calls=%async_computation.1 | async-start | bytes 1843200 | tf_op jit(solution)/shard_map/all_gather | solution.py:1137
  8.2 14.5 %collective-permute-start.3 = (bf16[24,3200]{1,0:T(8,128)(2,1)S(1)}, bf16[24,3200]{1,0:T(8,128)(2,1)S(1)}, u32[]{:S(2)}, u32[]{:S(2)}) collective-permute-start(bf16[24,3200]{1,0:T(8,128)(2,1)S(1)} %pack_first.1), channel_id=1, source_target_pairs={{0,3},{1,0},{2,1},{3,2},{4,7},{5,4},{6,5},{7,6},{8,11},{9,8},{10,9... | collective-permute-start | bytes 460808 | tf_op jit(solution)/shard_map/ppermute | solution.py:88
  22.8 81.2 %all-gather.6.cloned.1.call-start = ((), (), s32[]{:S(2)}) async-start(), calls=%async_computation.3 | async-start | bytes 1474560 | tf_op jit(solution)/shard_map/all_gather | solution.py:1148
  26.6 15.3 %collective-permute-start.9 = (bf16[96,3200]{1,0:T(8,128)(2,1)S(1)}, bf16[96,3200]{1,0:T(8,128)(2,1)S(1)}, u32[]{:S(2)}, u32[]{:S(2)}) collective-permute-start(bf16[96,3200]{1,0:T(8,128)(2,1)S(1)} %bitcast.81), channel_id=1, source_target_pairs={{0,16},{4,20},{8,24},{12,28},{16,0},{20,4},{24,8},{28,12},{1,17},{... | collective-permute-start | bytes 1843208 | tf_op jit(solution)/shard_map/ppermute | solution.py:94
  28.2 16.4 %collective-permute-start.7 = (bf16[96,3200]{1,0:T(8,128)(2,1)S(1)}, bf16[96,3200]{1,0:T(8,128)(2,1)}, u32[]{:S(2)}, u32[]{:S(2)}) collective-permute-start(bf16[96,3200]{1,0:T(8,128)(2,1)S(1)} %bitcast.83), channel_id=1, source_target_pairs={{0,8},{4,12},{8,0},{12,4},{16,24},{20,28},{24,16},{28,20},{1,9},{5... | collective-permute-start | bytes 1843208 | tf_op jit(solution)/shard_map/ppermute | solution.py:94
  45.1 15.8 %collective-permute-start.22 = (bf16[24,1536]{1,0:T(8,128)(2,1)S(1)}, bf16[24,1536]{1,0:T(8,128)(2,1)S(1)}, u32[]{:S(2)}, u32[]{:S(2)}) collective-permute-start(bf16[24,1536]{1,0:T(8,128)(2,1)S(1)} %get-tuple-element.125), channel_id=1, source_target_pairs={{0,16},{4,20},{8,24},{12,28},{16,0},{20,4},{24,8},{28,12},{1,17},{... | collective-permute-start | bytes 221192 | tf_op jit(solution)/shard_map/ppermute | solution.py:94
  57.9 33.6 %collective-permute-start.18 = (bf16[96,7680]{1,0:T(8,128)(2,1)}, bf16[96,7680]{1,0:T(8,128)(2,1)}, u32[]{:S(2)}, u32[]{:S(2)}) collective-permute-start(bf16[96,7680]{1,0:T(8,128)(2,1)} %all-gather.4.cloned.1.call-done.refs_0_.refs_6_), channel_id=1, source_target_pairs={{0,16},{4,20},{8,24},{12,28},{16,0},{20,4},{24,8},{28,12},{1,17},{... | collective-permute-start | bytes 4423688 | tf_op jit(solution)/shard_map/ppermute | solution.py:94
  59.4 32.1 %collective-permute-start.17 = (bf16[96,7680]{1,0:T(8,128)(2,1)}, bf16[96,7680]{1,0:T(8,128)(2,1)}, u32[]{:S(2)}, u32[]{:S(2)}) collective-permute-start(bf16[96,7680]{1,0:T(8,128)(2,1)} %all-gather.4.cloned.1.call-done.refs_0_.refs_6_), channel_id=1, source_target_pairs={{0,4},{4,0},{8,12},{12,8},{16,20},{20,16},{24,28},{28,24},{1,5},{5... | collective-permute-start | bytes 4423688 | tf_op jit(solution)/shard_map/ppermute | solution.py:94
  59.4 35.0 %collective-permute-start.16 = (bf16[96,7680]{1,0:T(8,128)(2,1)}, bf16[96,7680]{1,0:T(8,128)(2,1)}, u32[]{:S(2)}, u32[]{:S(2)}) collective-permute-start(bf16[96,7680]{1,0:T(8,128)(2,1)} %all-gather.4.cloned.1.call-done.refs_0_.refs_6_), channel_id=1, source_target_pairs={{0,8},{4,12},{8,0},{12,4},{16,24},{20,28},{24,16},{28,20},{1,9},{5... | collective-permute-start | bytes 4423688 | tf_op jit(solution)/shard_map/ppermute | solution.py:94
  62.3 148.7 %reduce-scatter.2.cloned.1.call-start = ((), (), s32[]{:S(2)}) async-start(), calls=%async_computation.2 | async-start | bytes 3686400 | tf_op jit(solution)/shard_map/reduce_scatter | solution.py:1236
  94.4 18.5 %collective-permute-start.19 = (bf16[96,7680]{1,0:T(8,128)(2,1)}, bf16[96,7680]{1,0:T(8,128)(2,1)}, u32[]{:S(2)}, u32[]{:S(2)}) collective-permute-start(bf16[96,7680]{1,0:T(8,128)(2,1)} %collective-permute-done.16.refs_2_.refs_8_), channel_id=1, source_target_pairs={{0,4},{4,0},{8,12},{12,8},{16,20},{20,16},{24,28},{28,24},{1,5},{5... | collective-permute-start | bytes 4423688 | tf_op jit(solution)/shard_map/ppermute | solution.py:94
  94.4 18.5 %collective-permute-start.20 = (bf16[96,7680]{1,0:T(8,128)(2,1)}, bf16[96,7680]{1,0:T(8,128)(2,1)}, u32[]{:S(2)}, u32[]{:S(2)}) collective-permute-start(bf16[96,7680]{1,0:T(8,128)(2,1)} %collective-permute-done.18.refs_4_.refs_10_), channel_id=1, source_target_pairs={{0,4},{4,0},{8,12},{12,8},{16,20},{20,16},{24,28},{28,24},{1,5},{5... | collective-permute-start | bytes 4423688 | tf_op jit(solution)/shard_map/ppermute | solution.py:94
  107.7 15.4 %collective-permute-start.27 = (bf16[384,1536]{1,0:T(8,128)(2,1)}, bf16[384,1536]{1,0:T(8,128)(2,1)}, u32[]{:S(2)}, u32[]{:S(2)}) collective-permute-start(bf16[384,1536]{1,0:T(8,128)(2,1)} %bitcast.42.refs_6_), channel_id=1, source_target_pairs={{0,4},{4,0},{8,12},{12,8},{16,20},{20,16},{24,28},{28,24},{1,5},{5... | collective-permute-start | bytes 3538952 | tf_op jit(solution)/shard_map/ppermute | solution.py:94
  149.5 14.3 %collective-permute-start.35 = (bf16[2,96,1152]{2,1,0:T(8,128)(2,1)S(1)}, bf16[2,96,1152]{2,1,0:T(8,128)(2,1)S(1)}, u32[]{:S(2)}, u32[]{:S(2)}) collective-permute-start(bf16[2,96,1152]{2,1,0:T(8,128)(2,1)S(1)} %copy-done.26), channel_id=1, source_target_pairs={{0,16},{4,20},{8,24},{12,28},{16,0},{20,4},{24,8},{28,12},{1,17},{... | collective-permute-start | bytes 1327112 | tf_op jit(solution)/shard_map/ppermute | solution.py:94
  169.7 19.2 %collective-permute-start.41 = (bf16[2,96,1920]{2,1,0:T(8,128)(2,1)S(1)}, bf16[2,96,1920]{2,1,0:T(8,128)(2,1)S(1)}, u32[]{:S(2)}, u32[]{:S(2)}) collective-permute-start(bf16[2,96,1920]{2,1,0:T(8,128)(2,1)S(1)} %get-tuple-element.175), channel_id=1, source_target_pairs={{0,16},{4,20},{8,24},{12,28},{16,0},{20,4},{24,8},{28,12},{1,17},{... | collective-permute-start | bytes 2211848 | tf_op jit(solution)/shard_map/ppermute | solution.py:94
  170.8 18.2 %collective-permute-start.42 = (bf16[2,96,1920]{2,1,0:T(8,128)(2,1)S(1)}, bf16[2,96,1920]{2,1,0:T(8,128)(2,1)S(1)}, u32[]{:S(2)}, u32[]{:S(2)}) collective-permute-start(bf16[2,96,1920]{2,1,0:T(8,128)(2,1)S(1)} %get-tuple-element.177), channel_id=1, source_target_pairs={{0,8},{4,12},{8,0},{12,4},{16,24},{20,28},{24,16},{28,20},{1,9},{5... | collective-permute-start | bytes 2211848 | tf_op jit(solution)/shard_map/ppermute | solution.py:94
  191.0 16.5 %collective-permute-start.43 = (bf16[96,3072]{1,0:T(8,128)(2,1)}, bf16[96,3072]{1,0:T(8,128)(2,1)S(1)}, u32[]{:S(2)}, u32[]{:S(2)}) collective-permute-start(bf16[96,3072]{1,0:T(8,128)(2,1)} %get-tuple-element.196), channel_id=1, source_target_pairs={{0,8},{4,12},{8,0},{12,4},{16,24},{20,28},{24,16},{28,20},{1,9},{5... | collective-permute-start | bytes 1769480 | tf_op jit(solution)/shard_map/ppermute | solution.py:94
  192.4 16.4 %collective-permute-start.44 = (bf16[96,3072]{1,0:T(8,128)(2,1)}, bf16[96,3072]{1,0:T(8,128)(2,1)S(1)}, u32[]{:S(2)}, u32[]{:S(2)}) collective-permute-start(bf16[96,3072]{1,0:T(8,128)(2,1)} %get-tuple-element.198), channel_id=1, source_target_pairs={{0,16},{4,20},{8,24},{12,28},{16,0},{20,4},{24,8},{28,12},{1,17},{... | collective-permute-start | bytes 1769480 | tf_op jit(solution)/shard_map/ppermute | solution.py:94
  193.4 22.8 %collective-permute-start.46 = (bf16[2,96,1152]{2,1,0:T(8,128)(2,1)}, bf16[2,96,1152]{2,1,0:T(8,128)(2,1)}, u32[]{:S(2)}, u32[]{:S(2)}) collective-permute-start(bf16[2,96,1152]{2,1,0:T(8,128)(2,1)} %copy-done.24), channel_id=1, source_target_pairs={{0,8},{4,12},{8,0},{12,4},{16,24},{20,28},{24,16},{28,20},{1,9},{5... | collective-permute-start | bytes 1327112 | tf_op jit(solution)/shard_map/ppermute | solution.py:94
  194.1 25.4 %collective-permute-start.45 = (bf16[2,96,1280]{2,1,0:T(8,128)(2,1)}, bf16[2,96,1280]{2,1,0:T(8,128)(2,1)}, u32[]{:S(2)}, u32[]{:S(2)}) collective-permute-start(bf16[2,96,1280]{2,1,0:T(8,128)(2,1)} %copy-done.23), channel_id=1, source_target_pairs={{0,16},{4,20},{8,24},{12,28},{16,0},{20,4},{24,8},{28,12},{1,17},{... | collective-permute-start | bytes 1474568 | tf_op jit(solution)/shard_map/ppermute | solution.py:94
  210.4 16.9 %collective-permute-start.48 = (bf16[2,24,6144]{2,1,0:T(8,128)(2,1)}, bf16[2,24,6144]{2,1,0:T(8,128)(2,1)S(1)}, u32[]{:S(2)}, u32[]{:S(2)}) collective-permute-start(bf16[2,24,6144]{2,1,0:T(8,128)(2,1)} %get-tuple-element.208), channel_id=1, source_target_pairs={{0,1},{1,0},{2,3},{3,2},{4,5},{5,4},{6,7},{7,6},{8,9},{9,8},{10,11... | collective-permute-start | bytes 1769480 | tf_op jit(solution)/shard_map/ppermute | solution.py:987
  212.1 15.2 %collective-permute-start.47 = (bf16[2,24,3840]{2,1,0:T(8,128)(2,1)S(1)}, bf16[2,24,3840]{2,1,0:T(8,128)(2,1)S(1)}, u32[]{:S(2)}, u32[]{:S(2)}) collective-permute-start(bf16[2,24,3840]{2,1,0:T(8,128)(2,1)S(1)} %get-tuple-element.234), channel_id=1, source_target_pairs={{0,16},{4,20},{8,24},{12,28},{16,0},{20,4},{24,8},{28,12},{1,17},{... | collective-permute-start | bytes 1105928 | tf_op jit(solution)/shard_map/ppermute | solution.py:94
  232.2 17.7 %collective-permute-start.54 = (bf16[24,2432]{1,0:T(8,128)(2,1)S(1)}, bf16[24,2432]{1,0:T(8,128)(2,1)S(1)}, u32[]{:S(2)}, u32[]{:S(2)}) collective-permute-start(bf16[24,2432]{1,0:T(8,128)(2,1)S(1)} %get-tuple-element.219), channel_id=1, source_target_pairs={{0,2},{1,3},{2,0},{3,1},{4,6},{5,7},{6,4},{7,5},{8,10},{9,11},{10,... | collective-permute-start | bytes 350216 | tf_op jit(solution)/shard_map/ppermute | solution.py:88
  234.0 15.9 %collective-permute-start.55 = (bf16[24,2432]{1,0:T(8,128)(2,1)S(1)}, bf16[24,2432]{1,0:T(8,128)(2,1)S(1)}, u32[]{:S(2)}, u32[]{:S(2)}) collective-permute-start(bf16[24,2432]{1,0:T(8,128)(2,1)S(1)} %get-tuple-element.220), channel_id=1, source_target_pairs={{0,3},{1,0},{2,1},{3,2},{4,7},{5,4},{6,5},{7,6},{8,11},{9,8},{10,9... | collective-permute-start | bytes 350216 | tf_op jit(solution)/shard_map/ppermute | solution.py:88
  (77 other events, 597.5 us)
Sparse Core Ops, SparseCore 0:
  22.9 34.9 all-gather.3
  62.4 28.1 all-gather.5
  148.7 55.6 reduce-scatter.1

commit v4 on v3

--- a/solution.py
+++ b/solution.py
@@ -236,7 +236,9 @@
         kernel,
         name=name,
         in_specs=[pl.BlockSpec(memory_space=space) for _, space in inputs],
-        out_specs=[pl.BlockSpec(memory_space=pltpu.VMEM) for _ in outputs],
+        out_specs=[
+            pl.BlockSpec(memory_space=pltpu.HBM if output[2:] == (pltpu.HBM,) else pltpu.VMEM) for output in outputs
+        ],
         out_shape=shapes,
         scratch_shapes=list(scratch),
         input_output_aliases=dict(aliases),
@@ -433,7 +435,7 @@
 
     def kernel(place, x, mem, gains, row_ids, col_ids, *refs):
         pieces, refs = refs[:count], refs[count:]
-        q, kv, probs, out, keep, send, matrix, allowed, att, sems = refs
+        q_far, kv_far, probs_far, out, keep, send, q, kv, probs, matrix, allowed, att, out_sems, sems = refs
         wait, wait_late = weights.load(place, pieces, [matrix], sems, [(2 * width, 4 * width), (0, 2 * width)])
         allowed[...] = (row_ids[...] == col_ids[...]).astype(F32)
         residual = x[...]
@@ -444,10 +446,14 @@
         kv[...] = dot(mem[...], matrix[:, 2 * width :]).astype(LOW)
         wait_late()
         q[...] = dot(normed, matrix[:, :width]).astype(LOW)
+        waits = fetch((q, kv), (q_far, kv_far), out_sems)
         attend(q, kv, kv, (0, 0, width), allowed, None, probs, att)
+        waits += fetch((probs,), (probs_far,), out_sems.at[pl.ds(2, 1)])
         attended = att[...]
         split_rows(attended, place[2], keep.at[1], send.at[1])
         out[...] = residual + dot(attended, matrix[:, width : 2 * width], TN)
+        for copied in waits:
+            copied()
 
     halves = ((3, blocks, block, rows), LOW)
     return run(
@@ -455,17 +461,21 @@
         kernel,
         [(place, pltpu.SMEM)] + vmem(after_self, memory, gains, row_ids, col_ids),
         [
-            ((rows, width), LOW, None),
-            ((mem_rows, 2 * width), LOW, None),
-            ((2 * PAIRS, mem_rows, rows), LOW, None),
+            ((rows, width), LOW, pltpu.HBM),
+            ((mem_rows, 2 * width), LOW, pltpu.HBM),
+            ((2 * PAIRS, mem_rows, rows), LOW, pltpu.HBM),
             ((rows, width), F32),
             halves,
             halves,
         ],
         [
+            pltpu.VMEM((rows, width), LOW),
+            pltpu.VMEM((mem_rows, 2 * width), LOW),
+            pltpu.VMEM((2 * PAIRS, mem_rows, rows), LOW),
             pltpu.VMEM((width, 4 * width), LOW),
             pltpu.VMEM((mem_rows, rows), F32),
             pltpu.VMEM((width, rows), LOW),
+            pltpu.SemaphoreType.DMA((3,)),
         ]
         + weights.sems(2),
         flops=8 * rows * width * width,
@@ -578,6 +588,29 @@
         [(array, pltpu.HBM) for array in arrays],
         [((share, 4 * width + late + ff), LOW, None), ((share, early_cols), LOW, None)],
         scratch,
+    )
+
+
+def cut_halves(upper, lower, half, column):
+    cols = upper.shape[1]
+
+    def kernel(upper, lower, *refs):
+        outs, sems = refs[:4], refs[4]
+        top, bottom = upper.at[pl.ds(0, half)], lower.at[pl.ds(half, half)]
+        sources = [
+            ref.at[:, pl.ds(first, size)]
+            for first, size in ((0, column), (column, cols - column))
+            for ref in (top, bottom)
+        ]
+        for wait in fetch(sources, outs, sems):
+            wait()
+
+    return run(
+        "cut_halves",
+        kernel,
+        [(upper, pltpu.HBM), (lower, pltpu.HBM)],
+        [((half, column), LOW)] * 2 + [((half, cols - column), LOW)] * 2,
+        [pltpu.SemaphoreType.DMA((4,))],
     )
 
 
@@ -673,14 +706,14 @@
     def kernel(place, gains, *refs):
         far, refs = refs[:6], refs[6:]
         pieces, refs = refs[:count], refs[count:]
-        out, mem_grad, back_out, gain_out, branch, grad, x, q, kv, probs, matrix, att, own_sems, sems = refs
-        ranges = [(width, 2 * width), (0, width), (2 * width, 4 * width)]
+        out, back_out, gain_out, branch, grad, x, q, kv, probs, matrix, att, own_sems, sems = refs
+        ranges = [(width, 2 * width), (0, width)]
         branch_wait = fetch(far[:1], (branch,), own_sems)
         loaded = weights.load(place, pieces, [matrix], sems, ranges, True)
         for copy in loaded[0][0]:
             copy.start()
         waits = fetch(far[1:4], (kv, probs, q), own_sems.at[pl.ds(1, 3)])
-        for copy in loaded[1][0] + loaded[2][0]:
+        for copy in loaded[1][0]:
             copy.start()
         late_waits = fetch(far[4:], (x, grad), own_sems.at[pl.ds(4, 2)])
         branch_wait[0]()
@@ -691,7 +724,6 @@
             wait()
         attend_back(q, kv, kv, (0, 0, width), att, probs, outs, None)
         loaded[1][1]()
-        loaded[2][1]()
         for wait in late_waits:
             wait()
         back, gain = norm_back(x[...], gains[1:2, :], dot(out[:, :width], matrix[:, :width], NT))
@@ -699,7 +731,6 @@
         back_out[...] = total
         out[:, 3 * width :] = total.astype(LOW)
         gain_out[...] = gain
-        mem_grad[...] = dot(out[:, width : 3 * width], matrix[:, 2 * width :], NT)
 
     return run(
         "cross_backward",
@@ -709,7 +740,6 @@
         + [(array, pltpu.HBM) for array in (branch, kv, probs, q, after_self, grad)],
         [
             ((rows, 4 * width), LOW),
-            ((mem_rows, width), F32, None),
             ((rows, width), F32),
             ((1, width), F32),
         ],
@@ -720,14 +750,36 @@
             pltpu.VMEM((rows, width), LOW),
             pltpu.VMEM((mem_rows, 2 * width), LOW),
             pltpu.VMEM((2 * PAIRS, mem_rows, rows), LOW),
-            pltpu.VMEM((width, 4 * width), LOW),
+            pltpu.VMEM((width, 2 * width), LOW),
             pltpu.VMEM((rows, width), LOW),
             pltpu.SemaphoreType.DMA((6,)),
         ]
-        + weights.sems(3),
+        + weights.sems(2),
         flops=8 * rows * width * width,
         weights=[weights],
     )
+
+
+def memory_gradient(place, grads, weights):
+    rows = grads.shape[0]
+    width = grads.shape[1] // 4
+    count = len(weights.arrays)
+
+    def kernel(place, grads, *refs):
+        pieces, (out, matrix, sems) = refs[:count], refs[count:]
+        (wait,) = weights.load(place, pieces, [matrix], sems, [(2 * width, 4 * width)])
+        wait()
+        out[...] = dot(grads[:, width : 3 * width], matrix[:, 2 * width :], NT)
+
+    return run(
+        "memory_gradient",
+        kernel,
+        [(place, pltpu.SMEM)] + vmem(grads),
+        [((rows, width), F32, None)],
+        [pltpu.VMEM((width, 4 * width), LOW)] + weights.sems(),
+        flops=4 * rows * width * width,
+        weights=[weights],
+    )[0]
 
 
 def self_backward(place, grad, cross_grads, tokens, gains, cross_gain, hidden_gain, qk, v, probs, hot, weights, cut, block):
@@ -882,8 +934,9 @@
     arrays = [array for pair in lefts for array in pair] + [array for pair in rights for array in pair]
     outputs = []
     if sections:
-        outputs += [((counts[1], block, cols[0]), LOW)] * counts[0]
-        outputs += [((counts[0], block, cols[1]), LOW)] * counts[1]
+        for half in range(2):
+            shape = (counts[1 - half], block, cols[half])
+            outputs += [(shape, LOW, None)] + [(shape, LOW)] * (counts[half] - 1)
     if straight:
         outputs.append(((nz, blocks, block // nz, across_z), LOW, None))
     return run(
@@ -982,7 +1035,7 @@
                 at += size
 
     arrays = [part for parts in sides for part in parts]
-    keep, send = run("halve", kernel, [(place, pltpu.SMEM)] + vmem(*arrays), [(shape, LOW), (shape, LOW)])
+    keep, send = run("halve", kernel, [(place, pltpu.SMEM)] + vmem(*arrays), [(shape, LOW, None), (shape, LOW)])
     pairs = [(i, mirrored(i, count)) for i in range(grid_sizes()["z"])]
     return keep, lax.ppermute(send, "narrow", pairs)
 
@@ -1163,8 +1216,8 @@
     if pieces:
         twin = swapped(rest_near[0])
         rest_x, rest_y = (after(array, after_self, s_far, twin) for array in rest_near[1:])
-        corner = from_corner(rest_x[:half, :ff], rest_y[half:, :ff])
-        upper, lower = rest_x[:half, ff:], rest_y[half:, ff:]
+        top, bottom, upper, lower = cut_halves(rest_x, rest_y, half, ff)
+        corner = from_corner(top, bottom)
         in_all = jnp.transpose(after(in_all, twin), (1, 0, 2, 3)).reshape(4 * block, early_cols)
         corner = [after(array, upper, lower, in_all) for array in corner]
         rest_arrays = [rest_near[0], twin] + with_twins([rest_x, rest_y])
@@ -1239,7 +1292,7 @@
     cross_cols = 2 * width + side + ff_cols
 
     branch_far = swapped(branch)
-    cross_grads, memory_grad, grad, cross_gain_part = cross_backward(
+    cross_grads, grad, cross_gain_part = cross_backward(
         place, grad, after(branch, branch_far), after_self, gains, q, kv, cross_probs, w_cross
     )
     cross_parts = weight_grads(
@@ -1283,7 +1336,8 @@
     cross_first, cross_second = cross_parts[:nx], cross_parts[nx:]
     cross_first, cross_second = sent(cross_first, "x"), sent(cross_second, "y")
     cross_parts = halve(place, [by_blocks(cross_first), by_blocks(cross_second)], 2, True)
-    self_first = [after(self_first[0], cross_parts[0])] + self_first[1:]
+    memory_grad = memory_gradient(after(place, *self_parts), cross_grads, w_cross)
+    self_first = [after(self_first[0], cross_parts[0], memory_grad)] + self_first[1:]
     self_parts = add_stage(place, [self_first], [self_second])
     self_first, self_second = self_parts[:nx], self_parts[nx:]
     self_first, self_second = sent(self_first, "x"), sent(self_second, "y")

time: 259 us -> 257 us (level)
  local copies, waits for them, and re-layouts: 21.7 us -> 15.5 us
  Pallas kernels: 80.2 us -> 85.5 us
    slice x4 -> x0, local copies, waits for them, and re-layouts: 7.05 us -> none  [the longest x2 3.67 us: local(): upper, lower = (rest_x[:half, ff:], rest_y[half:, ff:])]
    pallas_call x19 -> x21, Pallas kernels: 80.2 us -> 85.5 us  [run(): pl.pallas_call(kernel, name=name, in_specs=[pl.BlockSpec(memory_space=spa...]
    unnamed x84 -> x98, local copies, waits for them, and re-layouts: 7.53 us -> 9.28 us
  transfers between devices with their start and end apart: 59 -> 59, of which waited for: 27 -> 30; matrix products, arithmetic and copies ran while one was open for 6% -> 3% of each run, Pallas kernels for 26% -> 28%
where the time goes in v4:
time: 257 us
  waiting for transfers between devices  93.7 us (36%)
  Pallas kernels  85.5 us (33%)
  starting transfers between devices  45 us (18%)
  local copies, waits for them, and re-layouts  15.5 us (6%)
  between operations  14.5 us (6%)
    pallas_call x21, Pallas kernels, run(): pl.pallas_call(kernel, name=name, in_specs=[pl.BlockSpec(memory_space=spa...  85.5 us
    ppermute x48, waiting for transfers between devices, shifted(): return lax.ppermute(array, 'wide', pairs)  76.9 us
    ppermute x48, starting transfers between devices, shifted(): return lax.ppermute(array, 'wide', pairs)  32.6 us
    ppermute x6, waiting for transfers between devices, shifted(): lax.ppermute(array, 'narrow', [(i, (i + step) % count) for i in range(cou...  12.8 us
    ppermute x6, starting transfers between devices, shifted(): lax.ppermute(array, 'narrow', [(i, (i + step) % count) for i in range(cou...  10.4 us
    unnamed x98, local copies, waits for them, and re-layouts  9.28 us
  transfers between devices with their start and end apart: 59, of which 30 were waited for; matrix products, arithmetic and copies ran while one was open for 3% of the time, Pallas kernels for 28%

profile of v4, /device:TPU:0, one launch (start us, length us, event | category | flops | bytes accessed | tf_op | source)
XLA Modules:
  0.0 256.7 jit_solution(13011163109367016690)
XLA Ops:
  8.2 5.1 %collective-permute-start.3 = (bf16[24,3200]{1,0:T(8,128)(2,1)S(1)}, bf16[24,3200]{1,0:T(8,128)(2,1)S(1)}, u32[]{:S(2)}, u32[]{:S(2)}) collective-permute-start(bf16[24,3200]{1,0:T(8,128)(2,1)S(1)} %pack_first.1), channel_id=1, source_target_pairs={{0,3},{1,0},{2,1},{3,2},{4,7},{5,4},{6,5},{7,6},{8,11},{9,8},{10,9... | collective-permute-start | bytes 460808 | tf_op jit(solution)/shard_map/ppermute | solution.py:88
  14.4 2.4 pack_rest.1
  18.4 2.9 %collective-permute-done.4 = bf16[24,1536]{1,0:T(8,128)(2,1)S(1)} collective-permute-done((bf16[24,1536]{1,0:T(8,128)(2,1)S(1)}, bf16[24,1536]{1,0:T(8,128)(2,1)S(1)}, u32[]{:S(2)}, u32[]{:S(2)}) %collective-permute-start.4) | collective-permute-done | bytes 73760 | tf_op jit(solution)/shard_map/ppermute | solution.py:94
  22.8 3.5 %collective-permute-done.2 = bf16[24,3200]{1,0:T(8,128)(2,1)S(1)} collective-permute-done((bf16[24,3200]{1,0:T(8,128)(2,1)S(1)}, bf16[24,3200]{1,0:T(8,128)(2,1)S(1)}, u32[]{:S(2)}, u32[]{:S(2)}) %collective-permute-start.2) | collective-permute-done | bytes 153632 | tf_op jit(solution)/shard_map/ppermute | solution.py:88
  30.2 12.2 %collective-permute-done.9.refs_4_ = bf16[96,3200]{1,0:T(8,128)(2,1)S(1)} collective-permute-done((bf16[96,3200]{1,0:T(8,128)(2,1)S(1)}, bf16[96,3200]{1,0:T(8,128)(2,1)S(1)}, u32[]{:S(2)}, u32[]{:S(2)}) %collective-permute-start.9) | collective-permute-done | bytes 614432 | tf_op jit(solution)/shard_map/ppermute | solution.py:94
  42.4 2.6 collective-permute-done.7.refs_2_
  49.2 6.0 %collective-permute-done.13.refs_8_ = bf16[48,3200]{1,0:T(8,128)(2,1)} collective-permute-done((bf16[48,3200]{1,0:T(8,128)(2,1)S(1)}, bf16[48,3200]{1,0:T(8,128)(2,1)}, u32[]{:S(2)}, u32[]{:S(2)}) %collective-permute-start.13) | collective-permute-done | bytes 307232 | tf_op jit(solution)/shard_map/ppermute | solution.py:94
  64.3 9.5 %self_forward.1 = (bf16[256,1536]{1,0:T(8,128)(2,1)S(1)}, bf16[256,768]{1,0:T(8,128)(2,1)S(1)}, bf16[12,256,256]{2,1,0:T(8,128)(2,1)S(1)}, f32[256,768]{1,0:T(8,...) custom-call(s32[20]{0:T(128)S(1)} %stack.118.place, ...), custom_call_target="tpu_custom_call" | custom-call | flops 1207959552 | bytes 2680360 | tf_op jit(solution)/shard_map/self_forward/pallas_call | solution.py:235
  78.5 13.1 %collective-permute-done.18.lower.refs_4_.refs_10_ = bf16[96,7680]{1,0:T(8,128)(2,1)} collective-permute-done((bf16[96,7680]{1,0:T(8,128)(2,1)}, bf16[96,7680]{1,0:T(8,128)(2,1)}, u32[]{:S(2)}, u32[]{:S(2)}) %collective-permute-start.18) | collective-permute-done | bytes 1474592 | tf_op jit(solution)/shard_map/ppermute | solution.py:94
  91.5 2.9 %collective-permute-done.16.upper.refs_2_.refs_8_ = bf16[96,7680]{1,0:T(8,128)(2,1)} collective-permute-done((bf16[96,7680]{1,0:T(8,128)(2,1)}, bf16[96,7680]{1,0:T(8,128)(2,1)}, u32[]{:S(2)}, u32[]{:S(2)}) %collective-permute-start.16) | collective-permute-done | bytes 1474592 | tf_op jit(solution)/shard_map/ppermute | solution.py:94
  101.8 4.8 %collective-permute-done.21.refs_6_.refs_12_ = bf16[48,3072]{1,0:T(8,128)(2,1)} collective-permute-done((bf16[48,3072]{1,0:T(8,128)(2,1)}, bf16[48,3072]{1,0:T(8,128)(2,1)}, u32[]{:S(2)}, u32[]{:S(2)}) %collective-permute-start.21) | collective-permute-done | bytes 294944 | tf_op jit(solution)/shard_map/ppermute | solution.py:94
  111.1 9.8 %cross_forward.1 = (bf16[256,768]{1,0:T(8,128)(2,1)S(1)}, bf16[256,1536]{1,0:T(8,128)(2,1)S(1)}, bf16[12,256,256]{2,1,0:T(8,128)(2,1)S(1)}, f32[256,768]{1,0:T(8...) custom-call(s32[20]{0:T(128)S(1)} %stack.118.place, ...), custom_call_target="tpu_custom_call" | custom-call | flops 1207959552 | bytes 5616680 | tf_op jit(solution)/shard_map/cross_forward/pallas_call | solution.py:235
  122.8 4.2 %hidden_early.1 = (bf16[768,3072]{1,0:T(8,128)(2,1)S(1)}, bf16[3072,768]{1,0:T(8,128)(2,1)S(1)}) custom-call(s32[20]{0:T(128)S(1)} %stack.118.place, bf16[96,7680]{1,0:T(8,128)(2,1)} %all-gather.4.cloned.1.call-done.refs_0_.refs_6_, bf16[96,7680]{1,0:T(8,128)(2,1)} %collective-permute-done.17.refs_1_.refs_7_, ...), custom_call_target="tpu_custom_call" | custom-call | bytes 5603368 | tf_op jit(solution)/shard_map/hidden_early/pallas_call | solution.py:235
  128.8 7.5 %hidden_first.1 = (bf16[256,3072]{1,0:T(8,128)(2,1)S(1)}, bf16[256,3072]{1,0:T(8,128)(2,1)S(1)}, bf16[4,480,256]{2,1,0:T(8,128)(2,1)S(1)}, bf16[4,480,256]{2,1,0...) custom-call(s32[20]{0:T(128)S(1)} %stack.118.place, ...), custom_call_target="tpu_custom_call", output_to_operand_aliasing={{4}: (4, {}), {5}: (5, {})} | custom-call | flops 2415919104 | bytes 6205480 | tf_op jit(solution)/shard_map/hidden_first/pallas_call | solution.py:235
  137.0 3.7 %hidden_second.1 = (bf16[256,768]{1,0:T(8,128)(2,1)}, f32[256,768]{1,0:T(8,128)S(1)}, bf16[256,768]{1,0:T(8,128)(2,1)S(1)}, f32[1,768]{1,0:T(1,128)S(1)}) custom-call(f32[256,768]{1,0:T(8,128)S(1)} %get-tuple-element.152.x, bf16[256,768]{1,0:T(8,128)(2,1)S(1)} %copy-done.1, f32[8,768]{1,0:T(8,128)S(1)} %copy-done.12, ...), custom_call_target="tpu_custom_call" | custom-call | flops 2415919104 | bytes 6893568 | tf_op jit(solution)/shard_map/hidden_second/pallas_call | solution.py:235
  141.3 5.1 %weight_grads.3 = (bf16[2,96,1152]{2,1,0:T(8,128)(2,1)S(1)}, bf16[2,96,1152]{2,1,0:T(8,128)(2,1)}, bf16[2,96,1152]{2,1,0:T(8,128)(2,1)S(1)}, bf16[2,96,1152]{2,1,0:T(8,128)(2,1)}, bf16[4,4,24,3840]{3,2,1,0:T(8,128)(2,1)}) custom-call(s32[20]{0:T(128)S(1)} %stack.118.place, bf16[1,4,480,256]{3,2,1,0:T(8,128)(2,1)S(1)} %bitcast.78, ...), custom_call_target="tpu_custom_call" | custom-call | flops 2415919104 | bytes 2949160 | tf_op jit(solution)/shard_map/weight_grads/pallas_call | solution.py:235
  150.9 9.5 %cross_backward.1 = (bf16[256,3072]{1,0:T(8,128)(2,1)S(1)}, f32[256,768]{1,0:T(8,128)S(1)}, f32[1,768]{1,0:T(1,128)S(1)}) custom-call(s32[20]{0:T(128)S(1)} %stack.118.place, f32[8,768]{1,0:T(8,128)S(1)} %copy-done.13, bf16[256,768]{1,0:T(8,128)(2,1)} %copy-done.5, bf16[256,1536]{1,0:T(8,128)(2,1)} %copy-done.8, bf16[12,256,256]{2,1,0:T(8,128)(2,1)} %copy-done.4, ...), custom_call_target="tpu_custom_call" | custom-call | flops 1207959552 | bytes 7385128 | tf_op jit(solution)/shard_map/cross_backward/pallas_call | solution.py:235
  161.1 3.4 %collective-permute-done.37.refs_5_ = bf16[256,3072]{1,0:T(8,128)(2,1)S(1)} collective-permute-done((bf16[256,3072]{1,0:T(8,128)(2,1)S(1)}, bf16[256,3072]{1,0:T(8,128)(2,1)S(1)}, u32[]{:S(2)}, u32[]{:S(2)}) %collective-permute-start.37) | collective-permute-done | bytes 1572896 | tf_op jit(solution)/shard_map/ppermute | solution.py:94
  168.9 12.6 %self_backward.1 = (bf16[256,768]{1,0:T(8,128)(2,1)S(1)}, bf16[256,768]{1,0:T(8,128)(2,1)S(1)}, bf16[320,768]{1,0:T(8,128)(2,1)S(1)}, f32[256,768]{1,0:T(8,128)}, bf16[4,96,128]{2,1,0:T(8,128)(2,1)S(1)}) custom-call(s32[20]{0:T(128)S(1)} %stack.118.place, f32[256,768]{1,0:T(8,128)S(1)} %get-tuple-element.186.grad, ...), custom_call_target="tpu_custom_call" | custom-call | flops 1207959552 | bytes 5250088 | tf_op jit(solution)/shard_map/self_backward/pallas_call | solution.py:235
  193.2 12.3 %collective-permute-done.43 = bf16[96,3072]{1,0:T(8,128)(2,1)S(1)} collective-permute-done((bf16[96,3072]{1,0:T(8,128)(2,1)}, bf16[96,3072]{1,0:T(8,128)(2,1)S(1)}, u32[]{:S(2)}, u32[]{:S(2)}) %collective-permute-start.43) | collective-permute-done | bytes 589856 | tf_op jit(solution)/shard_map/ppermute | solution.py:94
  213.1 3.9 %memory_gradient.1 = f32[256,768]{1,0:T(8,128)} custom-call(s32[20]{0:T(128)S(1)} %stack.118.place, bf16[256,3072]{1,0:T(8,128)(2,1)S(1)} %get-tuple-element.181.refs_4_.before.grads, bf16[96,7680]{1,0:T(8,128)(2,1)} %all-gather.4.cloned.1.call-done.refs_0_.refs_6_, bf16[96,7680]{1,0:T(8,128)(2,1)} %collective-permute-done.17.refs_1_.refs_7_, ...), custom_call_target="tpu_custom_call" | custom-call | flops 603979776 | bytes 5799976 | tf_op jit(solution)/shard_map/memory_gradient/pallas_call | solution.py:235
  221.2 4.2 %collective-permute-done.47.kept_far = bf16[2,24,3840]{2,1,0:T(8,128)(2,1)S(1)} collective-permute-done((bf16[2,24,3840]{2,1,0:T(8,128)(2,1)}, bf16[2,24,3840]{2,1,0:T(8,128)(2,1)S(1)}, u32[]{:S(2)}, u32[]{:S(2)}) %collective-permute-start.47) | collective-permute-done | bytes 368672 | tf_op jit(solution)/shard_map/ppermute | solution.py:94
  234.0 2.5 collective-permute-done.51.far
  238.9 9.1 %collective-permute-done.54.refs_2_ = bf16[24,2432]{1,0:T(8,128)(2,1)S(1)} collective-permute-done((bf16[24,2432]{1,0:T(8,128)(2,1)S(1)}, bf16[24,2432]{1,0:T(8,128)(2,1)S(1)}, u32[]{:S(2)}, u32[]{:S(2)}) %collective-permute-start.54) | collective-permute-done | bytes 116768 | tf_op jit(solution)/shard_map/ppermute | solution.py:88
  (237 shorter events, 89.3 us)
Async XLA Ops:
  7.2 50.7 %all-gather.4.cloned.1.call-start = ((), (), s32[]{:S(2)}) async-start(), calls=%async_computation.1 | async-start | bytes 1843200 | tf_op jit(solution)/shard_map/all_gather | solution.py:1190
  8.2 14.5 %collective-permute-start.3 = (bf16[24,3200]{1,0:T(8,128)(2,1)S(1)}, bf16[24,3200]{1,0:T(8,128)(2,1)S(1)}, u32[]{:S(2)}, u32[]{:S(2)}) collective-permute-start(bf16[24,3200]{1,0:T(8,128)(2,1)S(1)} %pack_first.1), channel_id=1, source_target_pairs={{0,3},{1,0},{2,1},{3,2},{4,7},{5,4},{6,5},{7,6},{8,11},{9,8},{10,9... | collective-permute-start | bytes 460808 | tf_op jit(solution)/shard_map/ppermute | solution.py:88
  13.4 13.0 %collective-permute-start.2 = (bf16[24,3200]{1,0:T(8,128)(2,1)S(1)}, bf16[24,3200]{1,0:T(8,128)(2,1)S(1)}, u32[]{:S(2)}, u32[]{:S(2)}) collective-permute-start(bf16[24,3200]{1,0:T(8,128)(2,1)S(1)} %pack_first.1), channel_id=1, source_target_pairs={{0,2},{1,3},{2,0},{3,1},{4,6},{5,7},{6,4},{7,5},{8,10},{9,11},{10,... | collective-permute-start | bytes 460808 | tf_op jit(solution)/shard_map/ppermute | solution.py:88
  22.8 76.7 %all-gather.6.cloned.1.call-start = ((), (), s32[]{:S(2)}) async-start(), calls=%async_computation.3 | async-start | bytes 1474560 | tf_op jit(solution)/shard_map/all_gather | solution.py:1201
  27.2 15.2 %collective-permute-start.9 = (bf16[96,3200]{1,0:T(8,128)(2,1)S(1)}, bf16[96,3200]{1,0:T(8,128)(2,1)S(1)}, u32[]{:S(2)}, u32[]{:S(2)}) collective-permute-start(bf16[96,3200]{1,0:T(8,128)(2,1)S(1)} %bitcast.80), channel_id=1, source_target_pairs={{0,16},{4,20},{8,24},{12,28},{16,0},{20,4},{24,8},{28,12},{1,17},{... | collective-permute-start | bytes 1843208 | tf_op jit(solution)/shard_map/ppermute | solution.py:94
  28.7 13.7 %collective-permute-start.6 = (bf16[96,3200]{1,0:T(8,128)(2,1)S(1)}, bf16[96,3200]{1,0:T(8,128)(2,1)S(1)}, u32[]{:S(2)}, u32[]{:S(2)}) collective-permute-start(bf16[96,3200]{1,0:T(8,128)(2,1)S(1)} %bitcast.81), channel_id=1, source_target_pairs={{0,4},{4,0},{8,12},{12,8},{16,20},{20,16},{24,28},{28,24},{1,5},{5... | collective-permute-start | bytes 1843208 | tf_op jit(solution)/shard_map/ppermute | solution.py:94
  28.7 16.3 %collective-permute-start.7 = (bf16[96,3200]{1,0:T(8,128)(2,1)S(1)}, bf16[96,3200]{1,0:T(8,128)(2,1)S(1)}, u32[]{:S(2)}, u32[]{:S(2)}) collective-permute-start(bf16[96,3200]{1,0:T(8,128)(2,1)S(1)} %bitcast.82), channel_id=1, source_target_pairs={{0,8},{4,12},{8,0},{12,4},{16,24},{20,28},{24,16},{28,20},{1,9},{5... | collective-permute-start | bytes 1843208 | tf_op jit(solution)/shard_map/ppermute | solution.py:94
  45.5 15.4 %collective-permute-start.22 = (bf16[24,1536]{1,0:T(8,128)(2,1)S(1)}, bf16[24,1536]{1,0:T(8,128)(2,1)}, u32[]{:S(2)}, u32[]{:S(2)}) collective-permute-start(bf16[24,1536]{1,0:T(8,128)(2,1)S(1)} %get-tuple-element.129), channel_id=1, source_target_pairs={{0,16},{4,20},{8,24},{12,28},{16,0},{20,4},{24,8},{28,12},{1,17},{... | collective-permute-start | bytes 221192 | tf_op jit(solution)/shard_map/ppermute | solution.py:94
  57.9 33.6 %collective-permute-start.18 = (bf16[96,7680]{1,0:T(8,128)(2,1)}, bf16[96,7680]{1,0:T(8,128)(2,1)}, u32[]{:S(2)}, u32[]{:S(2)}) collective-permute-start(bf16[96,7680]{1,0:T(8,128)(2,1)} %all-gather.4.cloned.1.call-done.refs_0_.refs_6_), channel_id=1, source_target_pairs={{0,16},{4,20},{8,24},{12,28},{16,0},{20,4},{24,8},{28,12},{1,17},{... | collective-permute-start | bytes 4423688 | tf_op jit(solution)/shard_map/ppermute | solution.py:94
  59.4 32.1 %collective-permute-start.17 = (bf16[96,7680]{1,0:T(8,128)(2,1)}, bf16[96,7680]{1,0:T(8,128)(2,1)}, u32[]{:S(2)}, u32[]{:S(2)}) collective-permute-start(bf16[96,7680]{1,0:T(8,128)(2,1)} %all-gather.4.cloned.1.call-done.refs_0_.refs_6_), channel_id=1, source_target_pairs={{0,4},{4,0},{8,12},{12,8},{16,20},{20,16},{24,28},{28,24},{1,5},{5... | collective-permute-start | bytes 4423688 | tf_op jit(solution)/shard_map/ppermute | solution.py:94
  59.4 35.0 %collective-permute-start.16 = (bf16[96,7680]{1,0:T(8,128)(2,1)}, bf16[96,7680]{1,0:T(8,128)(2,1)}, u32[]{:S(2)}, u32[]{:S(2)}) collective-permute-start(bf16[96,7680]{1,0:T(8,128)(2,1)} %all-gather.4.cloned.1.call-done.refs_0_.refs_6_), channel_id=1, source_target_pairs={{0,8},{4,12},{8,0},{12,4},{16,24},{20,28},{24,16},{28,20},{1,9},{5... | collective-permute-start | bytes 4423688 | tf_op jit(solution)/shard_map/ppermute | solution.py:94
  63.2 147.4 %reduce-scatter.2.cloned.1.call-start = ((), (), s32[]{:S(2)}) async-start(), calls=%async_computation.2 | async-start | bytes 3686400 | tf_op jit(solution)/shard_map/reduce_scatter | solution.py:1289
  94.4 16.6 %collective-permute-start.19 = (bf16[96,7680]{1,0:T(8,128)(2,1)}, bf16[96,7680]{1,0:T(8,128)(2,1)}, u32[]{:S(2)}, u32[]{:S(2)}) collective-permute-start(bf16[96,7680]{1,0:T(8,128)(2,1)} %collective-permute-done.16.upper.refs_2_.refs_8_), channel_id=1, source_target_pairs={{0,4},{4,0},{8,12},{12,8},{16,20},{20,16},{24,28},{28,24},{1,5},{5... | collective-permute-start | bytes 4423688 | tf_op jit(solution)/shard_map/ppermute | solution.py:94
  94.4 16.6 %collective-permute-start.20 = (bf16[96,7680]{1,0:T(8,128)(2,1)}, bf16[96,7680]{1,0:T(8,128)(2,1)}, u32[]{:S(2)}, u32[]{:S(2)}) collective-permute-start(bf16[96,7680]{1,0:T(8,128)(2,1)} %collective-permute-done.18.lower.refs_4_.refs_10_), channel_id=1, source_target_pairs={{0,4},{4,0},{8,12},{12,8},{16,20},{20,16},{24,28},{28,24},{1,5},{5... | collective-permute-start | bytes 4423688 | tf_op jit(solution)/shard_map/ppermute | solution.py:94
  107.2 15.6 %collective-permute-start.27 = (bf16[384,1536]{1,0:T(8,128)(2,1)}, bf16[384,1536]{1,0:T(8,128)(2,1)}, u32[]{:S(2)}, u32[]{:S(2)}) collective-permute-start(bf16[384,1536]{1,0:T(8,128)(2,1)} %bitcast.42.refs_6_), channel_id=1, source_target_pairs={{0,4},{4,0},{8,12},{12,8},{16,20},{20,16},{24,28},{28,24},{1,5},{5... | collective-permute-start | bytes 3538952 | tf_op jit(solution)/shard_map/ppermute | solution.py:94
  166.9 20.3 %collective-permute-start.41 = (bf16[2,96,1920]{2,1,0:T(8,128)(2,1)S(1)}, bf16[2,96,1920]{2,1,0:T(8,128)(2,1)S(1)}, u32[]{:S(2)}, u32[]{:S(2)}) collective-permute-start(bf16[2,96,1920]{2,1,0:T(8,128)(2,1)S(1)} %get-tuple-element.183), channel_id=1, source_target_pairs={{0,16},{4,20},{8,24},{12,28},{16,0},{20,4},{24,8},{28,12},{1,17},{... | collective-permute-start | bytes 2211848 | tf_op jit(solution)/shard_map/ppermute | solution.py:94
  168.4 18.8 %collective-permute-start.42 = (bf16[2,96,1920]{2,1,0:T(8,128)(2,1)S(1)}, bf16[2,96,1920]{2,1,0:T(8,128)(2,1)S(1)}, u32[]{:S(2)}, u32[]{:S(2)}) collective-permute-start(bf16[2,96,1920]{2,1,0:T(8,128)(2,1)S(1)} %get-tuple-element.185), channel_id=1, source_target_pairs={{0,8},{4,12},{8,0},{12,4},{16,24},{20,28},{24,16},{28,20},{1,9},{5... | collective-permute-start | bytes 2211848 | tf_op jit(solution)/shard_map/ppermute | solution.py:94
  189.1 16.4 %collective-permute-start.43 = (bf16[96,3072]{1,0:T(8,128)(2,1)}, bf16[96,3072]{1,0:T(8,128)(2,1)S(1)}, u32[]{:S(2)}, u32[]{:S(2)}) collective-permute-start(bf16[96,3072]{1,0:T(8,128)(2,1)} %get-tuple-element.204), channel_id=1, source_target_pairs={{0,8},{4,12},{8,0},{12,4},{16,24},{20,28},{24,16},{28,20},{1,9},{5... | collective-permute-start | bytes 1769480 | tf_op jit(solution)/shard_map/ppermute | solution.py:94
  190.6 16.5 %collective-permute-start.44 = (bf16[96,3072]{1,0:T(8,128)(2,1)}, bf16[96,3072]{1,0:T(8,128)(2,1)}, u32[]{:S(2)}, u32[]{:S(2)}) collective-permute-start(bf16[96,3072]{1,0:T(8,128)(2,1)} %get-tuple-element.206), channel_id=1, source_target_pairs={{0,16},{4,20},{8,24},{12,28},{16,0},{20,4},{24,8},{28,12},{1,17},{... | collective-permute-start | bytes 1769480 | tf_op jit(solution)/shard_map/ppermute | solution.py:94
  191.2 25.8 %collective-permute-start.46 = (bf16[2,96,1152]{2,1,0:T(8,128)(2,1)}, bf16[2,96,1152]{2,1,0:T(8,128)(2,1)}, u32[]{:S(2)}, u32[]{:S(2)}) collective-permute-start(bf16[2,96,1152]{2,1,0:T(8,128)(2,1)} %copy-done.34), channel_id=1, source_target_pairs={{0,8},{4,12},{8,0},{12,4},{16,24},{20,28},{24,16},{28,20},{1,9},{5... | collective-permute-start | bytes 1327112 | tf_op jit(solution)/shard_map/ppermute | solution.py:94
  192.6 25.0 %collective-permute-start.45 = (bf16[2,96,1280]{2,1,0:T(8,128)(2,1)}, bf16[2,96,1280]{2,1,0:T(8,128)(2,1)}, u32[]{:S(2)}, u32[]{:S(2)}) collective-permute-start(bf16[2,96,1280]{2,1,0:T(8,128)(2,1)} %copy-done.33), channel_id=1, source_target_pairs={{0,16},{4,20},{8,24},{12,28},{16,0},{20,4},{24,8},{28,12},{1,17},{... | collective-permute-start | bytes 1474568 | tf_op jit(solution)/shard_map/ppermute | solution.py:94
  210.0 15.4 %collective-permute-start.48 = (bf16[2,24,6144]{2,1,0:T(8,128)(2,1)}, bf16[2,24,6144]{2,1,0:T(8,128)(2,1)S(1)}, u32[]{:S(2)}, u32[]{:S(2)}) collective-permute-start(bf16[2,24,6144]{2,1,0:T(8,128)(2,1)} %get-tuple-element.216), channel_id=1, source_target_pairs={{0,1},{1,0},{2,3},{3,2},{4,5},{5,4},{6,7},{7,6},{8,9},{9,8},{10,11... | collective-permute-start | bytes 1769480 | tf_op jit(solution)/shard_map/ppermute | solution.py:1040
  230.3 17.7 %collective-permute-start.54 = (bf16[24,2432]{1,0:T(8,128)(2,1)S(1)}, bf16[24,2432]{1,0:T(8,128)(2,1)S(1)}, u32[]{:S(2)}, u32[]{:S(2)}) collective-permute-start(bf16[24,2432]{1,0:T(8,128)(2,1)S(1)} %get-tuple-element.227), channel_id=1, source_target_pairs={{0,2},{1,3},{2,0},{3,1},{4,6},{5,7},{6,4},{7,5},{8,10},{9,11},{10,... | collective-permute-start | bytes 350216 | tf_op jit(solution)/shard_map/ppermute | solution.py:88
  232.0 16.1 %collective-permute-start.55 = (bf16[24,2432]{1,0:T(8,128)(2,1)S(1)}, bf16[24,2432]{1,0:T(8,128)(2,1)S(1)}, u32[]{:S(2)}, u32[]{:S(2)}) collective-permute-start(bf16[24,2432]{1,0:T(8,128)(2,1)S(1)} %get-tuple-element.228), channel_id=1, source_target_pairs={{0,3},{1,0},{2,1},{3,2},{4,7},{5,4},{6,5},{7,6},{8,11},{9,8},{10,9... | collective-permute-start | bytes 350216 | tf_op jit(solution)/shard_map/ppermute | solution.py:88
  (84 other events, 677.9 us)
Sparse Core Ops, SparseCore 0:
  22.9 34.9 all-gather.3
  63.3 27.7 all-gather.5
  148.0 55.1 reduce-scatter.1

commit v5 on v4

--- a/solution.py
+++ b/solution.py
@@ -1335,9 +1335,10 @@
     cross_parts = add_stage(place, [cross_first, ff_first], [cross_second, ff_second])
     cross_first, cross_second = cross_parts[:nx], cross_parts[nx:]
     cross_first, cross_second = sent(cross_first, "x"), sent(cross_second, "y")
+    memory_grad = memory_gradient(after(place, *cross_parts), cross_grads, w_cross)
+    cross_first = [after(cross_first[0], memory_grad)] + cross_first[1:]
     cross_parts = halve(place, [by_blocks(cross_first), by_blocks(cross_second)], 2, True)
-    memory_grad = memory_gradient(after(place, *self_parts), cross_grads, w_cross)
-    self_first = [after(self_first[0], cross_parts[0], memory_grad)] + self_first[1:]
+    self_first = [after(self_first[0], cross_parts[0])] + self_first[1:]
     self_parts = add_stage(place, [self_first], [self_second])
     self_first, self_second = self_parts[:nx], self_parts[nx:]
     self_first, self_second = sent(self_first, "x"), sent(self_second, "y")
@@ -1349,7 +1350,6 @@
         count *= 2
         earlier = (*self_parts, *in_early) if pieces else self_parts
         cross_parts = halve(place, [[after(part, *earlier) for part in cross_parts]], count, False)
-    self_first = [after(self_first[0], cross_parts[0])] + self_first[1:]
     self_sums = add_last(place, (self_first, self_second))
     self_parts = sent(self_sums, "z")
     if pieces:

time: 257 us -> 257 us (level)
    unnamed x98 -> x94, local copies, waits for them, and re-layouts: 9.28 us -> 8.44 us
  transfers between devices with their start and end apart: 59 -> 59, of which waited for: 30 -> 31; matrix products, arithmetic and copies ran while one was open for 3% -> 3% of each run, Pallas kernels for 28% -> 28%
where the time goes in v5:
time: 257 us
  waiting for transfers between devices  94.5 us (37%)
  Pallas kernels  85.5 us (33%)
  starting transfers between devices  45 us (18%)
  local copies, waits for them, and re-layouts  14.7 us (6%)
  between operations  14.5 us (6%)
    pallas_call x21, Pallas kernels, run(): pl.pallas_call(kernel, name=name, in_specs=[pl.BlockSpec(memory_space=spa...  85.5 us
    ppermute x48, waiting for transfers between devices, shifted(): return lax.ppermute(array, 'wide', pairs)  77.8 us
    ppermute x48, starting transfers between devices, shifted(): return lax.ppermute(array, 'wide', pairs)  32.6 us
    ppermute x6, waiting for transfers between devices, shifted(): lax.ppermute(array, 'narrow', [(i, (i + step) % count) for i in range(cou...  12.8 us
    ppermute x6, starting transfers between devices, shifted(): lax.ppermute(array, 'narrow', [(i, (i + step) % count) for i in range(cou...  10.4 us
    unnamed x94, local copies, waits for them, and re-layouts  8.44 us
  transfers between devices with their start and end apart: 59, of which 31 were waited for; matrix products, arithmetic and copies ran while one was open for 3% of the time, Pallas kernels for 28%

profile of v5, /device:TPU:0, one launch (start us, length us, event | category | flops | bytes accessed | tf_op | source)
XLA Modules:
  0.0 256.6 jit_solution(6212435173329376192)
XLA Ops:
  8.2 5.1 %collective-permute-start.3 = (bf16[24,3200]{1,0:T(8,128)(2,1)S(1)}, bf16[24,3200]{1,0:T(8,128)(2,1)S(1)}, u32[]{:S(2)}, u32[]{:S(2)}) collective-permute-start(bf16[24,3200]{1,0:T(8,128)(2,1)S(1)} %pack_first.1), channel_id=1, source_target_pairs={{0,3},{1,0},{2,1},{3,2},{4,7},{5,4},{6,5},{7,6},{8,11},{9,8},{10,9... | collective-permute-start | bytes 460808 | tf_op jit(solution)/shard_map/ppermute | solution.py:88
  18.4 2.9 %collective-permute-done.4 = bf16[24,1536]{1,0:T(8,128)(2,1)S(1)} collective-permute-done((bf16[24,1536]{1,0:T(8,128)(2,1)S(1)}, bf16[24,1536]{1,0:T(8,128)(2,1)S(1)}, u32[]{:S(2)}, u32[]{:S(2)}) %collective-permute-start.4) | collective-permute-done | bytes 73760 | tf_op jit(solution)/shard_map/ppermute | solution.py:94
  22.8 3.5 %collective-permute-done.2 = bf16[24,3200]{1,0:T(8,128)(2,1)S(1)} collective-permute-done((bf16[24,3200]{1,0:T(8,128)(2,1)S(1)}, bf16[24,3200]{1,0:T(8,128)(2,1)S(1)}, u32[]{:S(2)}, u32[]{:S(2)}) %collective-permute-start.2) | collective-permute-done | bytes 153632 | tf_op jit(solution)/shard_map/ppermute | solution.py:88
  30.2 12.2 %collective-permute-done.9.refs_4_ = bf16[96,3200]{1,0:T(8,128)(2,1)S(1)} collective-permute-done((bf16[96,3200]{1,0:T(8,128)(2,1)S(1)}, bf16[96,3200]{1,0:T(8,128)(2,1)S(1)}, u32[]{:S(2)}, u32[]{:S(2)}) %collective-permute-start.9) | collective-permute-done | bytes 614432 | tf_op jit(solution)/shard_map/ppermute | solution.py:94
  42.4 2.6 collective-permute-done.7.refs_2_
  49.2 6.0 %collective-permute-done.13.refs_8_ = bf16[48,3200]{1,0:T(8,128)(2,1)} collective-permute-done((bf16[48,3200]{1,0:T(8,128)(2,1)S(1)}, bf16[48,3200]{1,0:T(8,128)(2,1)}, u32[]{:S(2)}, u32[]{:S(2)}) %collective-permute-start.13) | collective-permute-done | bytes 307232 | tf_op jit(solution)/shard_map/ppermute | solution.py:94
  64.3 9.5 %self_forward.1 = (bf16[256,1536]{1,0:T(8,128)(2,1)S(1)}, bf16[256,768]{1,0:T(8,128)(2,1)S(1)}, bf16[12,256,256]{2,1,0:T(8,128)(2,1)S(1)}, f32[256,768]{1,0:T(8,...) custom-call(s32[20]{0:T(128)S(1)} %stack.118.place, ...), custom_call_target="tpu_custom_call" | custom-call | flops 1207959552 | bytes 2680360 | tf_op jit(solution)/shard_map/self_forward/pallas_call | solution.py:235
  78.5 13.1 %collective-permute-done.18.lower.refs_4_.refs_10_ = bf16[96,7680]{1,0:T(8,128)(2,1)} collective-permute-done((bf16[96,7680]{1,0:T(8,128)(2,1)}, bf16[96,7680]{1,0:T(8,128)(2,1)}, u32[]{:S(2)}, u32[]{:S(2)}) %collective-permute-start.18) | collective-permute-done | bytes 1474592 | tf_op jit(solution)/shard_map/ppermute | solution.py:94
  91.5 2.9 %collective-permute-done.16.upper.refs_2_.refs_8_ = bf16[96,7680]{1,0:T(8,128)(2,1)} collective-permute-done((bf16[96,7680]{1,0:T(8,128)(2,1)}, bf16[96,7680]{1,0:T(8,128)(2,1)}, u32[]{:S(2)}, u32[]{:S(2)}) %collective-permute-start.16) | collective-permute-done | bytes 1474592 | tf_op jit(solution)/shard_map/ppermute | solution.py:94
  101.8 4.8 %collective-permute-done.21.refs_6_.refs_12_ = bf16[48,3072]{1,0:T(8,128)(2,1)} collective-permute-done((bf16[48,3072]{1,0:T(8,128)(2,1)}, bf16[48,3072]{1,0:T(8,128)(2,1)}, u32[]{:S(2)}, u32[]{:S(2)}) %collective-permute-start.21) | collective-permute-done | bytes 294944 | tf_op jit(solution)/shard_map/ppermute | solution.py:94
  111.1 9.8 %cross_forward.1 = (bf16[256,768]{1,0:T(8,128)(2,1)S(1)}, bf16[256,1536]{1,0:T(8,128)(2,1)S(1)}, bf16[12,256,256]{2,1,0:T(8,128)(2,1)S(1)}, f32[256,768]{1,0:T(8...) custom-call(s32[20]{0:T(128)S(1)} %stack.118.place, ...), custom_call_target="tpu_custom_call" | custom-call | flops 1207959552 | bytes 5616680 | tf_op jit(solution)/shard_map/cross_forward/pallas_call | solution.py:235
  122.8 4.2 %hidden_early.1 = (bf16[768,3072]{1,0:T(8,128)(2,1)S(1)}, bf16[3072,768]{1,0:T(8,128)(2,1)S(1)}) custom-call(s32[20]{0:T(128)S(1)} %stack.118.place, bf16[96,7680]{1,0:T(8,128)(2,1)} %all-gather.4.cloned.1.call-done.refs_0_.refs_6_, bf16[96,7680]{1,0:T(8,128)(2,1)} %collective-permute-done.17.refs_1_.refs_7_, ...), custom_call_target="tpu_custom_call" | custom-call | bytes 5603368 | tf_op jit(solution)/shard_map/hidden_early/pallas_call | solution.py:235
  128.8 7.5 %hidden_first.1 = (bf16[256,3072]{1,0:T(8,128)(2,1)S(1)}, bf16[256,3072]{1,0:T(8,128)(2,1)S(1)}, bf16[4,480,256]{2,1,0:T(8,128)(2,1)S(1)}, bf16[4,480,256]{2,1,0...) custom-call(s32[20]{0:T(128)S(1)} %stack.118.place, ...), custom_call_target="tpu_custom_call", output_to_operand_aliasing={{4}: (4, {}), {5}: (5, {})} | custom-call | flops 2415919104 | bytes 6205480 | tf_op jit(solution)/shard_map/hidden_first/pallas_call | solution.py:235
  136.9 3.7 %hidden_second.1 = (bf16[256,768]{1,0:T(8,128)(2,1)}, f32[256,768]{1,0:T(8,128)S(1)}, bf16[256,768]{1,0:T(8,128)(2,1)S(1)}, f32[1,768]{1,0:T(1,128)S(1)}) custom-call(f32[256,768]{1,0:T(8,128)S(1)} %get-tuple-element.152.x, bf16[256,768]{1,0:T(8,128)(2,1)S(1)} %copy-done.1, f32[8,768]{1,0:T(8,128)S(1)} %copy-done.12, ...), custom_call_target="tpu_custom_call" | custom-call | flops 2415919104 | bytes 6893568 | tf_op jit(solution)/shard_map/hidden_second/pallas_call | solution.py:235
  141.2 5.1 %weight_grads.3 = (bf16[2,96,1152]{2,1,0:T(8,128)(2,1)S(1)}, bf16[2,96,1152]{2,1,0:T(8,128)(2,1)}, bf16[2,96,1152]{2,1,0:T(8,128)(2,1)S(1)}, bf16[2,96,1152]{2,1,0:T(8,128)(2,1)}, bf16[4,4,24,3840]{3,2,1,0:T(8,128)(2,1)}) custom-call(s32[20]{0:T(128)S(1)} %stack.118.place, bf16[1,4,480,256]{3,2,1,0:T(8,128)(2,1)S(1)} %bitcast.78, ...), custom_call_target="tpu_custom_call" | custom-call | flops 2415919104 | bytes 2949160 | tf_op jit(solution)/shard_map/weight_grads/pallas_call | solution.py:235
  150.9 9.5 %cross_backward.1 = (bf16[256,3072]{1,0:T(8,128)(2,1)S(1)}, f32[256,768]{1,0:T(8,128)S(1)}, f32[1,768]{1,0:T(1,128)S(1)}) custom-call(s32[20]{0:T(128)S(1)} %stack.118.place, f32[8,768]{1,0:T(8,128)S(1)} %copy-done.13, bf16[256,768]{1,0:T(8,128)(2,1)} %copy-done.5, bf16[256,1536]{1,0:T(8,128)(2,1)} %copy-done.8, bf16[12,256,256]{2,1,0:T(8,128)(2,1)} %copy-done.4, ...), custom_call_target="tpu_custom_call" | custom-call | flops 1207959552 | bytes 7385128 | tf_op jit(solution)/shard_map/cross_backward/pallas_call | solution.py:235
  161.0 3.4 %collective-permute-done.37.refs_5_ = bf16[256,3072]{1,0:T(8,128)(2,1)S(1)} collective-permute-done((bf16[256,3072]{1,0:T(8,128)(2,1)S(1)}, bf16[256,3072]{1,0:T(8,128)(2,1)S(1)}, u32[]{:S(2)}, u32[]{:S(2)}) %collective-permute-start.37) | collective-permute-done | bytes 1572896 | tf_op jit(solution)/shard_map/ppermute | solution.py:94
  168.9 12.6 %self_backward.1 = (bf16[256,768]{1,0:T(8,128)(2,1)S(1)}, bf16[256,768]{1,0:T(8,128)(2,1)S(1)}, bf16[320,768]{1,0:T(8,128)(2,1)S(1)}, f32[256,768]{1,0:T(8,128)}, bf16[4,96,128]{2,1,0:T(8,128)(2,1)S(1)}) custom-call(s32[20]{0:T(128)S(1)} %stack.118.place, f32[256,768]{1,0:T(8,128)S(1)} %get-tuple-element.186.grad, ...), custom_call_target="tpu_custom_call" | custom-call | flops 1207959552 | bytes 5250088 | tf_op jit(solution)/shard_map/self_backward/pallas_call | solution.py:235
  193.1 3.9 %memory_gradient.1 = f32[256,768]{1,0:T(8,128)} custom-call(s32[20]{0:T(128)S(1)} %stack.118.place, bf16[256,3072]{1,0:T(8,128)(2,1)S(1)} %get-tuple-element.181.refs_4_.before.grads, bf16[96,7680]{1,0:T(8,128)(2,1)} %all-gather.4.cloned.1.call-done.refs_0_.refs_6_, bf16[96,7680]{1,0:T(8,128)(2,1)} %collective-permute-done.17.refs_1_.refs_7_, ...), custom_call_target="tpu_custom_call" | custom-call | flops 603979776 | bytes 5799976 | tf_op jit(solution)/shard_map/memory_gradient/pallas_call | solution.py:235
  197.1 8.4 %collective-permute-done.43 = bf16[96,3072]{1,0:T(8,128)(2,1)S(1)} collective-permute-done((bf16[96,3072]{1,0:T(8,128)(2,1)}, bf16[96,3072]{1,0:T(8,128)(2,1)S(1)}, u32[]{:S(2)}, u32[]{:S(2)}) %collective-permute-start.43) | collective-permute-done | bytes 589856 | tf_op jit(solution)/shard_map/ppermute | solution.py:94
  214.2 3.4 %collective-permute-done.45.refs_1_ = bf16[2,96,1280]{2,1,0:T(8,128)(2,1)} collective-permute-done((bf16[2,96,1280]{2,1,0:T(8,128)(2,1)}, bf16[2,96,1280]{2,1,0:T(8,128)(2,1)}, u32[]{:S(2)}, u32[]{:S(2)}) %collective-permute-start.45) | collective-permute-done | bytes 491552 | tf_op jit(solution)/shard_map/ppermute | solution.py:94
  221.2 4.2 %collective-permute-done.49.kept_far = bf16[2,24,3840]{2,1,0:T(8,128)(2,1)S(1)} collective-permute-done((bf16[2,24,3840]{2,1,0:T(8,128)(2,1)}, bf16[2,24,3840]{2,1,0:T(8,128)(2,1)S(1)}, u32[]{:S(2)}, u32[]{:S(2)}) %collective-permute-start.49) | collective-permute-done | bytes 368672 | tf_op jit(solution)/shard_map/ppermute | solution.py:94
  233.9 2.5 collective-permute-done.51.far
  238.9 9.1 %collective-permute-done.54.refs_2_ = bf16[24,2432]{1,0:T(8,128)(2,1)S(1)} collective-permute-done((bf16[24,2432]{1,0:T(8,128)(2,1)S(1)}, bf16[24,2432]{1,0:T(8,128)(2,1)S(1)}, u32[]{:S(2)}, u32[]{:S(2)}) %collective-permute-start.54) | collective-permute-done | bytes 116768 | tf_op jit(solution)/shard_map/ppermute | solution.py:88
  (233 shorter events, 92.2 us)
Async XLA Ops:
  7.2 50.7 %all-gather.4.cloned.1.call-start = ((), (), s32[]{:S(2)}) async-start(), calls=%async_computation.1 | async-start | bytes 1843200 | tf_op jit(solution)/shard_map/all_gather | solution.py:1190
  8.2 14.5 %collective-permute-start.3 = (bf16[24,3200]{1,0:T(8,128)(2,1)S(1)}, bf16[24,3200]{1,0:T(8,128)(2,1)S(1)}, u32[]{:S(2)}, u32[]{:S(2)}) collective-permute-start(bf16[24,3200]{1,0:T(8,128)(2,1)S(1)} %pack_first.1), channel_id=1, source_target_pairs={{0,3},{1,0},{2,1},{3,2},{4,7},{5,4},{6,5},{7,6},{8,11},{9,8},{10,9... | collective-permute-start | bytes 460808 | tf_op jit(solution)/shard_map/ppermute | solution.py:88
  22.8 76.6 %all-gather.6.cloned.1.call-start = ((), (), s32[]{:S(2)}) async-start(), calls=%async_computation.3 | async-start | bytes 1474560 | tf_op jit(solution)/shard_map/all_gather | solution.py:1201
  27.2 15.2 %collective-permute-start.9 = (bf16[96,3200]{1,0:T(8,128)(2,1)S(1)}, bf16[96,3200]{1,0:T(8,128)(2,1)S(1)}, u32[]{:S(2)}, u32[]{:S(2)}) collective-permute-start(bf16[96,3200]{1,0:T(8,128)(2,1)S(1)} %bitcast.80), channel_id=1, source_target_pairs={{0,16},{4,20},{8,24},{12,28},{16,0},{20,4},{24,8},{28,12},{1,17},{... | collective-permute-start | bytes 1843208 | tf_op jit(solution)/shard_map/ppermute | solution.py:94
  28.7 13.7 %collective-permute-start.6 = (bf16[96,3200]{1,0:T(8,128)(2,1)S(1)}, bf16[96,3200]{1,0:T(8,128)(2,1)S(1)}, u32[]{:S(2)}, u32[]{:S(2)}) collective-permute-start(bf16[96,3200]{1,0:T(8,128)(2,1)S(1)} %bitcast.81), channel_id=1, source_target_pairs={{0,4},{4,0},{8,12},{12,8},{16,20},{20,16},{24,28},{28,24},{1,5},{5... | collective-permute-start | bytes 1843208 | tf_op jit(solution)/shard_map/ppermute | solution.py:94
  28.7 16.3 %collective-permute-start.7 = (bf16[96,3200]{1,0:T(8,128)(2,1)S(1)}, bf16[96,3200]{1,0:T(8,128)(2,1)S(1)}, u32[]{:S(2)}, u32[]{:S(2)}) collective-permute-start(bf16[96,3200]{1,0:T(8,128)(2,1)S(1)} %bitcast.82), channel_id=1, source_target_pairs={{0,8},{4,12},{8,0},{12,4},{16,24},{20,28},{24,16},{28,20},{1,9},{5... | collective-permute-start | bytes 1843208 | tf_op jit(solution)/shard_map/ppermute | solution.py:94
  45.5 15.4 %collective-permute-start.22 = (bf16[24,1536]{1,0:T(8,128)(2,1)S(1)}, bf16[24,1536]{1,0:T(8,128)(2,1)}, u32[]{:S(2)}, u32[]{:S(2)}) collective-permute-start(bf16[24,1536]{1,0:T(8,128)(2,1)S(1)} %get-tuple-element.129), channel_id=1, source_target_pairs={{0,16},{4,20},{8,24},{12,28},{16,0},{20,4},{24,8},{28,12},{1,17},{... | collective-permute-start | bytes 221192 | tf_op jit(solution)/shard_map/ppermute | solution.py:94
  57.9 33.6 %collective-permute-start.18 = (bf16[96,7680]{1,0:T(8,128)(2,1)}, bf16[96,7680]{1,0:T(8,128)(2,1)}, u32[]{:S(2)}, u32[]{:S(2)}) collective-permute-start(bf16[96,7680]{1,0:T(8,128)(2,1)} %all-gather.4.cloned.1.call-done.refs_0_.refs_6_), channel_id=1, source_target_pairs={{0,16},{4,20},{8,24},{12,28},{16,0},{20,4},{24,8},{28,12},{1,17},{... | collective-permute-start | bytes 4423688 | tf_op jit(solution)/shard_map/ppermute | solution.py:94
  59.4 32.1 %collective-permute-start.17 = (bf16[96,7680]{1,0:T(8,128)(2,1)}, bf16[96,7680]{1,0:T(8,128)(2,1)}, u32[]{:S(2)}, u32[]{:S(2)}) collective-permute-start(bf16[96,7680]{1,0:T(8,128)(2,1)} %all-gather.4.cloned.1.call-done.refs_0_.refs_6_), channel_id=1, source_target_pairs={{0,4},{4,0},{8,12},{12,8},{16,20},{20,16},{24,28},{28,24},{1,5},{5... | collective-permute-start | bytes 4423688 | tf_op jit(solution)/shard_map/ppermute | solution.py:94
  59.4 35.0 %collective-permute-start.16 = (bf16[96,7680]{1,0:T(8,128)(2,1)}, bf16[96,7680]{1,0:T(8,128)(2,1)}, u32[]{:S(2)}, u32[]{:S(2)}) collective-permute-start(bf16[96,7680]{1,0:T(8,128)(2,1)} %all-gather.4.cloned.1.call-done.refs_0_.refs_6_), channel_id=1, source_target_pairs={{0,8},{4,12},{8,0},{12,4},{16,24},{20,28},{24,16},{28,20},{1,9},{5... | collective-permute-start | bytes 4423688 | tf_op jit(solution)/shard_map/ppermute | solution.py:94
  63.2 146.5 %reduce-scatter.2.cloned.1.call-start = ((), (), s32[]{:S(2)}) async-start(), calls=%async_computation.2 | async-start | bytes 3686400 | tf_op jit(solution)/shard_map/reduce_scatter | solution.py:1289
  94.4 16.6 %collective-permute-start.19 = (bf16[96,7680]{1,0:T(8,128)(2,1)}, bf16[96,7680]{1,0:T(8,128)(2,1)}, u32[]{:S(2)}, u32[]{:S(2)}) collective-permute-start(bf16[96,7680]{1,0:T(8,128)(2,1)} %collective-permute-done.16.upper.refs_2_.refs_8_), channel_id=1, source_target_pairs={{0,4},{4,0},{8,12},{12,8},{16,20},{20,16},{24,28},{28,24},{1,5},{5... | collective-permute-start | bytes 4423688 | tf_op jit(solution)/shard_map/ppermute | solution.py:94
  94.4 16.6 %collective-permute-start.20 = (bf16[96,7680]{1,0:T(8,128)(2,1)}, bf16[96,7680]{1,0:T(8,128)(2,1)}, u32[]{:S(2)}, u32[]{:S(2)}) collective-permute-start(bf16[96,7680]{1,0:T(8,128)(2,1)} %collective-permute-done.18.lower.refs_4_.refs_10_), channel_id=1, source_target_pairs={{0,4},{4,0},{8,12},{12,8},{16,20},{20,16},{24,28},{28,24},{1,5},{5... | collective-permute-start | bytes 4423688 | tf_op jit(solution)/shard_map/ppermute | solution.py:94
  107.2 15.6 %collective-permute-start.27 = (bf16[384,1536]{1,0:T(8,128)(2,1)}, bf16[384,1536]{1,0:T(8,128)(2,1)}, u32[]{:S(2)}, u32[]{:S(2)}) collective-permute-start(bf16[384,1536]{1,0:T(8,128)(2,1)} %bitcast.42.refs_6_), channel_id=1, source_target_pairs={{0,4},{4,0},{8,12},{12,8},{16,20},{20,16},{24,28},{28,24},{1,5},{5... | collective-permute-start | bytes 3538952 | tf_op jit(solution)/shard_map/ppermute | solution.py:94
  166.9 20.3 %collective-permute-start.41 = (bf16[2,96,1920]{2,1,0:T(8,128)(2,1)S(1)}, bf16[2,96,1920]{2,1,0:T(8,128)(2,1)S(1)}, u32[]{:S(2)}, u32[]{:S(2)}) collective-permute-start(bf16[2,96,1920]{2,1,0:T(8,128)(2,1)S(1)} %get-tuple-element.183), channel_id=1, source_target_pairs={{0,16},{4,20},{8,24},{12,28},{16,0},{20,4},{24,8},{28,12},{1,17},{... | collective-permute-start | bytes 2211848 | tf_op jit(solution)/shard_map/ppermute | solution.py:94
  168.4 18.8 %collective-permute-start.42 = (bf16[2,96,1920]{2,1,0:T(8,128)(2,1)S(1)}, bf16[2,96,1920]{2,1,0:T(8,128)(2,1)S(1)}, u32[]{:S(2)}, u32[]{:S(2)}) collective-permute-start(bf16[2,96,1920]{2,1,0:T(8,128)(2,1)S(1)} %get-tuple-element.185), channel_id=1, source_target_pairs={{0,8},{4,12},{8,0},{12,4},{16,24},{20,28},{24,16},{28,20},{1,9},{5... | collective-permute-start | bytes 2211848 | tf_op jit(solution)/shard_map/ppermute | solution.py:94
  189.1 16.4 %collective-permute-start.43 = (bf16[96,3072]{1,0:T(8,128)(2,1)}, bf16[96,3072]{1,0:T(8,128)(2,1)S(1)}, u32[]{:S(2)}, u32[]{:S(2)}) collective-permute-start(bf16[96,3072]{1,0:T(8,128)(2,1)} %get-tuple-element.203), channel_id=1, source_target_pairs={{0,8},{4,12},{8,0},{12,4},{16,24},{20,28},{24,16},{28,20},{1,9},{5... | collective-permute-start | bytes 1769480 | tf_op jit(solution)/shard_map/ppermute | solution.py:94
  190.5 16.5 %collective-permute-start.44 = (bf16[96,3072]{1,0:T(8,128)(2,1)}, bf16[96,3072]{1,0:T(8,128)(2,1)}, u32[]{:S(2)}, u32[]{:S(2)}) collective-permute-start(bf16[96,3072]{1,0:T(8,128)(2,1)} %get-tuple-element.205), channel_id=1, source_target_pairs={{0,16},{4,20},{8,24},{12,28},{16,0},{20,4},{24,8},{28,12},{1,17},{... | collective-permute-start | bytes 1769480 | tf_op jit(solution)/shard_map/ppermute | solution.py:94
  191.1 23.1 %collective-permute-start.46 = (bf16[2,96,1152]{2,1,0:T(8,128)(2,1)}, bf16[2,96,1152]{2,1,0:T(8,128)(2,1)}, u32[]{:S(2)}, u32[]{:S(2)}) collective-permute-start(bf16[2,96,1152]{2,1,0:T(8,128)(2,1)} %copy-done.32), channel_id=1, source_target_pairs={{0,8},{4,12},{8,0},{12,4},{16,24},{20,28},{24,16},{28,20},{1,9},{5... | collective-permute-start | bytes 1327112 | tf_op jit(solution)/shard_map/ppermute | solution.py:94
  192.6 25.0 %collective-permute-start.45 = (bf16[2,96,1280]{2,1,0:T(8,128)(2,1)}, bf16[2,96,1280]{2,1,0:T(8,128)(2,1)}, u32[]{:S(2)}, u32[]{:S(2)}) collective-permute-start(bf16[2,96,1280]{2,1,0:T(8,128)(2,1)} %copy-done.31), channel_id=1, source_target_pairs={{0,16},{4,20},{8,24},{12,28},{16,0},{20,4},{24,8},{28,12},{1,17},{... | collective-permute-start | bytes 1474568 | tf_op jit(solution)/shard_map/ppermute | solution.py:94
  209.2 16.2 %collective-permute-start.50 = (bf16[2,24,6144]{2,1,0:T(8,128)(2,1)}, bf16[2,24,6144]{2,1,0:T(8,128)(2,1)S(1)}, u32[]{:S(2)}, u32[]{:S(2)}) collective-permute-start(bf16[2,24,6144]{2,1,0:T(8,128)(2,1)} %get-tuple-element.218), channel_id=1, source_target_pairs={{0,1},{1,0},{2,3},{3,2},{4,5},{5,4},{6,7},{7,6},{8,9},{9,8},{10,11... | collective-permute-start | bytes 1769480 | tf_op jit(solution)/shard_map/ppermute | solution.py:1040
  211.6 13.8 %collective-permute-start.49 = (bf16[2,24,3840]{2,1,0:T(8,128)(2,1)}, bf16[2,24,3840]{2,1,0:T(8,128)(2,1)S(1)}, u32[]{:S(2)}, u32[]{:S(2)}) collective-permute-start(bf16[2,24,3840]{2,1,0:T(8,128)(2,1)} %get-tuple-element.242), channel_id=1, source_target_pairs={{0,16},{4,20},{8,24},{12,28},{16,0},{20,4},{24,8},{28,12},{1,17},{... | collective-permute-start | bytes 1105928 | tf_op jit(solution)/shard_map/ppermute | solution.py:94
  230.3 17.7 %collective-permute-start.54 = (bf16[24,2432]{1,0:T(8,128)(2,1)S(1)}, bf16[24,2432]{1,0:T(8,128)(2,1)S(1)}, u32[]{:S(2)}, u32[]{:S(2)}) collective-permute-start(bf16[24,2432]{1,0:T(8,128)(2,1)S(1)} %get-tuple-element.227), channel_id=1, source_target_pairs={{0,2},{1,3},{2,0},{3,1},{4,6},{5,7},{6,4},{7,5},{8,10},{9,11},{10,... | collective-permute-start | bytes 350216 | tf_op jit(solution)/shard_map/ppermute | solution.py:88
  232.0 16.0 %collective-permute-start.55 = (bf16[24,2432]{1,0:T(8,128)(2,1)S(1)}, bf16[24,2432]{1,0:T(8,128)(2,1)S(1)}, u32[]{:S(2)}, u32[]{:S(2)}) collective-permute-start(bf16[24,2432]{1,0:T(8,128)(2,1)S(1)} %get-tuple-element.228), channel_id=1, source_target_pairs={{0,3},{1,0},{2,1},{3,2},{4,7},{5,4},{6,5},{7,6},{8,11},{9,8},{10,9... | collective-permute-start | bytes 350216 | tf_op jit(solution)/shard_map/ppermute | solution.py:88
  (82 other events, 676.6 us)
Sparse Core Ops, SparseCore 0:
  22.9 34.9 all-gather.3
  63.3 27.7 all-gather.5
  148.0 55.1 reduce-scatter.1
